TPU v7x, 128 devices: a whole 4x4x4 slice. The times are simulated.
128 devices in a mesh: tok: 8 (over z, core), narrow: 2 (over x_lo), wide: 8 (over y, x_hi).
Axes of the slice: x: 4 (x_hi: 2, x_lo: 2; x = x_hi * 2 + x_lo), y: 4, z: 4, core: 2. Of those that a mesh axis runs over, the one named last changes fastest.
Arguments:
- layer_input: bfloat16 [12288, 2048], P('tok', ('narrow', 'wide')), may hold values from -6 to 6
- doc_lengths: int32 [8, 2], P('tok'), may hold values from 256 to 1024, as said below
- attn_gain: float32 [2048], replicated, may hold values from 0.1 to 1.9
- w_query: bfloat16 [2048, 2048], P(None, ('narrow', 'wide')), may hold values from -0.25 to 0.25
- w_key: bfloat16 [2048, 512], P(None, 'narrow'), may hold values from -0.125 to 0.125
- w_value: bfloat16 [2048, 512], P(None, 'narrow'), may hold values from -0.125 to 0.125
- w_output: bfloat16 [2048, 2048], P(None, ('narrow', 'wide')), may hold values from -0.75 to 0.75
- ffn_gain: float32 [2048], P(('narrow', 'wide')), may hold values from 0.1 to 1.9
- w_gate: bfloat16 [2048, 8192], P('narrow', 'wide'), may hold values from -0.125 to 0.125
- w_up: bfloat16 [2048, 8192], P('narrow', 'wide'), may hold values from -0.125 to 0.125
- w_down: bfloat16 [8192, 2048], P('wide', 'narrow'), may hold values from -0.125 to 0.125
- output_grad: bfloat16 [12288, 2048], P('tok', ('narrow', 'wide')), may hold values from -6 to 6
Outputs:
- layer_output: bfloat16 [12288, 2048], P('tok', ('narrow', 'wide'))
- input_grad: bfloat16 [12288, 2048], P('tok', ('narrow', 'wide'))
- attn_gain_grad: float32 [16, 128], P(('narrow', 'wide'), 'tok')
- query_grad: float32 [2048, 2048], P('tok', ('narrow', 'wide'))
- key_grad: float32 [2048, 512], P(('tok', 'wide'), 'narrow')
- value_grad: float32 [2048, 512], P(('tok', 'wide'), 'narrow')
- output_proj_grad: float32 [2048, 2048], P('tok', ('narrow', 'wide'))
- ffn_gain_grad: float32 [16, 128], P(('narrow', 'wide'), 'tok')
- gate_grad: float32 [16, 128, 8192], P('narrow', 'tok', 'wide')
- up_grad: float32 [16, 128, 8192], P('narrow', 'tok', 'wide')
- down_grad: float32 [64, 128, 2048], P('wide', 'tok', 'narrow')
Inputs may be any that keep to these rules, and one draw needn't show every extreme that they name: `doc_lengths`: each row lists the lengths of the 2 documents packed in order into one index of tok; a row sums to 1536, and in every row exactly one document has 1024 tokens, the most.
All inputs are finite; a program needn't handle non-finite values.
Results may differ from a plain program's by a relative error of at most 0.024.
Values may be sent and summed in bfloat16 or wider, within the bound.
A program may use at most 192 MiB of HBM per device.

v0:
```python
import math

import jax
import jax.numpy as jnp
from jax import lax
from jax.sharding import PartitionSpec as P

HEADS = 32
KV_HEADS = 8
HEAD_DIM = 64
GROUP = 128


EPS = 1e-05
THETA = 500000.0
FACTOR = 32.0
LOW_FACTOR = 1.0
HIGH_FACTOR = 4.0
INITIAL = 8192.0
NEG = -1e30


def rope_tables(positions, head_size):
    halfway = head_size // 2
    position_k = jnp.arange(halfway, dtype=jnp.float32)
    inverse = jnp.exp(-2.0 * position_k / head_size * math.log(THETA))
    wavelen = 2.0 * math.pi / inverse
    scaled = inverse / FACTOR
    smooth = (INITIAL / wavelen - LOW_FACTOR) / (HIGH_FACTOR - LOW_FACTOR)
    middle = (1.0 - smooth) * scaled + smooth * inverse
    frequency = jnp.where(
        wavelen < INITIAL / HIGH_FACTOR,
        inverse,
        jnp.where(wavelen > INITIAL / LOW_FACTOR, scaled, middle),
    )
    angles = positions[:, None] * frequency[None, :]
    return (jnp.cos(angles), jnp.sin(angles))


def rotate(tensor, cosine, sine_table):
    halfway = tensor.shape[-1] // 2
    front = tensor[..., :halfway]
    behind = tensor[..., halfway:]
    cos_rows = cosine[:, None, :]
    sin_rows = sine_table[:, None, :]
    return jnp.concatenate(
        [front * cos_rows - behind * sin_rows, behind * cos_rows + front * sin_rows], axis=-1
    )


def doc_layout(lengths, length_all):
    finish = jnp.cumsum(lengths)
    starts = finish - lengths
    row_ids = jnp.arange(length_all, dtype=jnp.int32)
    inside = (row_ids[:, None] >= starts[None, :]) & (row_ids[:, None] < finish[None, :])
    doc_first = jnp.sum(jnp.where(inside, starts[None, :], 0), axis=1)
    return (doc_first, (row_ids - doc_first).astype(jnp.float32))


def gather_rows(shard_part):
    return lax.all_gather(shard_part, ("narrow", "wide"), axis=1, tiled=True)


def head_total(term):
    return lax.psum_scatter(term, ("narrow", "wide"), scatter_dimension=1, tiled=True)


def row_total(term):
    return lax.psum(term, ("narrow", "wide"))


def gather_half(shard_part):
    return lax.all_gather(shard_part, "wide", axis=1, tiled=True)


def half_total(term):
    return lax.psum_scatter(term, "wide", scatter_dimension=1, tiled=True)


def contract_rows(left_side, right_side):
    return lax.dot_general(
        left_side, right_side, (((0,), (0,)), ((), ())), preferred_element_type=jnp.float32
    )


def contract_cols(left_side, right_side):
    return lax.dot_general(
        left_side, right_side, (((1,), (1,)), ((), ())), preferred_element_type=jnp.float32
    )


def per_device(
    layer_input,
    doc_lengths,
    attn_gain,
    w_query,
    w_key,
    w_value,
    w_output,
    ffn_gain,
    w_gate,
    w_up,
    w_down,
    output_grad,
):
    wide_count = lax.axis_size("wide")
    narrow_pos = lax.axis_index("narrow")
    wide_pos = lax.axis_index("wide")
    length_all = layer_input.shape[0]
    local_cols = layer_input.shape[1]
    col_start = (narrow_pos * wide_count + wide_pos) * local_cols
    heads_here = w_query.shape[1] // HEAD_DIM
    kv_slot = wide_pos * heads_here // (HEADS // KV_HEADS)
    score_scale = HEAD_DIM ** (-0.5)
    doc_first, positions = doc_layout(doc_lengths[0], length_all)
    cosine, sine_table = rope_tables(positions, HEAD_DIM)
    rows_local = layer_input.astype(jnp.float32)
    full_input = gather_rows(layer_input)
    model_width = full_input.shape[1]
    scale_one = lax.rsqrt(
        jnp.mean(jnp.square(full_input.astype(jnp.float32)), axis=1, keepdims=True) + EPS
    )
    normed = (full_input * scale_one * attn_gain).astype(jnp.bfloat16)
    key_cols = lax.dynamic_slice_in_dim(w_key, kv_slot * HEAD_DIM, HEAD_DIM, 1)
    value_cols = lax.dynamic_slice_in_dim(w_value, kv_slot * HEAD_DIM, HEAD_DIM, 1)
    query_lin = jnp.dot(normed, w_query, preferred_element_type=jnp.float32)
    key_lin = jnp.dot(normed, key_cols, preferred_element_type=jnp.float32)
    value_lin = jnp.dot(normed, value_cols, preferred_element_type=jnp.float32)
    queries = rotate(
        query_lin.reshape(length_all, heads_here, HEAD_DIM), cosine, sine_table
    ).astype(jnp.bfloat16)
    keys_here = rotate(key_lin.reshape(length_all, 1, HEAD_DIM), cosine, sine_table)[:, 0].astype(
        jnp.bfloat16
    )
    values_here = value_lin.astype(jnp.bfloat16)
    block_rows = min(512, length_all)
    key_index = jnp.arange(length_all, dtype=jnp.int32)

    def block_scores(block_start):
        query_block = lax.dynamic_slice_in_dim(queries, block_start, block_rows, 0)
        first_block = lax.dynamic_slice_in_dim(doc_first, block_start, block_rows, 0)
        query_index = block_start + jnp.arange(block_rows, dtype=jnp.int32)
        scores = (
            jnp.einsum("qhd,kd->hqk", query_block, keys_here, preferred_element_type=jnp.float32)
            * score_scale
        )
        allowed = (key_index[None, :] <= query_index[:, None]) & (
            key_index[None, :] >= first_block[:, None]
        )
        return (query_block, jnp.where(allowed[None], scores, NEG))

    def attend(block_start):
        query_block, scores = block_scores(block_start)
        highest = jnp.max(scores, axis=2, keepdims=True)
        raised = jnp.exp(scores - highest)
        row_mass = jnp.sum(raised, axis=2, keepdims=True)
        soft_low = (raised / row_mass).astype(jnp.bfloat16)
        mixed_block = jnp.einsum(
            "hqk,kd->qhd", soft_low, values_here, preferred_element_type=jnp.float32
        )
        return (mixed_block, (highest + jnp.log(row_mass))[:, :, 0])

    block_starts = jnp.arange(length_all // block_rows, dtype=jnp.int32) * block_rows
    mixed_blocks, log_masses = lax.map(attend, block_starts)
    heads_out = mixed_blocks.reshape(length_all, heads_here * HEAD_DIM).astype(jnp.bfloat16)
    attn_local = head_total(contract_cols(heads_out, w_output))
    resid = rows_local + attn_local
    scale_two = lax.rsqrt(row_total(jnp.sum(resid * resid, axis=1)) / model_width + EPS)[:, None]
    ffn_input = (resid * scale_two * ffn_gain).astype(jnp.bfloat16)
    ffn_half = gather_half(ffn_input)
    hidden = w_gate.shape[1]
    joined = lax.psum_scatter(
        jnp.concatenate(
            [
                jnp.dot(ffn_half, w_gate, preferred_element_type=jnp.float32),
                jnp.dot(ffn_half, w_up, preferred_element_type=jnp.float32),
            ],
            axis=1,
        ),
        "narrow",
        scatter_dimension=0,
        tiled=True,
    )
    gate_lin = joined[:, :hidden]
    up_lin = joined[:, hidden:]
    act_part = (jax.nn.silu(gate_lin) * up_lin).astype(jnp.bfloat16)
    act_full = lax.all_gather(act_part, "narrow", axis=0, tiled=True)
    down_local = half_total(jnp.dot(act_full, w_down, preferred_element_type=jnp.float32))
    layer_output = (resid + down_local).astype(jnp.bfloat16)
    grad_half = gather_half(output_grad)
    down_wgrad = contract_rows(act_full, grad_half)
    act_back = lax.psum_scatter(
        contract_cols(grad_half, w_down).astype(jnp.bfloat16),
        "narrow",
        scatter_dimension=0,
        tiled=True,
    ).astype(jnp.float32)
    sigmoid_gate = jax.nn.sigmoid(gate_lin)
    gate_back = (act_back * up_lin * sigmoid_gate * (1.0 + gate_lin * (1.0 - sigmoid_gate))).astype(
        jnp.bfloat16
    )
    up_back = (act_back * gate_lin * sigmoid_gate).astype(jnp.bfloat16)
    gate_back, up_back = (
        lax.all_gather(gate_back, "narrow", axis=0, tiled=True),
        lax.all_gather(up_back, "narrow", axis=0, tiled=True),
    )
    gate_wgrad = contract_rows(ffn_half, gate_back)
    up_wgrad = contract_rows(ffn_half, up_back)
    ffn_input_back = half_total(contract_cols(gate_back, w_gate) + contract_cols(up_back, w_up))
    inner_two = row_total(jnp.sum(ffn_input_back * ffn_gain * resid, axis=1))[:, None]
    resid_back = (
        output_grad.astype(jnp.float32)
        + scale_two * ffn_gain * ffn_input_back
        - resid * scale_two**3 * inner_two / model_width
    )
    ffn_gain_back = jnp.sum(ffn_input_back * resid * scale_two, axis=0)
    mix_back = resid_back.astype(jnp.bfloat16)
    full_back = gather_rows(mix_back)
    out_wgrad = contract_rows(full_back, heads_out)
    heads_back = jnp.dot(full_back, w_output, preferred_element_type=jnp.float32).astype(
        jnp.bfloat16
    )
    heads_back = heads_back.reshape(length_all, heads_here, HEAD_DIM)

    def attend_back(carry, inputs):
        key_acc, value_acc = carry
        block_start, log_mass = inputs
        query_block, scores = block_scores(block_start)
        soft = jnp.exp(scores - log_mass[:, :, None])
        back_block = lax.dynamic_slice_in_dim(heads_back, block_start, block_rows, 0)
        prob_back = jnp.einsum(
            "qhd,kd->hqk", back_block, values_here, preferred_element_type=jnp.float32
        )
        score_back = (soft * (prob_back - jnp.sum(soft * prob_back, axis=2, keepdims=True))).astype(
            jnp.bfloat16
        )
        query_part = (
            jnp.einsum("hqk,kd->qhd", score_back, keys_here, preferred_element_type=jnp.float32)
            * score_scale
        )
        key_acc = (
            key_acc
            + jnp.einsum("hqk,qhd->kd", score_back, query_block, preferred_element_type=jnp.float32)
            * score_scale
        )
        value_acc = value_acc + jnp.einsum(
            "hqk,qhd->kd", soft.astype(jnp.bfloat16), back_block, preferred_element_type=jnp.float32
        )
        return ((key_acc, value_acc), query_part)

    zero_rows = jnp.zeros((length_all, HEAD_DIM), jnp.float32)
    (key_acc, value_acc), query_parts = lax.scan(
        attend_back, (zero_rows, zero_rows), (block_starts, log_masses)
    )
    query_back = rotate(query_parts.reshape(length_all, heads_here, HEAD_DIM), cosine, -sine_table)
    query_back = query_back.reshape(length_all, heads_here * HEAD_DIM).astype(jnp.bfloat16)
    key_back = rotate(key_acc[:, None, :], cosine, -sine_table)[:, 0].astype(jnp.bfloat16)
    value_back = value_acc.astype(jnp.bfloat16)
    query_wgrad = contract_rows(normed, query_back)
    key_wgrad = contract_rows(normed, key_back)
    value_wgrad = contract_rows(normed, value_back)
    normed_term = (
        contract_cols(query_back, w_query)
        + contract_cols(key_back, key_cols)
        + contract_cols(value_back, value_cols)
    )
    normed_back = head_total(normed_term)
    gain_local = lax.dynamic_slice_in_dim(attn_gain, col_start, local_cols, 0)
    inner_one = row_total(jnp.sum(normed_back * gain_local * rows_local, axis=1))[:, None]
    input_grad = (
        resid_back
        + scale_one * gain_local * normed_back
        - rows_local * scale_one**3 * inner_one / model_width
    ).astype(jnp.bfloat16)
    attn_gain_back = jnp.sum(normed_back * rows_local * scale_one, axis=0)
    key_padded = lax.dynamic_update_slice_in_dim(
        jnp.zeros(w_key.shape, jnp.float32), key_wgrad, kv_slot * HEAD_DIM, 1
    )
    value_padded = lax.dynamic_update_slice_in_dim(
        jnp.zeros(w_value.shape, jnp.float32), value_wgrad, kv_slot * HEAD_DIM, 1
    )
    key_grad, value_grad = (
        lax.psum_scatter(key_padded, ("tok", "wide"), scatter_dimension=0, tiled=True),
        lax.psum_scatter(value_padded, ("tok", "wide"), scatter_dimension=0, tiled=True),
    )
    query_grad, output_proj_grad = (
        lax.psum_scatter(
            query_wgrad.astype(jnp.bfloat16), "tok", scatter_dimension=0, tiled=True
        ).astype(jnp.float32),
        lax.psum_scatter(
            out_wgrad.astype(jnp.bfloat16), "tok", scatter_dimension=0, tiled=True
        ).astype(jnp.float32),
    )
    feature_rows = gate_wgrad.shape[0]
    gate_grad, up_grad, down_grad, attn_gain_grad, ffn_gain_grad = (
        lax.psum_scatter(
            gate_wgrad.reshape(feature_rows // GROUP, GROUP, hidden).astype(jnp.bfloat16),
            "tok",
            scatter_dimension=1,
            tiled=True,
        ).astype(jnp.float32),
        lax.psum_scatter(
            up_wgrad.reshape(feature_rows // GROUP, GROUP, hidden).astype(jnp.bfloat16),
            "tok",
            scatter_dimension=1,
            tiled=True,
        ).astype(jnp.float32),
        lax.psum_scatter(
            down_wgrad.reshape(hidden // GROUP, GROUP, feature_rows).astype(jnp.bfloat16),
            "tok",
            scatter_dimension=1,
            tiled=True,
        ).astype(jnp.float32),
        lax.psum_scatter(
            attn_gain_back.reshape(local_cols // GROUP, GROUP).astype(jnp.bfloat16),
            "tok",
            scatter_dimension=1,
            tiled=True,
        ).astype(jnp.float32),
        lax.psum_scatter(
            ffn_gain_back.reshape(local_cols // GROUP, GROUP).astype(jnp.bfloat16),
            "tok",
            scatter_dimension=1,
            tiled=True,
        ).astype(jnp.float32),
    )
    return (
        layer_output,
        input_grad,
        attn_gain_grad,
        query_grad,
        key_grad,
        value_grad,
        output_proj_grad,
        ffn_gain_grad,
        gate_grad,
        up_grad,
        down_grad,
    )


def solution(mesh):
    in_specs = (
        P("tok", ("narrow", "wide")),
        P("tok", None),
        P(),
        P(None, ("narrow", "wide")),
        P(None, "narrow"),
        P(None, "narrow"),
        P(None, ("narrow", "wide")),
        P(("narrow", "wide")),
        P("narrow", "wide"),
        P("narrow", "wide"),
        P("wide", "narrow"),
        P("tok", ("narrow", "wide")),
    )
    out_specs = (
        P("tok", ("narrow", "wide")),
        P("tok", ("narrow", "wide")),
        P(("narrow", "wide"), "tok"),
        P("tok", ("narrow", "wide")),
        P(("tok", "wide"), "narrow"),
        P(("tok", "wide"), "narrow"),
        P("tok", ("narrow", "wide")),
        P(("narrow", "wide"), "tok"),
        P("narrow", "tok", "wide"),
        P("narrow", "tok", "wide"),
        P("wide", "tok", "narrow"),
    )
    return jax.shard_map(
        per_device, mesh=mesh, in_specs=in_specs, out_specs=out_specs, check_vma=False
    )
```

profile of v0, /device:TPU:0, one launch (start us, length us, event | category | flops | bytes accessed | tf_op | source)
XLA Modules:
  0.0 2641.1 jit_solution(14955969129431137613)
XLA Ops:
  12.5 167.8 %all-gather.8.cloned.1.call-done = bf16[1536,2048]{1,0:T(8,128)(2,1)} async-done(((bf16[1536,128]{1,0:T(8,128)(2,1)}), bf16[1536,2048]{1,0:T(8,128)(2,1)}) %all-gather.8.cloned.1.call-update) | async-done | bytes 6291472 | tf_op jit(solution)/shard_map/all_gather | solution.py:61
  196.2 39.1 %while.30 = (s32[]{:T(128)}, bf16[3,512,2,64]{1,3,2,0:T(8,128)(2,1)S(1)}, f32[3,2,512]{2,1,0:T(2,128)}, s32[3]{0:T(128)}, s32[1536]{0:T(1024)S(1)}, /*index=5*/b...) while((s32[]{:T(128)}, ...), condition=%wide.region_6.7_spmd.clone.clone, body=%wide.region_3.6_spmd.clone.clone.sunk | while | flops 423886336 | bytes 22849720 | solution.py:164
  243.5 291.1 %reduce-scatter.20.cloned.1.call-done = f32[1536,128]{1,0:T(8,128)} async-done(((f32[1536,2048]{1,0:T(8,128)}), f32[1536,128]{1,0:T(8,128)}) %reduce-scatter.20.cloned.1.call-update) | async-done | bytes 786448 | tf_op jit(solution)/shard_map/reduce_scatter | solution.py:65
  536.0 39.0 %psum.21 = f32[1536]{0:T(1024)S(1)} all-reduce(f32[1536]{0:T(1024)S(1)} %get-tuple-element.284), channel_id=1, replica_groups=mesh['tok'=8,'narrow'=2,'wide'=8] {'narrow','wide'}, use_global_device_ids=true, to_apply=%region_9.10 | all-reduce | flops 1536 | bytes 12288 | tf_op jit(solution)/shard_map/psum | solution.py:69
  584.0 51.9 %all-gather.10.cloned.1.call-done = bf16[1536,1024]{1,0:T(8,128)(2,1)} async-done(((bf16[1536,128]{1,0:T(8,128)(2,1)}), bf16[1536,1024]{1,0:T(8,128)(2,1)}) %all-gather.10.cloned.1.call-update) | async-done | bytes 3145744 | tf_op jit(solution)/shard_map/all_gather | solution.py:73
  660.8 21.0 reduce-scatter.26.cloned.1.call-done
  681.9 150.4 %reduce-scatter.22.cloned.1.call-done = f32[768,2048]{0,1:T(8,128)} async-done(((f32[1536,2048]{0,1:T(8,128)}), f32[768,2048]{0,1:T(8,128)}) %reduce-scatter.22.cloned.1.call-update) | async-done | bytes 6291472 | tf_op jit(solution)/shard_map/reduce_scatter | solution.py:172
  839.7 46.5 %all-gather.16.cloned.1.call-done = bf16[1536,1024]{0,1:T(8,128)(2,1)} async-done(((bf16[768,1024]{0,1:T(8,128)(2,1)}), bf16[1536,1024]{0,1:T(8,128)(2,1)}) %all-gather.16.cloned.1.call-update) | async-done | bytes 3145744 | tf_op jit(solution)/shard_map/all_gather | solution.py:204
  893.5 42.7 %all-gather.18.cloned.1.call-done = bf16[1536,1024]{0,1:T(8,128)(2,1)} async-done(((bf16[768,1024]{0,1:T(8,128)(2,1)}), bf16[1536,1024]{0,1:T(8,128)(2,1)}) %all-gather.18.cloned.1.call-update) | async-done | bytes 3145744 | tf_op jit(solution)/shard_map/all_gather | solution.py:205
  946.8 39.4 %all-gather.12.cloned.1.call-done = bf16[1536,1024]{0,1:T(8,128)(2,1)} async-done(((bf16[768,1024]{0,1:T(8,128)(2,1)}), bf16[1536,1024]{0,1:T(8,128)(2,1)}) %all-gather.12.cloned.1.call-update) | async-done | bytes 3145744 | tf_op jit(solution)/shard_map/all_gather | solution.py:187
  993.6 96.0 %reduce-scatter.28.cloned.1.call-done = f32[1536,128]{1,0:T(8,128)} async-done(((f32[1536,1024]{1,0:T(8,128)}), f32[1536,128]{1,0:T(8,128)}) %reduce-scatter.28.cloned.1.call-update) | async-done | bytes 786448 | tf_op jit(solution)/shard_map/reduce_scatter | solution.py:77
  1091.7 55.8 %psum.22 = f32[1536]{0:T(1024)S(1)} all-reduce(f32[1536]{0:T(1024)S(1)} %get-tuple-element.241), channel_id=1, replica_groups=mesh['tok'=8,'narrow'=2,'wide'=8] {'narrow','wide'}, use_global_device_ids=true, to_apply=%region_15.16 | all-reduce | flops 1536 | bytes 12288 | tf_op jit(solution)/shard_map/psum | solution.py:69
  1147.5 43.7 %reduce-scatter.24.cloned.1.call-done = f32[1536,128]{1,0:T(8,128)} async-done(((f32[1536,1024]{1,0:T(8,128)}), f32[1536,128]{1,0:T(8,128)}) %reduce-scatter.24.cloned.1.call-update) | async-done | bytes 786448 | tf_op jit(solution)/shard_map/reduce_scatter | solution.py:77
  1194.5 165.7 %all-gather.20.cloned.1.call-done = bf16[1536,2048]{1,0:T(8,128)(2,1)} async-done(((bf16[1536,128]{1,0:T(8,128)(2,1)}), bf16[1536,2048]{1,0:T(8,128)(2,1)}) %all-gather.20.cloned.1.call-update) | async-done | bytes 6291472 | tf_op jit(solution)/shard_map/all_gather | solution.py:61
  1365.3 67.7 %while.31 = (s32[]{:T(128)}, f32[1536,64]{0,1:T(8,128)S(1)}, f32[1536,64]{0,1:T(8,128)S(1)}, f32[3,512,2,64]{1,0,3,2:T(4,128)}, s32[3]{0:T(128)}, /*index=5*/s32...) while((s32[]{:T(128)}, f32[1536,64]{0,1:T(8,128)S(1)}, ...), condition=%wide.region_18.19_spmd.clone.clone, body=%wide.region_16.18_spmd.clone.clone.sunk | while | flops 1023704576 | bytes 52787428 | solution.py:252
  1493.7 234.4 %reduce-scatter.30.cloned.1.call-done = f32[1536,128]{1,0:T(8,128)} async-done(((f32[1536,2048]{1,0:T(8,128)}), f32[1536,128]{1,0:T(8,128)}) %reduce-scatter.30.cloned.1.call-update) | async-done | bytes 786448 | tf_op jit(solution)/shard_map/reduce_scatter | solution.py:65
  1764.9 33.1 %reduce-scatter.42.cloned.1.call-done = bf16[8,16,1024]{2,1,0:T(8,128)(2,1)} async-done(((bf16[8,128,1024]{2,1,0:T(8,128)(2,1)}), bf16[8,16,1024]{2,1,0:T(8,128)(2,1)}) %reduce-scatter.42.cloned.1.call-update) | async-done | bytes 262160 | tf_op jit(solution)/shard_map/reduce_scatter | solution.py:302
  1799.8 33.3 %reduce-scatter.40.cloned.1.call-done = bf16[8,16,1024]{2,1,0:T(8,128)(2,1)} async-done(((bf16[8,128,1024]{2,1,0:T(8,128)(2,1)}), bf16[8,16,1024]{2,1,0:T(8,128)(2,1)}) %reduce-scatter.40.cloned.1.call-update) | async-done | bytes 262160 | tf_op jit(solution)/shard_map/reduce_scatter | solution.py:296
  1834.9 30.3 %reduce-scatter.48.cloned.1.call-done = bf16[16,1]{1,0:T(8,128)(2,1)} async-done(((bf16[128,1]{1,0:T(8,128)(2,1)}), bf16[16,1]{1,0:T(8,128)(2,1)}) %reduce-scatter.48.cloned.1.call-update) | async-done | bytes 48
  1866.4 31.0 %reduce-scatter.38.cloned.1.call-done = bf16[256,128]{1,0:T(8,128)(2,1)} async-done(((bf16[2048,128]{1,0:T(8,128)(2,1)}), bf16[256,128]{1,0:T(8,128)(2,1)}) %reduce-scatter.38.cloned.1.call-update) | async-done | bytes 65552 | tf_op jit(solution)/shard_map/reduce_scatter | solution.py:290
  1898.9 30.6 %reduce-scatter.32.cloned.1.call-done = bf16[256,128]{1,0:T(8,128)(2,1)} async-done(((bf16[2048,128]{1,0:T(8,128)(2,1)}), bf16[256,128]{1,0:T(8,128)(2,1)}) %reduce-scatter.32.cloned.1.call-update) | async-done | bytes 65552 | tf_op jit(solution)/shard_map/reduce_scatter | solution.py:287
  1931.1 40.9 %psum.23 = f32[1536]{0:T(1024)S(1)} all-reduce(f32[1536]{0:T(1024)S(1)} %get-tuple-element.243), channel_id=1, replica_groups=mesh['tok'=8,'narrow'=2,'wide'=8] {'narrow','wide'}, use_global_device_ids=true, to_apply=%region_21.22 | all-reduce | flops 1536 | bytes 12288 | tf_op jit(solution)/shard_map/psum | solution.py:69
  1976.0 323.2 %reduce-scatter.34.cloned.1.call-done = f32[32,256]{1,0:T(8,128)} async-done(((f32[2048,256]{1,0:T(8,128)}), f32[32,256]{1,0:T(8,128)}) %reduce-scatter.34.cloned.1.call-update) | async-done | bytes 32784 | tf_op jit(solution)/shard_map/reduce_scatter | solution.py:283
  2299.1 334.2 %reduce-scatter.36.cloned.1.call-done = f32[32,256]{1,0:T(8,128)} async-done(((f32[2048,256]{1,0:T(8,128)}), f32[32,256]{1,0:T(8,128)}) %reduce-scatter.36.cloned.1.call-update) | async-done | bytes 32784 | tf_op jit(solution)/shard_map/reduce_scatter | solution.py:284
  (241 shorter events, 310.4 us)
Async XLA Ops:
  8.0 636.7 %copy-start = (bf16[1024,1024]{1,0:T(8,128)(2,1)S(1)}, bf16[1024,1024]{1,0:T(8,128)(2,1)}, u32[]{:S(2)}) copy-start(bf16[1024,1024]{1,0:T(8,128)(2,1)} %param.24) | copy-start | bytes 6291460
  8.0 172.2 %all-gather.8.cloned.1.call-start = ((), (), s32[]{:S(2)}) async-start(), calls=%async_computation.15 | async-start | bytes 6684672 | tf_op jit(solution)/shard_map/all_gather | solution.py:61
  8.8 525.8 %reduce-scatter.20.cloned.1.call-start = ((), (), s32[]{:S(2)}) async-start(), calls=%async_computation.16 | async-start | bytes 13369344 | tf_op jit(solution)/shard_map/reduce_scatter | solution.py:65
  242.9 333.2 %all-gather.14.cloned.1.call-start = ((), (), s32[]{:S(2)}) async-start(), calls=%async_computation.21 | async-start | bytes 3538944 | tf_op jit(solution)/shard_map/all_gather | solution.py:73
  243.4 392.5 %all-gather.10.cloned.1.call-start = ((), (), s32[]{:S(2)}) async-start(), calls=%async_computation.17 | async-start | bytes 3538944 | tf_op jit(solution)/shard_map/all_gather | solution.py:73
  576.0 105.8 %reduce-scatter.26.cloned.1.call-start = ((), (), s32[]{:S(2)}) async-start(), calls=%async_computation.22 | async-start | bytes 4718592 | tf_op jit(solution)/shard_map/reduce_scatter | solution.py:192
  583.7 248.6 %reduce-scatter.22.cloned.1.call-start = ((), (), s32[]{:S(2)}) async-start(), calls=%async_computation.18 | async-start | bytes 18874368 | tf_op jit(solution)/shard_map/reduce_scatter | solution.py:172
  660.8 225.4 %all-gather.16.cloned.1.call-start = ((), (), s32[]{:S(2)}) async-start(), calls=%async_computation.23 | async-start | bytes 4718592 | tf_op jit(solution)/shard_map/all_gather | solution.py:204
  837.9 98.4 %all-gather.18.cloned.1.call-start = ((), (), s32[]{:S(2)}) async-start(), calls=%async_computation.24 | async-start | bytes 4718592 | tf_op jit(solution)/shard_map/all_gather | solution.py:205
  838.6 147.6 %all-gather.12.cloned.1.call-start = ((), (), s32[]{:S(2)}) async-start(), calls=%async_computation.19 | async-start | bytes 4718592 | tf_op jit(solution)/shard_map/all_gather | solution.py:187
  839.2 250.4 %reduce-scatter.28.cloned.1.call-start = ((), (), s32[]{:S(2)}) async-start(), calls=%async_computation.25 | async-start | bytes 7077888 | tf_op jit(solution)/shard_map/reduce_scatter | solution.py:77
  946.8 244.5 %reduce-scatter.24.cloned.1.call-start = ((), (), s32[]{:S(2)}) async-start(), calls=%async_computation.20 | async-start | bytes 7077888 | tf_op jit(solution)/shard_map/reduce_scatter | solution.py:77
  993.5 366.7 %all-gather.20.cloned.1.call-start = ((), (), s32[]{:S(2)}) async-start(), calls=%async_computation.26 | async-start | bytes 6684672 | tf_op jit(solution)/shard_map/all_gather | solution.py:61
  1194.3 533.7 %reduce-scatter.30.cloned.1.call-start = ((), (), s32[]{:S(2)}) async-start(), calls=%async_computation.27 | async-start | bytes 13369344 | tf_op jit(solution)/shard_map/reduce_scatter | solution.py:65
  1457.4 305.6 %reduce-scatter.44.cloned.1.call-start = ((), (), s32[]{:S(2)}) async-start(), calls=%async_computation.34 | async-start | bytes 2359296 | tf_op jit(solution)/shard_map/reduce_scatter | solution.py:308
  1465.1 332.9 %reduce-scatter.42.cloned.1.call-start = ((), (), s32[]{:S(2)}) async-start(), calls=%async_computation.33 | async-start | bytes 2359296 | tf_op jit(solution)/shard_map/reduce_scatter | solution.py:302
  1472.8 360.2 %reduce-scatter.40.cloned.1.call-start = ((), (), s32[]{:S(2)}) async-start(), calls=%async_computation.32 | async-start | bytes 2359296 | tf_op jit(solution)/shard_map/reduce_scatter | solution.py:296
  1480.9 384.2 %reduce-scatter.48.cloned.1.call-start = ((), (), s32[]{:S(2)}) async-start(), calls=%async_computation.36 | async-start | bytes 36864
  1481.7 415.7 %reduce-scatter.38.cloned.1.call-start = ((), (), s32[]{:S(2)}) async-start(), calls=%async_computation.31 | async-start | bytes 589824 | tf_op jit(solution)/shard_map/reduce_scatter | solution.py:290
  1487.3 442.3 %reduce-scatter.32.cloned.1.call-start = ((), (), s32[]{:S(2)}) async-start(), calls=%async_computation.28 | async-start | bytes 589824 | tf_op jit(solution)/shard_map/reduce_scatter | solution.py:287
  1492.8 481.9 %reduce-scatter.46.cloned.1.call-start = ((), (), s32[]{:S(2)}) async-start(), calls=%async_computation.35 | async-start | bytes 36864
  1730.4 568.7 %reduce-scatter.34.cloned.1.call-start = ((), (), s32[]{:S(2)}) async-start(), calls=%async_computation.29 | async-start | bytes 2129920 | tf_op jit(solution)/shard_map/reduce_scatter | solution.py:283
  1742.5 890.8 %reduce-scatter.36.cloned.1.call-start = ((), (), s32[]{:S(2)}) async-start(), calls=%async_computation.30 | async-start | bytes 2129920 | tf_op jit(solution)/shard_map/reduce_scatter | solution.py:284
  1755.0 878.3 %copy-start.1 = (bf16[1024,1024]{1,0:T(8,128)(2,1)S(1)}, bf16[1024,1024]{1,0:T(8,128)(2,1)}, u32[]{:S(2)}) copy-start(bf16[1024,1024]{1,0:T(8,128)(2,1)} %param.24) | copy-start | bytes 6291460
  (28 other events, 3042.4 us)
Sparse Core Ops, SparseCore 0:
  10.4 169.7 all-gather.7
  243.0 291.5 reduce-scatter.19
  1194.4 165.8 all-gather.19
  1457.6 270.4 reduce-scatter.29
  1730.4 32.6 reduce-scatter.43
  1765.5 32.4 reduce-scatter.41
  1800.5 32.5 reduce-scatter.39
  1836.1 28.9 reduce-scatter.47
  1867.5 29.8 reduce-scatter.37
  1899.8 29.7 reduce-scatter.31
  1931.9 29.3 reduce-scatter.45
  1964.2 334.8 reduce-scatter.33
  2302.0 331.1 reduce-scatter.35
Sparse Core Ops, SparseCore 1:
  245.5 91.2 all-gather.13
  576.1 59.8 all-gather.9
  638.1 43.7 reduce-scatter.25
  684.4 147.8 reduce-scatter.21
  837.9 48.2 all-gather.15
  888.0 48.2 all-gather.17
  937.9 48.2 all-gather.11
  990.4 99.1 reduce-scatter.27
  1093.8 97.4 reduce-scatter.23
where the time goes:
time: 2650 us; the launch traced here: 2640 us
  waiting for transfers between devices  2180 us (82%)
  matrix products  175 us (7%)
  blocking collectives  136 us (5%)
  other arithmetic  71.1 us (3%)
  local copies, waits for them, and re-layouts  51 us (2%)
    reduce_scatter x2, waiting for transfers between devices, head_total(): lax.psum_scatter(term, ('narrow', 'wide'), scatter_dimension=1, tiled=True)  525 us
    reduce_scatter x1, waiting for transfers between devices, per_device(): lax.psum_scatter(value_padded, ('tok', 'wide'), scatter_dimension=0, tile...  334 us
    all_gather x2, waiting for transfers between devices, gather_rows(): return lax.all_gather(shard_part, ('narrow', 'wide'), axis=1, tiled=True)  334 us
    reduce_scatter x1, waiting for transfers between devices, per_device(): lax.psum_scatter(key_padded, ('tok', 'wide'), scatter_dimension=0, tiled=...  323 us
    reduce_scatter x1, waiting for transfers between devices, per_device(): lax.psum_scatter(jnp.concatenate([jnp.dot(ffn_half, w_gate, preferred_ele...  150 us
    reduce_scatter x2, waiting for transfers between devices, half_total(): return lax.psum_scatter(term, 'wide', scatter_dimension=1, tiled=True)  140 us
    psum x3, blocking collectives, row_total(): return lax.psum(term, ('narrow', 'wide'))  136 us
  transfers between devices with their start and end apart: 22, of which 20 were waited for; matrix products, arithmetic and copies ran while one was open for 5% of the time, Pallas kernels for 0%

commit v1 on v0

v1 whole, which is shorter than its diff:
```python
import functools
import math

import jax
import jax.numpy as jnp
import numpy as np
from jax import lax
from jax.experimental import pallas as pl
from jax.experimental.pallas import tpu as pltpu
from jax.sharding import PartitionSpec as P

HEADS = 32
KV_HEADS = 8
HEAD_DIM = 64
GROUP = 128
EPS = 1e-05
THETA = 500000.0
FACTOR = 32.0
LOW_FACTOR = 1.0
HIGH_FACTOR = 4.0
INITIAL = 8192.0
NEG = -1e30

D = 2048
ROWS = 1536
CHUNK = 384
SUB = 96
SHORT = 512
BF = jnp.bfloat16
F32 = jnp.float32
MESH = pl.DeviceIdType.MESH
SDS = jax.ShapeDtypeStruct

HERE = (0, 0, 0, 0, 0)
XOFF = [(0, 0, 0, 0, 0), (0, 0, 1, 0, 0), (0, 0, 0, 0, 1), (0, 0, 1, 0, 1)]
YOFF = [(0, 0, 0, d, 0) for d in range(4)]
PLANE = [(0, 0, a, b, e) for b in range(4) for a in range(2) for e in range(2)]
SIBLING = (1, 0, 0, 0, 0)
TOKS = [(a, b, 0, 0, 0) for b in range(4) for a in range(2)]


class Place:
    def __init__(self, core, z, xl, y, xh):
        self.core, self.z, self.xl, self.y, self.xh = core, z, xl, y, xh
        self.tok = z * 2 + core
        self.wide = y * 2 + xh
        self.block = xl * 8 + self.wide
        self.chunk = xl * 2 + xh

    def at(self, off):
        return Place(
            (self.core + off[0]) % 2,
            (self.z + off[1]) % 4,
            (self.xl + off[2]) % 2,
            (self.y + off[3]) % 4,
            (self.xh + off[4]) % 2,
        )

    def device(self):
        return (self.tok, self.xl, self.wide)


def whereami():
    tok = lax.axis_index("tok")
    wide = lax.axis_index("wide")
    return Place(tok % 2, tok // 2, lax.axis_index("narrow"), wide // 2, wide % 2)


def rows(start, size):
    return pl.ds(pl.multiple_of(start, size), size)


def exchange(name, number, plan, ins, outs):
    n_in, n_out = len(ins), len(outs)

    def count():
        fake = Place(0, 0, 0, 0, 0)
        probe = [_Any() for _ in range(n_in)], [_Any() for _ in range(n_out)]
        local, sends = plan(fake, *probe)
        return len(local), sum(1 + len(s[3]) for s in sends)

    n_local, n_send = count()

    def body(*refs):
        sources, targets = refs[:n_in], refs[n_in : n_in + n_out]
        send_sem, recv_sem, local_sem = refs[n_in + n_out :]
        me = whereami()
        local, sends = plan(me, sources, targets)
        offsets = []
        for off, _, _, forwards in sends:
            for o in [off] + [f[0] for f in forwards]:
                if o not in offsets:
                    offsets.append(o)
        barrier = pltpu.get_barrier_semaphore()
        for off in offsets:
            back = tuple(-v for v in off)
            pl.semaphore_signal(
                barrier, inc=1, device_id=me.at(back).device(), device_id_type=MESH
            )
        near = []
        for i, (src, dst) in enumerate(local):
            near.append(pltpu.make_async_copy(src, dst, local_sem.at[i]))
            near[-1].start()
        pl.semaphore_wait(barrier, len(offsets))
        slot = 0

        def launch(off, src, dst):
            nonlocal slot
            copy = pltpu.make_async_remote_copy(
                src_ref=src,
                dst_ref=dst,
                send_sem=send_sem.at[slot],
                recv_sem=recv_sem.at[slot],
                device_id=me.at(off).device(),
                device_id_type=MESH,
            )
            copy.start()
            slot += 1
            return copy

        first = [(launch(off, src, dst), forwards) for off, src, dst, forwards in sends]
        second = []
        for copy, forwards in first:
            if forwards:
                copy.wait_recv()
                second += [launch(*f) for f in forwards]
        for copy, forwards in first:
            copy.wait_send()
            if not forwards:
                copy.wait_recv()
        for copy in second:
            copy.wait()
        for copy in near:
            copy.wait()

    return pl.pallas_call(
        body,
        name=name,
        out_shape=outs,
        in_specs=[pl.BlockSpec(memory_space=pl.ANY)] * n_in,
        out_specs=[pl.BlockSpec(memory_space=pltpu.VMEM)] * n_out,
        scratch_shapes=[
            pltpu.SemaphoreType.DMA((n_send,)),
            pltpu.SemaphoreType.DMA((n_send,)),
            pltpu.SemaphoreType.DMA((max(n_local, 1),)),
        ],
        compiler_params=pltpu.CompilerParams(
            collective_id=number, has_side_effects=True, vmem_limit_bytes=40 * 2**20
        ),
    )(*ins)


class _Any:
    @property
    def at(self):
        return self

    def __getitem__(self, key):
        return self


def lanes(index, size=128):
    return pl.ds(pl.multiple_of(index * size, size), size)


def spread_plan(me, src, dst):
    local = [(src.at[rows(me.chunk * CHUNK, CHUNK), :], dst.at[:, lanes(me.block)])]
    sends = [
        (off, src.at[rows(me.at(off).chunk * CHUNK, CHUNK), :], dst.at[:, lanes(me.block)], [])
        for off in PLANE[1:]
    ]
    return local, sends


def enter_plan(me, ins, outs):
    hidden, w_q, w_kv, gain = ins
    full, w_attn, gains = outs
    half = rows(me.core * 1024, 1024)
    local, sends = spread_plan(me, hidden, full)
    local += [
        (w_q, w_attn.at[:, 0:128]),
        (w_kv, w_attn.at[:, 512:640]),
        (gain, gains.at[me.block]),
    ]
    head = []
    for k in (1, 2, 3):
        cols = slice(k * 128, k * 128 + 128)
        block = w_attn.at[half, cols]
        head.append((XOFF[k], w_q.at[half, :], block, [(SIBLING, block, block)]))
    block = w_attn.at[half, 640:768]
    head.append((XOFF[1], w_kv.at[half, :], block, [(SIBLING, block, block)]))
    sends = head + sends
    sends += [(off, gain, gains.at[me.block], []) for off in PLANE[1:]]
    return local, sends


def to_heads_plan(me, ins, outs):
    (lin,) = ins
    q, kv = outs
    mine = rows(me.chunk * CHUNK, CHUNK)
    local, sends = [], []
    for k, off in enumerate(XOFF):
        kv_col = 512 + 128 * off[2]
        pairs = [
            (lin.at[:, k * 128 : k * 128 + 128], q.at[mine, :]),
            (lin.at[:, kv_col : kv_col + 128], kv.at[mine, :]),
        ]
        if k == 0:
            local += pairs
        else:
            sends += [(off, s, d, []) for s, d in pairs]
    return local, sends


def from_heads_moves(me, src, dst, first_col=0):
    local, sends = [], []
    for k, off in enumerate(XOFF):
        col = first_col + k * 128
        pair = (src.at[rows(me.at(off).chunk * CHUNK, CHUNK), :], dst.at[:, col : col + 128])
        if k == 0:
            local.append(pair)
        else:
            sends.append((off, *pair, []))
    return local, sends


def heads_out_plan(me, ins, outs):
    heads, w_out, half1, half2, half3 = ins
    cat, w_cat = outs
    local, sends = from_heads_moves(me, heads, cat)
    half = rows(me.core * 1024, 1024)
    local.append((w_out, w_cat.at[:, 0:128]))
    for k, part in ((1, half1), (2, half2), (3, half3)):
        block = w_cat.at[half, k * 128 : k * 128 + 128]
        local.append((part, block))
        sends.append((SIBLING, part, block, []))
    return local, sends


def heads_back_plan(me, ins, outs):
    (cat,) = ins
    (heads,) = outs
    mine = rows(me.chunk * CHUNK, CHUNK)
    local, sends = [], []
    for k, off in enumerate(XOFF):
        pair = (cat.at[:, k * 128 : k * 128 + 128], heads.at[mine, :])
        if k == 0:
            local.append(pair)
        else:
            sends.append((off, *pair, []))
    return local, sends


def grads_out_plan(me, ins, outs):
    q, kv = ins
    (cat,) = outs
    local, sends = from_heads_moves(me, q, cat)
    local2, sends2 = from_heads_moves(me, kv, cat, 512)
    return local + local2, sends + sends2


def scatter_moves(me, src, dst):
    local = [(src.at[rows(me.y * SUB, SUB), :], dst.at[me.y])]
    sends = [(off, src.at[rows(me.at(off).y * SUB, SUB), :], dst.at[me.y], []) for off in YOFF[1:]]
    return local, sends


def out_sum_plan(me, ins, outs):
    local, sends = scatter_moves(me, ins[0], outs[0])
    local2, sends2 = spread_plan(me, ins[1], outs[1])
    return local + local2, sends + sends2


def sum_plan(me, ins, outs):
    local, sends = [], []
    for src, dst in zip(ins, outs):
        a, b = scatter_moves(me, src, dst)
        local, sends = local + a, sends + b
    return local, sends


def gather_moves(me, src, dst):
    block = dst.at[rows(me.y * SUB, SUB), :]
    return [(src, block)], [(off, src, block, []) for off in YOFF[1:]]


def gather_plan(me, ins, outs):
    return gather_moves(me, ins[0], outs[0])


def weight_moves(me, own, parts, dst):
    local = [(own, dst.at[rows(me.xl * 1024, 1024), lanes(me.xh, 1024)])]
    sends = []
    for off, part in zip(XOFF[1:], parts):
        there = me.at(off)
        block = dst.at[rows(there.xl * 1024 + me.core * 512, 512), lanes(there.xh, 1024)]
        local.append((part, block))
        sends.append((SIBLING, part, block, []))
    return local, sends


def weight_moves_t(me, own, parts, dst):
    local = [(own, dst.at[rows(me.xh * 1024, 1024), lanes(me.xl, 1024)])]
    sends = []
    for off, part in zip(XOFF[1:], parts):
        there = me.at(off)
        block = dst.at[rows(there.xh * 1024 + me.core * 512, 512), lanes(there.xl, 1024)]
        local.append((part, block))
        sends.append((SIBLING, part, block, []))
    return local, sends


def ffn_enter_plan(me, ins, outs):
    hidden, gate, up, p1, p2, p3 = ins
    full, w_gate, w_up = outs
    local, sends = gather_moves(me, hidden, full)
    for j, (own, dst) in enumerate(((gate, w_gate), (up, w_up))):
        a, b = weight_moves(me, own, [p.at[j] for p in (p1, p2, p3)], dst)
        local, sends = local + a, sends + b
    return local, sends


def down_plan(me, ins, outs):
    return weight_moves_t(me, ins[0], ins[1:], outs[0])


def leave_plan(me, ins, outs):
    local, sends = [], []
    mine = rows(me.chunk * CHUNK + me.y * SUB, SUB)
    for k, off in enumerate(PLANE):
        there = me.at(off)
        pairs = [(src.at[:, lanes(there.block)], dst.at[mine, :]) for src, dst in zip(ins[:2], outs[:2])]
        pairs.append((ins[2].at[:, lanes(there.block)], outs[2].at[me.block]))
        if k == 0:
            local += pairs
        else:
            sends += [(off, s, d, []) for s, d in pairs]
    return local, sends


def gains_plan(me, ins, outs):
    local = [(ins[0], outs[0].at[me.tok])]
    sends = [(off, ins[0], outs[0].at[me.tok], []) for off in TOKS[1:]]
    return local, sends


def block_probs(q_ref, kv_ref, start, i, stack):
    n = 256 * (i + 1)
    keys = kv_ref[rows_256(start, n), 0:64]
    scores = lax.dot_general(
        keys, stack, (((1,), (1,)), ((), ())), preferred_element_type=F32
    ) * (HEAD_DIM**-0.5)
    last = scores[n - 256 :, :]
    key_id = lax.broadcasted_iota(jnp.int32, (256, 512), 0)
    query_id = lax.broadcasted_iota(jnp.int32, (256, 512), 1) % 256
    last = jnp.where(key_id <= query_id, last, NEG)
    if n > 256:
        scores = jnp.concatenate([scores[: n - 256, :], last], axis=0)
    else:
        scores = last
    raised = jnp.exp(scores - jnp.max(scores, axis=0, keepdims=True))
    return keys, raised, jnp.sum(raised, axis=0, keepdims=True)


def rows_256(start, size):
    return pl.ds(pl.multiple_of(start, 256), size)


def starts_of(len_ref):
    long_first = len_ref[0, 0] > SHORT
    long_start = jnp.where(long_first, 0, SHORT)
    short_start = jnp.where(long_first, 2 * SHORT, 0)
    return ((long_start, 4), (short_start, 2))


def both(block):
    return jnp.concatenate([block[:, 0:64], block[:, 64:128]], axis=0)


def attend_body(len_ref, q_ref, kv_ref, out_ref):
    for start, blocks in starts_of(len_ref):
        for i in range(blocks):
            mine = rows_256(start + 256 * i, 256)
            stack = both(q_ref[mine, :])
            keys, raised, mass = block_probs(q_ref, kv_ref, start, i, stack)
            soft = (raised * (1.0 / mass)).astype(BF)
            values = kv_ref[rows_256(start, 256 * (i + 1)), 64:128]
            mixed = lax.dot_general(
                soft, values, (((0,), (0,)), ((), ())), preferred_element_type=F32
            )
            out_ref[mine, :] = jnp.concatenate([mixed[:256], mixed[256:]], axis=1).astype(BF)


def unrope(tensor, cosine, sine):
    lane = lax.broadcasted_iota(jnp.int32, tensor.shape, 1)
    first = (lane % 64) < 32
    swapped = jnp.where(first, pltpu.roll(tensor, 96, 1), -pltpu.roll(tensor, 32, 1))
    return tensor * cosine + swapped * sine


def attend_back_body(len_ref, q_ref, kv_ref, back_ref, cos_ref, sin_ref, dq_ref, dkv_ref, acc_ref):
    for start, blocks in starts_of(len_ref):
        acc_ref[...] = jnp.zeros(acc_ref.shape, F32)
        for i in range(blocks):
            n = 256 * (i + 1)
            mine = rows_256(start + 256 * i, 256)
            stack = both(q_ref[mine, :])
            keys, raised, mass = block_probs(q_ref, kv_ref, start, i, stack)
            soft = raised * (1.0 / mass)
            values = kv_ref[rows_256(start, n), 64:128]
            backs = both(back_ref[mine, :])
            prob_back = lax.dot_general(
                values, backs, (((1,), (1,)), ((), ())), preferred_element_type=F32
            )
            inner = jnp.sum(soft * prob_back, axis=0, keepdims=True)
            score_back = (soft * (prob_back - inner)).astype(BF)
            dq = lax.dot_general(
                score_back, keys, (((0,), (0,)), ((), ())), preferred_element_type=F32
            ) * (HEAD_DIM**-0.5)
            dq = jnp.concatenate([dq[:256], dq[256:]], axis=1)
            pos = slice(256 * i, 256 * i + 256)
            dq_ref[mine, :] = unrope(dq, cos_ref[pos, :], sin_ref[pos, :]).astype(BF)
            dk = jnp.dot(score_back, stack, preferred_element_type=F32) * (HEAD_DIM**-0.5)
            dv = jnp.dot(soft.astype(BF), backs, preferred_element_type=F32)
            acc_ref[0:n, :] += jnp.concatenate([dk, dv], axis=1)
        m = 256 * blocks
        acc = acc_ref[0:m, :]
        lane = lax.broadcasted_iota(jnp.int32, acc.shape, 1)
        turned = unrope(acc, cos_ref[0:m, :], sin_ref[0:m, :])
        dkv_ref[rows_256(start, m), :] = jnp.where(lane < 64, turned, acc).astype(BF)


def vmem_call(name, body, ins, outs, scratch=(), flops=0):
    return pl.pallas_call(
        body,
        name=name,
        out_shape=outs,
        in_specs=[pl.BlockSpec(memory_space=pltpu.SMEM)]
        + [pl.BlockSpec(memory_space=pltpu.VMEM)] * (len(ins) - 1),
        out_specs=[pl.BlockSpec(memory_space=pltpu.VMEM)] * len(outs),
        scratch_shapes=list(scratch),
        compiler_params=pltpu.CompilerParams(vmem_limit_bytes=48 * 2**20),
        cost_estimate=pl.CostEstimate(flops=flops, bytes_accessed=2**20, transcendentals=0),
    )(*ins)


def rope_table():
    halfway = HEAD_DIM // 2
    k = np.arange(halfway, dtype=np.float32)
    inverse = np.exp(-2.0 * k / HEAD_DIM * math.log(THETA)).astype(np.float32)
    wavelen = (2.0 * math.pi / inverse).astype(np.float32)
    scaled = inverse / np.float32(FACTOR)
    smooth = (INITIAL / wavelen - LOW_FACTOR) / (HIGH_FACTOR - LOW_FACTOR)
    middle = (1.0 - smooth) * scaled + smooth * inverse
    frequency = np.where(
        wavelen < INITIAL / HIGH_FACTOR,
        inverse,
        np.where(wavelen > INITIAL / LOW_FACTOR, scaled, middle),
    ).astype(np.float32)
    positions = np.concatenate([np.arange(512), np.arange(1024), np.arange(512)]).astype(np.float32)
    angles = (positions[:, None] * frequency[None, :]).astype(np.float32).astype(np.float64)
    return (
        np.tile(np.cos(angles).astype(np.float32), (1, 4)),
        np.tile(np.sin(angles).astype(np.float32), (1, 4)),
    )


def x_permute(value, k):
    if k == 1:
        return lax.ppermute(value, "narrow", [(0, 1), (1, 0)])
    if k == 2:
        return lax.ppermute(value, "wide", [(i, i ^ 1) for i in range(8)])
    return lax.ppermute(value, ("narrow", "wide"), [(i, i ^ 9) for i in range(16)])


def z_permute(value, d):
    return lax.ppermute(value, "tok", [(i, (i + 2 * d) % 8) for i in range(8)])


def y_permute(value, d):
    return lax.ppermute(value, "wide", [(i, (i + 2 * d) % 8) for i in range(8)])


def core_permute(value):
    return lax.ppermute(value, "tok", [(i, i ^ 1) for i in range(8)])


def pick(array, index, axis):
    return lax.dynamic_index_in_dim(array, index, axis, keepdims=False)


def part(array, start, size, axis):
    return lax.dynamic_slice_in_dim(array, start, size, axis)


def total(terms):
    out = terms[0].astype(F32)
    for term in terms[1:]:
        out = out + term.astype(F32)
    return out


def reduce_ffn(me, partial, rows_by_xl):
    view = partial.reshape(2, 8, 4, 2, 16, 2048)
    mine = pick(view, me.core, 3)
    came = core_permute(pick(view, 1 - me.core, 3))

    def quarter(k):
        there = me.at(XOFF[k])
        r, c = (there.xl, there.xh) if rows_by_xl else (there.xh, there.xl)
        return total([part(pick(a, r, 0), c * 1024, 1024, 3) for a in (mine, came)])

    own = quarter(0)
    got = [x_permute(quarter(k).astype(BF), k) for k in (1, 2, 3)]
    summed = total([own] + got).astype(BF)
    own = pick(summed, me.z, 1)
    got = [z_permute(pick(summed, (me.z + d) % 4, 1), d) for d in (1, 2, 3)]
    return total([own] + got)


def reduce_core(me, partial):
    view = partial.reshape(4, 2, 256, partial.shape[1])
    return pick(view, me.core, 1), core_permute(pick(view, 1 - me.core, 1))


def reduce_z(me, summed):
    own = pick(summed, me.z, 0)
    got = [z_permute(pick(summed, (me.z + d) % 4, 0), d) for d in (1, 2, 3)]
    return total([own] + got)


def reduce_heads(me, pair):
    pieces = [total([a[:, :, k * 128 : k * 128 + 128] for a in pair]) for k in range(4)]
    got = [x_permute(pieces[k].astype(BF), k) for k in (1, 2, 3)]
    return reduce_z(me, total([pieces[0]] + got).astype(BF))


def contract_rows(left_side, right_side):
    return lax.dot_general(
        left_side, right_side, (((0,), (0,)), ((), ())), preferred_element_type=F32
    )


def contract_cols(left_side, right_side):
    return lax.dot_general(
        left_side, right_side, (((1,), (1,)), ((), ())), preferred_element_type=F32
    )


def multiply(left_side, right_side):
    return jnp.dot(left_side, right_side, preferred_element_type=F32)


def per_device(
    layer_input,
    doc_lengths,
    attn_gain,
    w_query,
    w_key,
    w_value,
    w_output,
    ffn_gain,
    w_gate,
    w_up,
    w_down,
    output_grad,
):
    me = whereami()
    cos_np, sin_np = rope_table()
    cos_all, sin_all = jnp.asarray(cos_np), jnp.asarray(sin_np)
    long_first = doc_lengths[0, 0] > SHORT
    table_start = jnp.where(long_first, SHORT, 0) + me.chunk * CHUNK
    cos_here = part(cos_all, table_start, CHUNK, 0)
    sin_here = part(sin_all, table_start, CHUNK, 0)
    cos_doc, sin_doc = cos_all[512:1536], sin_all[512:1536]

    w_kv = jnp.concatenate(
        [part(w_key, me.y * 64, 64, 1), part(w_value, me.y * 64, 64, 1)], axis=1
    )
    full_in, w_attn, gains = exchange(
        "enter",
        0,
        enter_plan,
        [layer_input, w_query, w_kv, jnp.broadcast_to(ffn_gain[None, :], (8, 128))],
        [SDS((CHUNK, D), BF), SDS((D, 768), BF), SDS((16, 8, 128), F32)],
    )
    ffn_gain_all = gains[:, 0, :].reshape(1, D)

    half_out = part(w_output, me.core * 1024, 1024, 0)
    half_gu = jnp.stack([part(w_gate, me.core * 512, 512, 0), part(w_up, me.core * 512, 512, 0)])
    half_down = part(w_down, me.core * 512, 512, 0)
    full_in, half_out, half_gu, half_down = lax.optimization_barrier(
        (full_in, half_out, half_gu, half_down)
    )
    got_out = [x_permute(half_out, k) for k in (1, 2, 3)]
    got_gu = [x_permute(half_gu, k) for k in (1, 2, 3)]
    got_down = [x_permute(half_down, k) for k in (1, 2, 3)]

    in_f = full_in.astype(F32)
    scale_one = lax.rsqrt(jnp.mean(in_f * in_f, axis=1, keepdims=True) + EPS)
    normed = (in_f * scale_one * attn_gain[None, :]).astype(BF)
    lin = multiply(normed, w_attn)

    def turn(block):
        lane = lax.broadcasted_iota(jnp.int32, block.shape, 1)
        swapped = jnp.where(
            (lane % 64) < 32, -jnp.roll(block, -32, axis=1), jnp.roll(block, 32, axis=1)
        )
        return block * cos_here + swapped * sin_here

    turned = [turn(lin[:, k * 128 : k * 128 + 128]) for k in range(6)]
    for k in (4, 5):
        turned[k] = jnp.concatenate(
            [turned[k][:, :64], lin[:, k * 128 + 64 : k * 128 + 128]], axis=1
        )
    lin = jnp.concatenate(turned, axis=1).astype(BF)
    queries, kv = exchange(
        "to_heads", 1, to_heads_plan, [lin], [SDS((ROWS, 128), BF), SDS((ROWS, 128), BF)]
    )
    (heads_out,) = vmem_call(
        "attend", attend_body, [doc_lengths, queries, kv], [SDS((ROWS, 128), BF)], flops=2 * 10**9
    )
    heads_cat, w_out = exchange(
        "heads_out",
        2,
        heads_out_plan,
        [heads_out, w_output] + got_out,
        [SDS((CHUNK, 512), BF), SDS((D, 512), BF)],
    )
    attn_term = contract_cols(heads_cat, w_out).astype(BF)
    attn_terms, grad_full = exchange(
        "out_sum",
        3,
        out_sum_plan,
        [attn_term, output_grad],
        [SDS((4, SUB, D), BF), SDS((CHUNK, D), BF)],
    )
    in_mine = part(full_in, me.y * SUB, SUB, 0).astype(F32)
    resid = in_mine + jnp.sum(attn_terms.astype(F32), axis=0)
    scale_two = lax.rsqrt(jnp.mean(resid * resid, axis=1, keepdims=True) + EPS)
    ffn_mine = (resid * scale_two * ffn_gain_all).astype(BF)
    ffn_input, wg, wu = exchange(
        "ffn_enter",
        4,
        ffn_enter_plan,
        [ffn_mine, w_gate, w_up] + got_gu,
        [SDS((CHUNK, D), BF), SDS((D, D), BF), SDS((D, D), BF)],
    )
    gate_lin = multiply(ffn_input, wg)
    up_lin = multiply(ffn_input, wu)
    sigmoid_gate = jax.nn.sigmoid(gate_lin)
    act = (gate_lin * sigmoid_gate * up_lin).astype(BF)
    (wd,) = exchange("down_weight", 5, down_plan, [w_down] + got_down, [SDS((D, D), BF)])
    down_term = multiply(act, wd).astype(BF)
    act_back = contract_cols(grad_full, wd)
    gate_back = (act_back * up_lin * sigmoid_gate * (1.0 + gate_lin * (1.0 - sigmoid_gate))).astype(
        BF
    )
    up_back = (act_back * gate_lin * sigmoid_gate).astype(BF)
    ffn_term = (contract_cols(gate_back, wg) + contract_cols(up_back, wu)).astype(BF)
    down_terms, ffn_terms = exchange(
        "ffn_sum",
        6,
        sum_plan,
        [down_term, ffn_term],
        [SDS((4, SUB, D), BF), SDS((4, SUB, D), BF)],
    )
    out_mine = (resid + jnp.sum(down_terms.astype(F32), axis=0)).astype(BF)
    ffn_input_back = jnp.sum(ffn_terms.astype(F32), axis=0)
    grad_mine = part(grad_full, me.y * SUB, SUB, 0).astype(F32)
    scaled_back = ffn_input_back * ffn_gain_all
    inner_two = jnp.sum(scaled_back * resid, axis=1, keepdims=True)
    resid_back = grad_mine + scale_two * scaled_back - resid * scale_two**3 * inner_two / D
    ffn_gain_part = jnp.sum(ffn_input_back * resid * scale_two, axis=0, keepdims=True)
    (mix_full,) = exchange(
        "mix_gather", 7, gather_plan, [resid_back.astype(BF)], [SDS((CHUNK, D), BF)]
    )
    back_cat = multiply(mix_full, w_out).astype(BF)
    (heads_back,) = exchange("heads_back", 8, heads_back_plan, [back_cat], [SDS((ROWS, 128), BF)])

    down_grad = reduce_ffn(me, contract_rows(act, grad_full).astype(BF), False)
    gate_grad = reduce_ffn(me, contract_rows(ffn_input, gate_back).astype(BF), True)
    up_grad = reduce_ffn(me, contract_rows(ffn_input, up_back).astype(BF), True)
    out_pair = reduce_core(me, contract_rows(mix_full, heads_cat).astype(BF))
    output_proj_grad = reduce_heads(me, out_pair)

    query_back, kv_back = vmem_call(
        "attend_back",
        attend_back_body,
        [doc_lengths, queries, kv, heads_back, cos_doc, sin_doc],
        [SDS((ROWS, 128), BF), SDS((ROWS, 128), BF)],
        scratch=[pltpu.VMEM((1024, 128), F32)],
        flops=5 * 10**9,
    )
    (cat_back,) = exchange(
        "grads_out", 9, grads_out_plan, [query_back, kv_back], [SDS((CHUNK, 1024), BF)]
    )
    normed_term = (
        contract_cols(cat_back[:, :768], w_attn) + contract_cols(cat_back[:, 768:], w_attn[:, 512:])
    ).astype(BF)
    (normed_terms,) = exchange(
        "normed_sum", 10, sum_plan, [normed_term], [SDS((4, SUB, D), BF)]
    )
    attn_partial = contract_rows(normed, cat_back)
    kv_partial = attn_partial[:, 512:768] + attn_partial[:, 768:]
    query_grad = reduce_heads(me, reduce_core(me, attn_partial[:, :512].astype(BF)))

    kv_pair = reduce_core(me, kv_partial.astype(BF))
    kv_pair = [a.reshape(4, 4, 2, 32, 256) for a in kv_pair]

    def kv_piece(k):
        return total([pick(a, me.at(XOFF[k]).xh, 2)[..., 128 * XOFF[k][2] : 128 * XOFF[k][2] + 128] for a in kv_pair])

    got = [x_permute(kv_piece(k).astype(BF), k) for k in (1, 2, 3)]
    kv_sum = reduce_z(me, total([kv_piece(0)] + got).astype(BF))
    kv_cols = jnp.stack(
        [pick(kv_sum, me.y, 0)] + [y_permute(pick(kv_sum, (me.y + d) % 4, 0), d) for d in (1, 2, 3)]
    )
    kv_cols = jnp.concatenate([pick(kv_cols, (me.y - h) % 4, 0) for h in range(4)], axis=1)
    kv_cols = kv_cols.reshape(32, 4, 2, 64)
    key_grad = kv_cols[:, :, 0, :].reshape(32, 256)
    value_grad = kv_cols[:, :, 1, :].reshape(32, 256)

    normed_back = jnp.sum(normed_terms.astype(F32), axis=0)
    scale_mine = part(scale_one, me.y * SUB, SUB, 0)
    scaled_back = normed_back * attn_gain[None, :]
    inner_one = jnp.sum(scaled_back * in_mine, axis=1, keepdims=True)
    in_grad_mine = (
        resid_back + scale_mine * scaled_back - in_mine * scale_mine**3 * inner_one / D
    ).astype(BF)
    attn_gain_part = jnp.sum(normed_back * in_mine * scale_mine, axis=0, keepdims=True)
    gain_parts = jnp.concatenate([attn_gain_part, ffn_gain_part, jnp.zeros((6, D), F32)], axis=0)
    layer_output, input_grad, gain_terms = exchange(
        "leave",
        11,
        leave_plan,
        [out_mine, in_grad_mine, gain_parts],
        [SDS((ROWS, 128), BF), SDS((ROWS, 128), BF), SDS((16, 8, 128), F32)],
    )
    (gain_toks,) = exchange(
        "gains", 12, gains_plan, [jnp.sum(gain_terms, axis=0)], [SDS((8, 8, 128), F32)]
    )
    gain_grads = part(jnp.sum(gain_toks, axis=0), me.tok * 16, 16, 1)
    return (
        layer_output,
        input_grad,
        gain_grads[0:1],
        query_grad,
        key_grad,
        value_grad,
        output_proj_grad,
        gain_grads[1:2],
        gate_grad,
        up_grad,
        down_grad,
    )


def solution(mesh):
    in_specs = (
        P("tok", ("narrow", "wide")),
        P("tok", None),
        P(),
        P(None, ("narrow", "wide")),
        P(None, "narrow"),
        P(None, "narrow"),
        P(None, ("narrow", "wide")),
        P(("narrow", "wide")),
        P("narrow", "wide"),
        P("narrow", "wide"),
        P("wide", "narrow"),
        P("tok", ("narrow", "wide")),
    )
    out_specs = (
        P("tok", ("narrow", "wide")),
        P("tok", ("narrow", "wide")),
        P(("narrow", "wide"), "tok"),
        P("tok", ("narrow", "wide")),
        P(("tok", "wide"), "narrow"),
        P(("tok", "wide"), "narrow"),
        P("tok", ("narrow", "wide")),
        P(("narrow", "wide"), "tok"),
        P("narrow", "tok", "wide"),
        P("narrow", "tok", "wide"),
        P("wide", "tok", "narrow"),
    )
    return jax.shard_map(
        per_device, mesh=mesh, in_specs=in_specs, out_specs=out_specs, check_vma=False
    )
```

time: 2650 us -> 834 us (0.31)
  waiting for transfers between devices: 2180 us -> 164 us
  Pallas kernels: 0 us -> 381 us
  blocking collectives: 136 us -> 0 us
  matrix products: 175 us -> 85.2 us
  starting transfers between devices: 2.36 us -> 74.5 us
    reduce_scatter x13 -> x0, waiting for transfers between devices: 1630 us -> none  [the longest x2 525 us: head_total(): lax.psum_scatter(term, ('narrow', 'wide'), scatter_dimension=1, tiled=True)]
    all_gather x7 -> x0, waiting for transfers between devices: 514 us -> none  [the longest x2 334 us: gather_rows(): return lax.all_gather(shard_part, ('narrow', 'wide'), axis=1, tiled=True)]
    pallas_call x0 -> x15, Pallas kernels: none -> 381 us  [the longest x13 368 us: exchange(): pl.pallas_call(body, name=name, out_shape=outs, in_specs=[pl.BlockSpec(me...]
    ppermute x0 -> x54, waiting for transfers between devices: none -> 164 us  [the longest x9 129 us: x_permute(): lax.ppermute(value, ('narrow', 'wide'), [(i, i ^ 9) for i in range(16)])]
    psum x3 -> x0, blocking collectives: 136 us -> none  [row_total(): return lax.psum(term, ('narrow', 'wide'))]
    ppermute x0 -> x54, starting transfers between devices: none -> 74.5 us  [the longest x18 29.4 us: z_permute(): return lax.ppermute(value, 'tok', [(i, (i + 2 * d) % 8) for i in range(8)])]
    dot_general x28 -> x5, matrix products: 80.5 us -> 23.6 us  [multiply(): return jnp.dot(left_side, right_side, preferred_element_type=F32)]
    unnamed x24 -> x0, waiting for transfers between devices: 33 us -> none
  transfers between devices with their start and end apart: 22 -> 54, of which waited for: 20 -> 20; matrix products, arithmetic and copies ran while one was open for 5% -> 12% of each run, Pallas kernels for 0% -> 25%
where the time goes in v1:
time: 834 us; the launch traced here: 825 us
  Pallas kernels  381 us (46%)
  waiting for transfers between devices  164 us (20%)
  matrix products  85.2 us (10%)
  starting transfers between devices  74.5 us (9%)
  local copies, waits for them, and re-layouts  67.7 us (8%)
  other arithmetic  50.3 us (6%)
    pallas_call x13, Pallas kernels, exchange(): pl.pallas_call(body, name=name, out_shape=outs, in_specs=[pl.BlockSpec(me...  368 us
    ppermute x9, waiting for transfers between devices, x_permute(): lax.ppermute(value, ('narrow', 'wide'), [(i, i ^ 9) for i in range(16)])  129 us
    dot_general x6, matrix products, contract_cols(): lax.dot_general(left_side, right_side, (((1,), (1,)), ((), ())), preferre...  37 us
    ppermute x18, starting transfers between devices, z_permute(): return lax.ppermute(value, 'tok', [(i, (i + 2 * d) % 8) for i in range(8)])  29.4 us
    dot_general x5, matrix products, contract_rows(): lax.dot_general(left_side, right_side, (((0,), (0,)), ((), ())), preferre...  24.6 us
    dot_general x5, matrix products, multiply(): return jnp.dot(left_side, right_side, preferred_element_type=F32)  23.6 us
    dynamic_slice x7, local copies, waits for them, and re-layouts, part(): return lax.dynamic_slice_in_dim(array, start, size, axis)  20.7 us
    unnamed x173, local copies, waits for them, and re-layouts  20.5 us
  transfers between devices with their start and end apart: 54, of which 20 were waited for; matrix products, arithmetic and copies ran while one was open for 12% of the time, Pallas kernels for 25%

profile of v1, /device:TPU:0, one launch (start us, length us, event | category | flops | bytes accessed | tf_op | source)
XLA Modules:
  0.0 825.0 jit_solution(7101073373718507351)
XLA Ops:
  8.4 43.9 %enter.1 = (bf16[384,2048]{1,0:T(8,128)(2,1)S(1)}, bf16[2048,768]{1,0:T(8,128)(2,1)S(1)}, f32[16,8,128]{2,1,0:T(8,128)S(1)}) custom-call(bf16[1536,128]{1,0:T(8,128)(2,1)S(1)} %copy-done.13, bf16[2048,128]{1,0:T(8,128)(2,1)S(1)} %copy-done.12, bf16[2048,128]{1,0:T(8,128)(2,1)S(1)} %pad_maximum_fusion.1.refs_2_, f32[8,128]{1,0:T(8,128)S(1)} %broadcast_in_dim.8.refs_3_), custom_call_target="tpu_custom_call" | custom-call | tf_op jit(solution)/shard_map/enter/pallas_call | solution.py:136
  80.6 40.4 %to_heads.1 = (bf16[1536,128]{1,0:T(8,128)(2,1)S(1)}, bf16[1536,128]{1,0:T(8,128)(2,1)S(1)}) custom-call(bf16[384,768]{1,0:T(8,128)(2,1)S(1)} %concatenate.73.refs_0_), custom_call_target="tpu_custom_call" | custom-call | tf_op jit(solution)/shard_map/to_heads/pallas_call | solution.py:136
  134.4 92.4 %heads_out.1 = (bf16[384,512]{1,0:T(8,128)(2,1)S(1)}, bf16[2048,512]{1,0:T(8,128)(2,1)S(1)}) custom-call(bf16[1536,128]{1,0:T(8,128)(2,1)S(1)} %attend.1.refs_0_, bf16[2048,128]{1,0:T(8,128)(2,1)S(1)} %copy-done.11, bf16[1024,128]{1,0:T(8,128)(2,1)S(1)} %collective-permute-done.refs_2_, bf16[1024,128]{1,0:T(8,128)(2,1)S(1)} %collective-permute-done.1.refs_3_, ...), custom_call_target="tpu_custom_call" | custom-call | tf_op jit(solution)/shard_map/heads_out/pallas_call | solution.py:136
  229.2 35.6 %out_sum.1 = (bf16[4,96,2048]{2,1,0:T(8,128)(2,1)S(1)}, bf16[384,2048]{1,0:T(8,128)(2,1)S(1)}) custom-call(bf16[384,2048]{1,0:T(8,128)(2,1)S(1)} %convolution_convert_fusion.5.refs_0_, bf16[1536,128]{1,0:T(8,128)(2,1)S(1)} %copy-done.14), custom_call_target="tpu_custom_call" | custom-call | tf_op jit(solution)/shard_map/out_sum/pallas_call | solution.py:136
  268.7 20.8 %collective-permute-done.8.refs_3_ = bf16[512,1024]{1,0:T(8,128)(2,1)S(1)} collective-permute-done((bf16[512,1024]{1,0:T(8,128)(2,1)}, bf16[512,1024]{1,0:T(8,128)(2,1)S(1)}, u32[]{:S(2)}, u32[]{:S(2)}) %collective-permute-start.8) | collective-permute-done | bytes 1048608 | tf_op jit(solution)/shard_map/ppermute | solution.py:473
  311.3 28.8 %ffn_enter.1 = (bf16[384,2048]{1,0:T(8,128)(2,1)S(1)}, bf16[2048,2048]{1,0:T(8,128)(2,1)}, bf16[2048,2048]{1,0:T(8,128)(2,1)}) custom-call(bf16[96,2048]{1,0:T(8,128)(2,1)S(1)} %multiply_convert_fusion.3.refs_0_, bf16[1024,1024]{1,0:T(8,128)(2,1)S(1)} %copy-done.3, bf16[1024,1024]{1,0:T(8,128)(2,1)S(1)} %copy-done.4, bf16[2,512,1024]{2,1,0:T(8,128)(2,1)S(1)} %copy-done.6, ...), custom_call_target="tpu_custom_call" | custom-call | tf_op jit(solution)/shard_map/ffn_enter/pallas_call | solution.py:136
  340.1 8.6 %fusion.84 = f32[384,2048]{1,0:T(8,128)} fusion(bf16[384,2048]{1,0:T(8,128)(2,1)S(1)} %get-tuple-element.45, bf16[2048,2048]{1,0:T(8,128)(2,1)} %get-tuple-element.47), kind=kOutput, calls=%fused_computation.252 | convolution fusion | flops 3221225472 | bytes 13107200 | tf_op jit(solution)/shard_map/dot_general | solution.py:551
  358.6 18.7 %fusion.86 = f32[384,2048]{1,0:T(8,128)S(1)} fusion(bf16[384,2048]{1,0:T(8,128)(2,1)S(1)} %get-tuple-element.81, bf16[2048,2048]{1,0:T(8,128)(2,1)} %get-tuple-element.47), kind=kOutput, calls=%fused_computation.254 | convolution fusion | flops 3221225472 | bytes 13107200 | tf_op jit(solution)/shard_map/dot_general | solution.py:545
  377.3 6.8 add_convert_fusion.1.refs_1_
  384.1 37.6 %ffn_sum.1 = (bf16[4,96,2048]{2,1,0:T(8,128)(2,1)S(1)}, bf16[4,96,2048]{2,1,0:T(8,128)(2,1)S(1)}) custom-call(bf16[384,2048]{1,0:T(8,128)(2,1)S(1)} %convolution_convert_fusion.4.refs_0_, bf16[384,2048]{1,0:T(8,128)(2,1)S(1)} %add_convert_fusion.1.refs_1_), custom_call_target="tpu_custom_call" | custom-call | tf_op jit(solution)/shard_map/ffn_sum/pallas_call | solution.py:136
  424.7 20.1 %mix_gather.1 = bf16[384,2048]{1,0:T(8,128)(2,1)S(1)} custom-call(bf16[96,2048]{1,0:T(8,128)(2,1)S(1)} %get-tuple-element.63.refs_0_), custom_call_target="tpu_custom_call" | custom-call | tf_op jit(solution)/shard_map/mix_gather/pallas_call | solution.py:136
  445.9 8.2 heads_back.1.back_ref
  454.2 7.7 attend_back.1
  461.9 10.4 %grads_out.1 = bf16[384,1024]{1,0:T(8,128)(2,1)S(1)} custom-call(bf16[1536,128]{1,0:T(8,128)(2,1)S(1)} %get-tuple-element.52.refs_0_, bf16[1536,128]{1,0:T(8,128)(2,1)S(1)} %get-tuple-element.53.refs_1_), custom_call_target="tpu_custom_call" | custom-call | tf_op jit(solution)/shard_map/grads_out/pallas_call | solution.py:136
  480.1 7.2 convolution_convert_fusion.2
  487.3 6.8 convolution_convert_fusion.1
  494.1 6.9 convolution_convert_fusion
  501.6 20.2 %normed_sum.1 = bf16[4,96,2048]{2,1,0:T(8,128)(2,1)S(1)} custom-call(bf16[384,2048]{1,0:T(8,128)(2,1)S(1)} %add_convert_fusion.refs_0_), custom_call_target="tpu_custom_call" | custom-call | tf_op jit(solution)/shard_map/normed_sum/pallas_call | solution.py:136
  568.0 19.2 %leave.1 = (bf16[1536,128]{1,0:T(8,128)(2,1)S(1)}, bf16[1536,128]{1,0:T(8,128)(2,1)S(1)}, f32[16,8,128]{2,1,0:T(8,128)S(1)}) custom-call(bf16[96,2048]{1,0:T(8,128)(2,1)S(1)} %get-tuple-element.146.refs_0_, bf16[96,2048]{1,0:T(8,128)(2,1)S(1)} %fusion.29.refs_1_, f32[8,2048]{1,0:T(8,128)S(1)} %maximum_maximum_fusion.refs_2_), custom_call_target="tpu_custom_call" | custom-call | tf_op jit(solution)/shard_map/leave/pallas_call | solution.py:136
  615.8 9.4 %collective-permute-done.12 = bf16[4,256,128]{2,1,0:T(8,128)(2,1)S(1)} collective-permute-done((bf16[4,256,128]{2,1,0:T(8,128)(2,1)S(1)}, bf16[4,256,128]{2,1,0:T(8,128)(2,1)S(1)}, u32[]{:S(2)}, u32[]{:S(2)}) %collective-permute-start.12) | collective-permute-done | bytes 262176 | tf_op jit(solution)/shard_map/ppermute | solution.py:473
  674.3 39.5 %collective-permute-done.36 = bf16[8,4,16,1024]{3,2,0,1:T(8,128)(2,1)} collective-permute-done((bf16[8,4,16,1024]{3,2,0,1:T(8,128)(2,1)}, bf16[8,4,16,1024]{3,2,0,1:T(8,128)(2,1)}, u32[]{:S(2)}, u32[]{:S(2)}) %collective-permute-start.36) | collective-permute-done | bytes 1048608 | tf_op jit(solution)/shard_map/ppermute | solution.py:473
  722.6 36.1 %collective-permute-done.43 = bf16[8,4,16,1024]{3,2,0,1:T(8,128)(2,1)} collective-permute-done((bf16[8,4,16,1024]{3,2,0,1:T(8,128)(2,1)}, bf16[8,4,16,1024]{3,2,0,1:T(8,128)(2,1)}, u32[]{:S(2)}, u32[]{:S(2)}) %collective-permute-start.43) | collective-permute-done | bytes 1048608 | tf_op jit(solution)/shard_map/ppermute | solution.py:473
  770.5 21.5 %collective-permute-done.50 = bf16[8,4,16,1024]{3,2,0,1:T(8,128)(2,1)S(1)} collective-permute-done((bf16[8,4,16,1024]{3,2,0,1:T(8,128)(2,1)S(1)}, bf16[8,4,16,1024]{3,2,0,1:T(8,128)(2,1)S(1)}, u32[]{:S(2)}, u32[]{:S(2)}) %collective-permute-start.50) | collective-permute-done | bytes 1048608 | tf_op jit(solution)/shard_map/ppermute | solution.py:473
  810.1 7.8 collective-permute-done.44
  (380 shorter events, 267.6 us)
Async XLA Ops:
  54.0 75.4 %collective-permute-start = (bf16[1024,128]{1,0:T(8,128)(2,1)}, bf16[1024,128]{1,0:T(8,128)(2,1)S(1)}, u32[]{:S(2)}, u32[]{:S(2)}) collective-permute-start(bf16[1024,128]{1,0:T(8,128)(2,1)} %constant_dynamic-slice_fusion.26), channel_id=1, source_target_pairs={{0,8},{8,0},{1,9},{9,1},{2,10},{10,2},{3,11},{11,3},{4,12},{12,4},... | collective-permute-start | bytes 786440 | tf_op jit(solution)/shard_map/ppermute | solution.py:470
  54.8 74.9 %collective-permute-start.1 = (bf16[1024,128]{1,0:T(8,128)(2,1)}, bf16[1024,128]{1,0:T(8,128)(2,1)S(1)}, u32[]{:S(2)}, u32[]{:S(2)}) collective-permute-start(bf16[1024,128]{1,0:T(8,128)(2,1)} %constant_dynamic-slice_fusion.26), channel_id=1, source_target_pairs={{0,1},{1,0},{2,3},{3,2},{4,5},{5,4},{6,7},{7,6},{8,9},{9,8},{10,11... | collective-permute-start | bytes 786440 | tf_op jit(solution)/shard_map/ppermute | solution.py:472
  57.4 74.9 %collective-permute-start.2 = (bf16[1024,128]{1,0:T(8,128)(2,1)}, bf16[1024,128]{1,0:T(8,128)(2,1)}, u32[]{:S(2)}, u32[]{:S(2)}) collective-permute-start(bf16[1024,128]{1,0:T(8,128)(2,1)} %constant_dynamic-slice_fusion.26), channel_id=1, source_target_pairs={{0,9},{1,8},{2,11},{3,10},{4,13},{5,12},{6,15},{7,14},{8,1},{9,0},... | collective-permute-start | bytes 786440 | tf_op jit(solution)/shard_map/ppermute | solution.py:473
  58.7 206.2 %collective-permute-start.6 = (bf16[512,1024]{1,0:T(8,128)(2,1)}, bf16[512,1024]{1,0:T(8,128)(2,1)}, u32[]{:S(2)}, u32[]{:S(2)}) collective-permute-start(bf16[512,1024]{1,0:T(8,128)(2,1)} %constant_dynamic-slice_fusion.25), channel_id=1, source_target_pairs={{0,8},{8,0},{1,9},{9,1},{2,10},{10,2},{3,11},{11,3},{4,12},{12,4},... | collective-permute-start | bytes 3145736 | tf_op jit(solution)/shard_map/ppermute | solution.py:470
  58.7 210.0 %collective-permute-start.7 = (bf16[512,1024]{1,0:T(8,128)(2,1)}, bf16[512,1024]{1,0:T(8,128)(2,1)}, u32[]{:S(2)}, u32[]{:S(2)}) collective-permute-start(bf16[512,1024]{1,0:T(8,128)(2,1)} %constant_dynamic-slice_fusion.25), channel_id=1, source_target_pairs={{0,1},{1,0},{2,3},{3,2},{4,5},{5,4},{6,7},{7,6},{8,9},{9,8},{10,11... | collective-permute-start | bytes 3145736 | tf_op jit(solution)/shard_map/ppermute | solution.py:472
  129.4 173.1 %collective-permute-start.3 = (bf16[2,512,1024]{2,1,0:T(8,128)(2,1)}, bf16[2,512,1024]{2,1,0:T(8,128)(2,1)S(1)}, u32[]{:S(2)}, u32[]{:S(2)}) collective-permute-start(bf16[2,512,1024]{2,1,0:T(8,128)(2,1)} %pad_maximum_fusion), channel_id=1, source_target_pairs={{0,8},{8,0},{1,9},{9,1},{2,10},{10,2},{3,11},{11,3},{4,12},{12,4},... | collective-permute-start | bytes 6291464 | tf_op jit(solution)/shard_map/ppermute | solution.py:470
  129.7 174.1 %collective-permute-start.4 = (bf16[2,512,1024]{2,1,0:T(8,128)(2,1)}, bf16[2,512,1024]{2,1,0:T(8,128)(2,1)S(1)}, u32[]{:S(2)}, u32[]{:S(2)}) collective-permute-start(bf16[2,512,1024]{2,1,0:T(8,128)(2,1)} %pad_maximum_fusion), channel_id=1, source_target_pairs={{0,1},{1,0},{2,3},{3,2},{4,5},{5,4},{6,7},{7,6},{8,9},{9,8},{10,11... | collective-permute-start | bytes 6291464 | tf_op jit(solution)/shard_map/ppermute | solution.py:472
  132.3 172.9 %collective-permute-start.5 = (bf16[2,512,1024]{2,1,0:T(8,128)(2,1)}, bf16[2,512,1024]{2,1,0:T(8,128)(2,1)S(1)}, u32[]{:S(2)}, u32[]{:S(2)}) collective-permute-start(bf16[2,512,1024]{2,1,0:T(8,128)(2,1)} %pad_maximum_fusion), channel_id=1, source_target_pairs={{0,9},{1,8},{2,11},{3,10},{4,13},{5,12},{6,15},{7,14},{8,1},{9,0},... | collective-permute-start | bytes 6291464 | tf_op jit(solution)/shard_map/ppermute | solution.py:473
  527.0 120.6 %collective-permute-start.33 = (bf16[2,8,4,16,2048]{4,3,1,2,0:T(8,128)(2,1)}, bf16[2,8,4,16,2048]{4,3,1,2,0:T(8,128)(2,1)}, u32[]{:S(2)}, u32[]{:S(2)}) collective-permute-start(bf16[2,8,4,16,2048]{4,3,1,2,0:T(8,128)(2,1)} %copy_bitcast_fusion.2), channel_id=1, source_target_pairs={{0,16},{16,0},{32,48},{48,32},{64,80},{80,64},{96,112},{112,96},{1... | collective-permute-start | bytes 12582920 | tf_op jit(solution)/shard_map/ppermute | solution.py:485
  532.5 125.3 %collective-permute-start.40 = (bf16[2,8,4,16,2048]{4,3,1,2,0:T(8,128)(2,1)}, bf16[2,8,4,16,2048]{4,3,1,2,0:T(8,128)(2,1)}, u32[]{:S(2)}, u32[]{:S(2)}) collective-permute-start(bf16[2,8,4,16,2048]{4,3,1,2,0:T(8,128)(2,1)} %copy_bitcast_fusion.1), channel_id=1, source_target_pairs={{0,16},{16,0},{32,48},{48,32},{64,80},{80,64},{96,112},{112,96},{1... | collective-permute-start | bytes 12582920 | tf_op jit(solution)/shard_map/ppermute | solution.py:485
  551.7 54.4 %collective-permute-start.9 = (bf16[4,256,512]{2,1,0:T(8,128)(2,1)}, bf16[4,256,512]{2,1,0:T(8,128)(2,1)}, u32[]{:S(2)}, u32[]{:S(2)}) collective-permute-start(bf16[4,256,512]{2,1,0:T(8,128)(2,1)} %get-tuple-element.106), channel_id=1, source_target_pairs={{0,16},{16,0},{32,48},{48,32},{64,80},{80,64},{96,112},{112,96},{1... | collective-permute-start | bytes 3145736 | tf_op jit(solution)/shard_map/ppermute | solution.py:485
  554.3 118.0 %collective-permute-start.47 = (bf16[2,8,4,16,2048]{4,3,1,2,0:T(8,128)(2,1)}, bf16[2,8,4,16,2048]{4,3,1,2,0:T(8,128)(2,1)}, u32[]{:S(2)}, u32[]{:S(2)}) collective-permute-start(bf16[2,8,4,16,2048]{4,3,1,2,0:T(8,128)(2,1)} %copy_bitcast_fusion), channel_id=1, source_target_pairs={{0,16},{16,0},{32,48},{48,32},{64,80},{80,64},{96,112},{112,96},{1... | collective-permute-start | bytes 12582920 | tf_op jit(solution)/shard_map/ppermute | solution.py:485
  563.5 49.5 %collective-permute-start.26 = (bf16[4,256,512]{2,1,0:T(8,128)(2,1)}, bf16[4,256,512]{2,1,0:T(8,128)(2,1)}, u32[]{:S(2)}, u32[]{:S(2)}) collective-permute-start(bf16[4,256,512]{2,1,0:T(8,128)(2,1)} %get-tuple-element.101), channel_id=1, source_target_pairs={{0,16},{16,0},{32,48},{48,32},{64,80},{80,64},{96,112},{112,96},{1... | collective-permute-start | bytes 3145736 | tf_op jit(solution)/shard_map/ppermute | solution.py:485
  657.8 56.1 %collective-permute-start.36 = (bf16[8,4,16,1024]{3,2,0,1:T(8,128)(2,1)}, bf16[8,4,16,1024]{3,2,0,1:T(8,128)(2,1)}, u32[]{:S(2)}, u32[]{:S(2)}) collective-permute-start(bf16[8,4,16,1024]{3,2,0,1:T(8,128)(2,1)} %get-tuple-element.89), channel_id=1, source_target_pairs={{0,9},{1,8},{2,11},{3,10},{4,13},{5,12},{6,15},{7,14},{8,1},{9,0},... | collective-permute-start | bytes 3145736 | tf_op jit(solution)/shard_map/ppermute | solution.py:473
  664.8 53.6 %collective-permute-start.35 = (bf16[8,4,16,1024]{3,2,0,1:T(8,128)(2,1)}, bf16[8,4,16,1024]{3,2,0,1:T(8,128)(2,1)}, u32[]{:S(2)}, u32[]{:S(2)}) collective-permute-start(bf16[8,4,16,1024]{3,2,0,1:T(8,128)(2,1)} %get-tuple-element.90), channel_id=1, source_target_pairs={{0,1},{1,0},{2,3},{3,2},{4,5},{5,4},{6,7},{7,6},{8,9},{9,8},{10,11... | collective-permute-start | bytes 3145736 | tf_op jit(solution)/shard_map/ppermute | solution.py:472
  666.9 51.6 %collective-permute-start.34 = (bf16[8,4,16,1024]{3,2,0,1:T(8,128)(2,1)}, bf16[8,4,16,1024]{3,2,0,1:T(8,128)(2,1)}, u32[]{:S(2)}, u32[]{:S(2)}) collective-permute-start(bf16[8,4,16,1024]{3,2,0,1:T(8,128)(2,1)} %get-tuple-element.88), channel_id=1, source_target_pairs={{0,8},{8,0},{1,9},{9,1},{2,10},{10,2},{3,11},{11,3},{4,12},{12,4},... | collective-permute-start | bytes 3145736 | tf_op jit(solution)/shard_map/ppermute | solution.py:470
  667.8 91.0 %collective-permute-start.43 = (bf16[8,4,16,1024]{3,2,0,1:T(8,128)(2,1)}, bf16[8,4,16,1024]{3,2,0,1:T(8,128)(2,1)}, u32[]{:S(2)}, u32[]{:S(2)}) collective-permute-start(bf16[8,4,16,1024]{3,2,0,1:T(8,128)(2,1)} %get-tuple-element.86), channel_id=1, source_target_pairs={{0,9},{1,8},{2,11},{3,10},{4,13},{5,12},{6,15},{7,14},{8,1},{9,0},... | collective-permute-start | bytes 3145736 | tf_op jit(solution)/shard_map/ppermute | solution.py:473
  672.3 90.6 %collective-permute-start.42 = (bf16[8,4,16,1024]{3,2,0,1:T(8,128)(2,1)}, bf16[8,4,16,1024]{3,2,0,1:T(8,128)(2,1)S(1)}, u32[]{:S(2)}, u32[]{:S(2)}) collective-permute-start(bf16[8,4,16,1024]{3,2,0,1:T(8,128)(2,1)} %get-tuple-element.87), channel_id=1, source_target_pairs={{0,1},{1,0},{2,3},{3,2},{4,5},{5,4},{6,7},{7,6},{8,9},{9,8},{10,11... | collective-permute-start | bytes 3145736 | tf_op jit(solution)/shard_map/ppermute | solution.py:472
  713.8 52.5 %collective-permute-start.41 = (bf16[8,4,16,1024]{3,2,0,1:T(8,128)(2,1)}, bf16[8,4,16,1024]{3,2,0,1:T(8,128)(2,1)S(1)}, u32[]{:S(2)}, u32[]{:S(2)}) collective-permute-start(bf16[8,4,16,1024]{3,2,0,1:T(8,128)(2,1)} %get-tuple-element.85), channel_id=1, source_target_pairs={{0,8},{8,0},{1,9},{9,1},{2,10},{10,2},{3,11},{11,3},{4,12},{12,4},... | collective-permute-start | bytes 3145736 | tf_op jit(solution)/shard_map/ppermute | solution.py:470
  718.5 73.6 %collective-permute-start.50 = (bf16[8,4,16,1024]{3,2,0,1:T(8,128)(2,1)S(1)}, bf16[8,4,16,1024]{3,2,0,1:T(8,128)(2,1)S(1)}, u32[]{:S(2)}, u32[]{:S(2)}) collective-permute-start(bf16[8,4,16,1024]{3,2,0,1:T(8,128)(2,1)S(1)} %get-tuple-element.83), channel_id=1, source_target_pairs={{0,9},{1,8},{2,11},{3,10},{4,13},{5,12},{6,15},{7,14},{8,1},{9,0},... | collective-permute-start | bytes 3145736 | tf_op jit(solution)/shard_map/ppermute | solution.py:473
  718.6 75.7 %collective-permute-start.49 = (bf16[8,4,16,1024]{3,2,0,1:T(8,128)(2,1)S(1)}, bf16[8,4,16,1024]{3,2,0,1:T(8,128)(2,1)S(1)}, u32[]{:S(2)}, u32[]{:S(2)}) collective-permute-start(bf16[8,4,16,1024]{3,2,0,1:T(8,128)(2,1)S(1)} %get-tuple-element.84), channel_id=1, source_target_pairs={{0,1},{1,0},{2,3},{3,2},{4,5},{5,4},{6,7},{7,6},{8,9},{9,8},{10,11... | collective-permute-start | bytes 3145736 | tf_op jit(solution)/shard_map/ppermute | solution.py:472
  758.7 39.9 %collective-permute-start.48 = (bf16[8,4,16,1024]{3,2,0,1:T(8,128)(2,1)S(1)}, bf16[8,4,16,1024]{3,2,0,1:T(8,128)(2,1)S(1)}, u32[]{:S(2)}, u32[]{:S(2)}) collective-permute-start(bf16[8,4,16,1024]{3,2,0,1:T(8,128)(2,1)S(1)} %get-tuple-element.82), channel_id=1, source_target_pairs={{0,8},{8,0},{1,9},{9,1},{2,10},{10,2},{3,11},{11,3},{4,12},{12,4},... | collective-permute-start | bytes 3145736 | tf_op jit(solution)/shard_map/ppermute | solution.py:470
  763.0 40.8 %collective-permute-start.39 = (bf16[8,16,1024]{2,1,0:T(8,128)(2,1)S(1)}, bf16[8,16,1024]{2,1,0:T(8,128)(2,1)S(1)}, u32[]{:S(2)}, u32[]{:S(2)}) collective-permute-start(bf16[8,16,1024]{2,1,0:T(8,128)(2,1)S(1)} %get-tuple-element.142), channel_id=1, source_target_pairs={{0,96},{16,112},{32,0},{48,16},{64,32},{80,48},{96,64},{112,80},{1... | collective-permute-start | bytes 786440 | tf_op jit(solution)/shard_map/ppermute | solution.py:477
  766.3 38.2 %collective-permute-start.38 = (bf16[8,16,1024]{2,1,0:T(8,128)(2,1)S(1)}, bf16[8,16,1024]{2,1,0:T(8,128)(2,1)S(1)}, u32[]{:S(2)}, u32[]{:S(2)}) collective-permute-start(bf16[8,16,1024]{2,1,0:T(8,128)(2,1)S(1)} %get-tuple-element.143), channel_id=1, source_target_pairs={{0,64},{16,80},{32,96},{48,112},{64,0},{80,16},{96,32},{112,48},{1... | collective-permute-start | bytes 786440 | tf_op jit(solution)/shard_map/ppermute | solution.py:477
  (114 other events, 1119.3 us)

commit v2 on v1

--- a/solution.py
+++ b/solution.py
@@ -163,10 +163,13 @@
     return pl.ds(pl.multiple_of(index * size, size), size)
 
 
-def spread_plan(me, src, dst):
-    local = [(src.at[rows(me.chunk * CHUNK, CHUNK), :], dst.at[:, lanes(me.block)])]
+def spread_plan(me, src, dst, own_first=False):
+    def block(off):
+        return lanes(off[2] * 8 + me.wide if own_first else me.block)
+
+    local = [(src.at[rows(me.chunk * CHUNK, CHUNK), :], dst.at[:, block(HERE)])]
     sends = [
-        (off, src.at[rows(me.at(off).chunk * CHUNK, CHUNK), :], dst.at[:, lanes(me.block)], [])
+        (off, src.at[rows(me.at(off).chunk * CHUNK, CHUNK), :], dst.at[:, block(off)], [])
         for off in PLANE[1:]
     ]
     return local, sends
@@ -267,7 +270,7 @@
 
 def out_sum_plan(me, ins, outs):
     local, sends = scatter_moves(me, ins[0], outs[0])
-    local2, sends2 = spread_plan(me, ins[1], outs[1])
+    local2, sends2 = spread_plan(me, ins[1], outs[1], True)
     return local + local2, sends + sends2
 
 
@@ -500,15 +503,14 @@
     return out
 
 
-def reduce_ffn(me, partial, rows_by_xl):
+def reduce_ffn(me, partial):
     view = partial.reshape(2, 8, 4, 2, 16, 2048)
     mine = pick(view, me.core, 3)
     came = core_permute(pick(view, 1 - me.core, 3))
 
     def quarter(k):
-        there = me.at(XOFF[k])
-        r, c = (there.xl, there.xh) if rows_by_xl else (there.xh, there.xl)
-        return total([part(pick(a, r, 0), c * 1024, 1024, 3) for a in (mine, came)])
+        r, c = XOFF[k][2], XOFF[k][4]
+        return total([a[r, ..., c * 1024 : c * 1024 + 1024] for a in (mine, came)])
 
     own = quarter(0)
     got = [x_permute(quarter(k).astype(BF), k) for k in (1, 2, 3)]
@@ -549,6 +551,391 @@
 
 def multiply(left_side, right_side):
     return jnp.dot(left_side, right_side, preferred_element_type=F32)
+
+
+class Wire:
+    def __init__(self, me, send_sem, recv_sem):
+        self.me, self.send_sem, self.recv_sem, self.used = me, send_sem, recv_sem, 0
+
+    def send(self, off, src, dst):
+        copy = pltpu.make_async_remote_copy(
+            src_ref=src,
+            dst_ref=dst,
+            send_sem=self.send_sem.at[self.used],
+            recv_sem=self.recv_sem.at[self.used],
+            device_id=self.me.at(off).device(),
+            device_id_type=MESH,
+        )
+        copy.start()
+        self.used += 1
+        return copy
+
+
+def meet(me, offsets):
+    barrier = pltpu.get_barrier_semaphore()
+    for off in offsets:
+        back = tuple(-v for v in off)
+        pl.semaphore_signal(barrier, inc=1, device_id=me.at(back).device(), device_id_type=MESH)
+    pl.semaphore_wait(barrier, len(offsets))
+
+
+def finish(copies):
+    for copy in copies:
+        copy.wait()
+
+
+ZOFF = [(0, d, 0, 0, 0) for d in range(4)]
+
+
+def weights_body(pieces, whole, send_sem, recv_sem):
+    me = whereami()
+    wire = Wire(me, send_sem, recv_sem)
+    meet(me, XOFF[1:] + ZOFF[1:] + [SIBLING])
+    over_x = [wire.send(XOFF[k], pieces, whole.at[k - 1, :, me.tok]) for k in (1, 2, 3)]
+    over_z, over_core = [], []
+    for k in (1, 2, 3):
+        over_x[k - 1].wait_recv()
+        block = whole.at[k - 1, :, me.tok]
+        over_core.append(wire.send(SIBLING, block, block))
+        over_z.append([wire.send(ZOFF[d], block, block) for d in (1, 2, 3)])
+    for k in (1, 2, 3):
+        for d in (1, 2, 3):
+            over_z[k - 1][d - 1].wait_recv()
+            block = whole.at[k - 1, :, (me.z - d + 4) % 4 * 2 + me.core]
+            over_core.append(wire.send(SIBLING, block, block))
+    for copy in over_x:
+        copy.wait_send()
+    for copies in over_z:
+        for copy in copies:
+            copy.wait_send()
+    finish(over_core)
+
+
+def gather_weights(pieces):
+    return pl.pallas_call(
+        weights_body,
+        name="weights",
+        out_shape=SDS((3, 3, 8, 128, 1024), BF),
+        in_specs=[pl.BlockSpec(memory_space=pl.ANY)],
+        out_specs=pl.BlockSpec(memory_space=pl.ANY),
+        scratch_shapes=[pltpu.SemaphoreType.DMA((24,)), pltpu.SemaphoreType.DMA((24,))],
+        compiler_params=pltpu.CompilerParams(collective_id=13, has_side_effects=True),
+    )(pieces)
+
+
+class PairSum:
+    def __init__(self, me, left, right, terms, came, send_sem, recv_sem):
+        self.me, self.left, self.right, self.terms, self.came = me, left, right, terms, came
+        self.send_sem, self.recv_sem = send_sem, recv_sem
+
+    def copy(self, i):
+        return pltpu.make_async_remote_copy(
+            src_ref=self.terms.at[i, :, :, 1 - self.me.core],
+            dst_ref=self.came.at[i],
+            send_sem=self.send_sem.at[i],
+            recv_sem=self.recv_sem.at[i],
+            device_id=self.me.at(SIBLING).device(),
+            device_id_type=MESH,
+        )
+
+    def multiply(self, first, last):
+        def step(i, _):
+            cols = pl.ds(pl.multiple_of(i * 256, 256), 256)
+            block = contract_rows(self.left[:, cols], self.right[...])
+            self.terms[i] = block.astype(BF).reshape(2, 4, 2, 16, 2048)
+            self.copy(i).start()
+            return 0
+
+        lax.fori_loop(first, last, step, 0)
+
+    def add(self, first, last):
+        def step(i, _):
+            copy = self.copy(i)
+            copy.wait_recv()
+            mine = self.terms[i, :, :, self.me.core].astype(F32) + self.came[i].astype(F32)
+            self.terms[i, :, :, self.me.core] = mine.astype(BF)
+            return 0
+
+        lax.fori_loop(first, last, step, 0)
+
+    def sent(self):
+        def step(i, _):
+            self.copy(i).wait_send()
+            return 0
+
+        lax.fori_loop(0, 8, step, 0)
+
+
+def ffn_body(
+    mine_ref,
+    grad_ref,
+    resid_ref,
+    scale_ref,
+    gain_ref,
+    w_out_ref,
+    own_gate,
+    own_up,
+    own_down,
+    whole,
+    out_mine,
+    resid_back,
+    gain_part,
+    mix_full,
+    heads_back,
+    ffn_in,
+    up_back,
+    down_own,
+    down_came,
+    gate_own,
+    gate_came,
+    turned,
+    act,
+    gate_back,
+    gate_tile,
+    up_tile,
+    down_tile,
+    down_acc,
+    ffn_acc,
+    down_send,
+    ffn_send,
+    down_recv,
+    ffn_recv,
+    mix_mine,
+    back_cat,
+    down_terms,
+    gate_terms,
+    came,
+    send_sem,
+    recv_sem,
+    core_send,
+    core_recv,
+    tile_sem,
+    local_sem,
+    ack,
+):
+    me = whereami()
+    wire = Wire(me, send_sem, recv_sem)
+    half = [lanes(me.xl, 1024), lanes(1 - me.xl, 1024)]
+    here = rows(me.y * SUB, SUB)
+
+    def tile_copies(e, q, slot):
+        copies = []
+        cols = pl.ds(pl.multiple_of(q * 256, 256), 256)
+        for dxl in range(2):
+            k = e * 2 + dxl
+            for j, (own, tile) in enumerate(
+                ((own_gate, gate_tile), (own_up, up_tile), (own_down, down_tile))
+            ):
+                block = own if k == 0 else whole.at[k - 1, j]
+                if j < 2:
+                    src, dst = block.at[:, :, cols], tile.at[slot, dxl]
+                else:
+                    src = block.at[pl.ds(q * 2, 2)]
+                    dst = tile.at[slot, :, :, dxl * 1024 : dxl * 1024 + 1024]
+                copies.append(pltpu.make_async_copy(src, dst, tile_sem.at[slot, dxl * 3 + j]))
+        return copies
+
+    def fetch(e, q, slot):
+        for copy in tile_copies(e, q, slot):
+            copy.start()
+
+    meet(me, YOFF[1:] + XOFF[1:] + ZOFF[1:] + [SIBLING])
+    for h in range(2):
+        turned[:, h * 1024 : h * 1024 + 1024] = mine_ref[:, half[h]]
+    gathers = [wire.send(off, turned, ffn_in.at[here, :]) for off in YOFF[1:]]
+    fetch(0, 0, 0)
+    ffn_in[here, :] = turned[...]
+    down_acc[...] = jnp.zeros(down_acc.shape, F32)
+    ffn_acc[...] = jnp.zeros(ffn_acc.shape, F32)
+    finish(gathers)
+
+    down_sum = PairSum(me, act, grad_ref, down_terms, came, core_send.at[0], core_recv.at[0])
+    gate_sum = PairSum(me, ffn_in, gate_back, gate_terms, came, core_send.at[1], core_recv.at[1])
+
+    for e in range(2):
+
+        def step(q, _, e=e):
+            slot = q % 2
+
+            @pl.when(q < 3)
+            def _():
+                fetch(e, q + 1, 1 - slot)
+
+            if e == 0:
+
+                @pl.when(q == 3)
+                def _():
+                    fetch(1, 0, 0)
+
+            for copy in tile_copies(e, q, slot):
+                copy.wait()
+            cols = pl.ds(pl.multiple_of(e * 1024 + q * 256, 256), 256)
+            w_g = gate_tile[slot].reshape(2048, 256)
+            w_u = up_tile[slot].reshape(2048, 256)
+            w_d = down_tile[slot].reshape(256, 2048)
+            gate = multiply(ffn_in[...], w_g)
+            up = multiply(ffn_in[...], w_u)
+            act_back = contract_cols(grad_ref[...], w_d)
+            sigmoid = jax.nn.sigmoid(gate)
+            silu = gate * sigmoid
+            act_here = (silu * up).astype(BF)
+            act[:, cols] = act_here
+            down_acc[...] += multiply(act_here, w_d)
+            g_back = (act_back * up * sigmoid * (1.0 + gate * (1.0 - sigmoid))).astype(BF)
+            u_back = (act_back * silu).astype(BF)
+            gate_back[:, cols] = g_back
+            up_back[:, cols] = u_back
+            ffn_acc[...] += contract_cols(g_back, w_g) + contract_cols(u_back, w_u)
+            return 0
+
+        lax.fori_loop(0, 4, step, 0)
+        if e == 0:
+            down_sum.multiply(0, 4)
+
+    ffn_send[...] = ffn_acc[...].astype(BF)
+    ffn_moves = [
+        wire.send(YOFF[d], ffn_send.at[rows(me.at(YOFF[d]).y * SUB, SUB), :], ffn_recv.at[d - 1])
+        for d in (1, 2, 3)
+    ]
+    down_sum.multiply(4, 8)
+    down_send[...] = down_acc[...].astype(BF)
+    down_moves = [
+        wire.send(YOFF[d], down_send.at[rows(me.at(YOFF[d]).y * SUB, SUB), :], down_recv.at[d - 1])
+        for d in (1, 2, 3)
+    ]
+
+    def down_block(k):
+        e, dxl = XOFF[k][4], XOFF[k][2]
+        return down_terms.at[e * 4 : e * 4 + 4, :, :, me.core, :, dxl * 1024 : dxl * 1024 + 1024]
+
+    down_sum.add(0, 4)
+    x_moves = [wire.send(XOFF[1], down_block(1), down_came.at[0])]
+    down_sum.add(4, 8)
+    x_moves += [wire.send(XOFF[k], down_block(k), down_came.at[k - 1]) for k in (2, 3)]
+    near = [pltpu.make_async_copy(down_block(0), down_own, local_sem.at[0])]
+    near[0].start()
+    pl.semaphore_signal(ack, inc=1, device_id=me.at(SIBLING).device(), device_id_type=MESH)
+
+    finish(ffn_moves)
+
+    def summed(send, recv, h):
+        cols = slice(h * 1024, h * 1024 + 1024)
+        out = send[here, cols].astype(F32)
+        for d in range(3):
+            out = out + recv[d, :, cols].astype(F32)
+        return out
+
+    scale = scale_ref[...]
+    inner = jnp.zeros((SUB, 1), F32)
+    for h in range(2):
+        back = summed(ffn_send, ffn_recv, h)
+        weighed = back * resid_ref[:, half[h]]
+        inner = inner + jnp.sum(weighed * gain_ref[:, half[h]], axis=1, keepdims=True)
+        gain_part[:, half[h]] = jnp.sum(weighed * scale, axis=0, keepdims=True)
+    pull = scale * scale * scale * inner / D
+    for h in range(2):
+        back = summed(ffn_send, ffn_recv, h)
+        grad = grad_ref[here, h * 1024 : h * 1024 + 1024].astype(F32)
+        total_back = grad + scale * gain_ref[:, half[h]] * back - resid_ref[:, half[h]] * pull
+        resid_back[:, half[h]] = total_back
+        mix_mine[:, half[h]] = total_back.astype(BF)
+    mix_full[here, :] = mix_mine[...]
+    mix_moves = [wire.send(off, mix_mine, mix_full.at[here, :]) for off in YOFF[1:]]
+
+    pl.semaphore_wait(ack, 1)
+    gate_sum.multiply(0, 8)
+    finish(down_moves)
+    for h in range(2):
+        out_mine[:, half[h]] = (resid_ref[:, half[h]] + summed(down_send, down_recv, h)).astype(BF)
+    gate_sum.add(0, 8)
+
+    def gate_block(z):
+        return gate_terms.at[:, :, z, me.core]
+
+    z_moves = [
+        wire.send(ZOFF[d], gate_block((me.z + d) % 4), gate_came.at[d - 1]) for d in (1, 2, 3)
+    ]
+    near.append(pltpu.make_async_copy(gate_block(me.z), gate_own, local_sem.at[1]))
+    near[1].start()
+
+    finish(mix_moves)
+    back_cat[...] = multiply(mix_full[...], w_out_ref[...]).astype(BF)
+    spot = rows(me.chunk * CHUNK, CHUNK)
+    head_moves = [
+        wire.send(XOFF[k], back_cat.at[:, k * 128 : k * 128 + 128], heads_back.at[spot, :])
+        for k in (1, 2, 3)
+    ]
+    heads_back[spot, :] = back_cat[:, 0:128]
+    finish(head_moves + x_moves + z_moves)
+    for copy in near:
+        copy.wait()
+    down_sum.sent()
+    gate_sum.sent()
+
+
+def ffn(ffn_mine, grad_full, resid, scale_two, gain, w_out, w_gate, w_up, w_down, whole):
+    vm = pl.BlockSpec(memory_space=pltpu.VMEM)
+    hbm = pl.BlockSpec(memory_space=pl.ANY)
+    return pl.pallas_call(
+        ffn_body,
+        name="ffn",
+        out_shape=[
+            SDS((SUB, D), BF),
+            SDS((SUB, D), F32),
+            SDS((1, D), F32),
+            SDS((CHUNK, D), BF),
+            SDS((ROWS, 128), BF),
+            SDS((CHUNK, D), BF),
+            SDS((CHUNK, D), BF),
+            SDS((4, 2, 4, 16, 1024), BF),
+            SDS((3, 4, 2, 4, 16, 1024), BF),
+            SDS((8, 2, 16, 2048), BF),
+            SDS((3, 8, 2, 16, 2048), BF),
+        ],
+        in_specs=[vm] * 6 + [hbm] * 4,
+        out_specs=[vm] * 7 + [hbm] * 4,
+        scratch_shapes=[
+            pltpu.VMEM((SUB, D), BF),
+            pltpu.VMEM((CHUNK, D), BF),
+            pltpu.VMEM((CHUNK, D), BF),
+            pltpu.VMEM((2, 2, 8, 128, 256), BF),
+            pltpu.VMEM((2, 2, 8, 128, 256), BF),
+            pltpu.VMEM((2, 2, 128, 2048), BF),
+            pltpu.VMEM((CHUNK, D), F32),
+            pltpu.VMEM((CHUNK, D), F32),
+            pltpu.VMEM((CHUNK, D), BF),
+            pltpu.VMEM((CHUNK, D), BF),
+            pltpu.VMEM((3, SUB, D), BF),
+            pltpu.VMEM((3, SUB, D), BF),
+            pltpu.VMEM((SUB, D), BF),
+            pltpu.VMEM((CHUNK, 512), BF),
+            pltpu.VMEM((8, 2, 4, 2, 16, 2048), BF),
+            pltpu.VMEM((8, 2, 4, 2, 16, 2048), BF),
+            pltpu.VMEM((8, 2, 4, 16, 2048), BF),
+            pltpu.SemaphoreType.DMA((24,)),
+            pltpu.SemaphoreType.DMA((24,)),
+            pltpu.SemaphoreType.DMA((2, 8)),
+            pltpu.SemaphoreType.DMA((2, 8)),
+            pltpu.SemaphoreType.DMA((2, 6)),
+            pltpu.SemaphoreType.DMA((2,)),
+            pltpu.SemaphoreType.REGULAR,
+        ],
+        compiler_params=pltpu.CompilerParams(
+            collective_id=14, has_side_effects=True, vmem_limit_bytes=60 * 2**20
+        ),
+        cost_estimate=pl.CostEstimate(flops=26 * 10**9, bytes_accessed=40 * 2**20, transcendentals=0),
+    )(
+        ffn_mine,
+        grad_full,
+        resid,
+        scale_two,
+        gain,
+        w_out,
+        w_gate.reshape(8, 128, 1024),
+        w_up.reshape(8, 128, 1024),
+        w_down.reshape(8, 128, 1024),
+        whole,
+    )
 
 
 def per_device(
@@ -587,14 +974,10 @@
     ffn_gain_all = gains[:, 0, :].reshape(1, D)
 
     half_out = part(w_output, me.core * 1024, 1024, 0)
-    half_gu = jnp.stack([part(w_gate, me.core * 512, 512, 0), part(w_up, me.core * 512, 512, 0)])
-    half_down = part(w_down, me.core * 512, 512, 0)
-    full_in, half_out, half_gu, half_down = lax.optimization_barrier(
-        (full_in, half_out, half_gu, half_down)
-    )
+    pieces = jnp.stack([part(w, me.tok * 128, 128, 0) for w in (w_gate, w_up, w_down)])
+    full_in, half_out, pieces = lax.optimization_barrier((full_in, half_out, pieces))
+    whole = gather_weights(pieces)
     got_out = [x_permute(half_out, k) for k in (1, 2, 3)]
-    got_gu = [x_permute(half_gu, k) for k in (1, 2, 3)]
-    got_down = [x_permute(half_down, k) for k in (1, 2, 3)]
 
     in_f = full_in.astype(F32)
     scale_one = lax.rsqrt(jnp.mean(in_f * in_f, axis=1, keepdims=True) + EPS)
@@ -639,48 +1022,33 @@
     resid = in_mine + jnp.sum(attn_terms.astype(F32), axis=0)
     scale_two = lax.rsqrt(jnp.mean(resid * resid, axis=1, keepdims=True) + EPS)
     ffn_mine = (resid * scale_two * ffn_gain_all).astype(BF)
-    ffn_input, wg, wu = exchange(
-        "ffn_enter",
-        4,
-        ffn_enter_plan,
-        [ffn_mine, w_gate, w_up] + got_gu,
-        [SDS((CHUNK, D), BF), SDS((D, D), BF), SDS((D, D), BF)],
-    )
-    gate_lin = multiply(ffn_input, wg)
-    up_lin = multiply(ffn_input, wu)
-    sigmoid_gate = jax.nn.sigmoid(gate_lin)
-    act = (gate_lin * sigmoid_gate * up_lin).astype(BF)
-    (wd,) = exchange("down_weight", 5, down_plan, [w_down] + got_down, [SDS((D, D), BF)])
-    down_term = multiply(act, wd).astype(BF)
-    act_back = contract_cols(grad_full, wd)
-    gate_back = (act_back * up_lin * sigmoid_gate * (1.0 + gate_lin * (1.0 - sigmoid_gate))).astype(
-        BF
-    )
-    up_back = (act_back * gate_lin * sigmoid_gate).astype(BF)
-    ffn_term = (contract_cols(gate_back, wg) + contract_cols(up_back, wu)).astype(BF)
-    down_terms, ffn_terms = exchange(
-        "ffn_sum",
-        6,
-        sum_plan,
-        [down_term, ffn_term],
-        [SDS((4, SUB, D), BF), SDS((4, SUB, D), BF)],
-    )
-    out_mine = (resid + jnp.sum(down_terms.astype(F32), axis=0)).astype(BF)
-    ffn_input_back = jnp.sum(ffn_terms.astype(F32), axis=0)
-    grad_mine = part(grad_full, me.y * SUB, SUB, 0).astype(F32)
-    scaled_back = ffn_input_back * ffn_gain_all
-    inner_two = jnp.sum(scaled_back * resid, axis=1, keepdims=True)
-    resid_back = grad_mine + scale_two * scaled_back - resid * scale_two**3 * inner_two / D
-    ffn_gain_part = jnp.sum(ffn_input_back * resid * scale_two, axis=0, keepdims=True)
-    (mix_full,) = exchange(
-        "mix_gather", 7, gather_plan, [resid_back.astype(BF)], [SDS((CHUNK, D), BF)]
-    )
-    back_cat = multiply(mix_full, w_out).astype(BF)
-    (heads_back,) = exchange("heads_back", 8, heads_back_plan, [back_cat], [SDS((ROWS, 128), BF)])
-
-    down_grad = reduce_ffn(me, contract_rows(act, grad_full).astype(BF), False)
-    gate_grad = reduce_ffn(me, contract_rows(ffn_input, gate_back).astype(BF), True)
-    up_grad = reduce_ffn(me, contract_rows(ffn_input, up_back).astype(BF), True)
+    (
+        out_mine,
+        resid_back,
+        ffn_gain_part,
+        mix_full,
+        heads_back,
+        ffn_input,
+        up_back,
+        down_own,
+        down_came,
+        gate_own,
+        gate_came,
+    ) = ffn(
+        ffn_mine, grad_full, resid, scale_two, ffn_gain_all, w_out, w_gate, w_up, w_down, whole
+    )
+
+    down_sum = (down_own.astype(F32) + total(list(down_came))).astype(BF).reshape(8, 4, 16, 1024)
+    down_grad = reduce_z(me, jnp.moveaxis(down_sum, 1, 0))
+    gate_sum = (gate_own.astype(F32) + total(list(gate_came))).astype(BF)
+    gate_sum = gate_sum.reshape(2, 8, 16, 2, 1024)
+
+    def gate_piece(k):
+        return gate_sum[XOFF[k][2], :, :, XOFF[k][4], :]
+
+    gate_grad = total([gate_piece(0)] + [x_permute(gate_piece(k), k) for k in (1, 2, 3)])
+    up_partial = contract_rows(ffn_input, up_back).astype(BF)
+    up_grad = reduce_ffn(me, up_partial)
     out_pair = reduce_core(me, contract_rows(mix_full, heads_cat).astype(BF))
     output_proj_grad = reduce_heads(me, out_pair)
 

time: 834 us -> 684 us (0.82)
  waiting for transfers between devices: 164 us -> 71.9 us
  matrix products: 85.2 us -> 22.2 us
  Pallas kernels: 381 us -> 435 us
  starting transfers between devices: 74.5 us -> 54 us
  local copies, waits for them, and re-layouts: 67.7 us -> 51.2 us
  other arithmetic: 50.3 us -> 41.8 us
    pallas_call x0 -> x2, Pallas kernels: none -> 261 us  [the longest x1 135 us: ffn(): pl.pallas_call(ffn_body, name='ffn', out_shape=[SDS((SUB, D), BF), SDS((S...]
    pallas_call x13 -> x8, Pallas kernels: 368 us -> 161 us  [exchange(): pl.pallas_call(body, name=name, out_shape=outs, in_specs=[pl.BlockSpec(me...]
    ppermute x9 -> x6, waiting for transfers between devices: 129 us -> 6.86 us  [x_permute(): lax.ppermute(value, ('narrow', 'wide'), [(i, i ^ 9) for i in range(16)])]
    ppermute x9 -> x6, waiting for transfers between devices: 6.42 us -> 55.1 us  [x_permute(): return lax.ppermute(value, 'wide', [(i, i ^ 1) for i in range(8)])]
    dot_general x6 -> x3, matrix products: 37 us -> 4.65 us  [contract_cols(): lax.dot_general(left_side, right_side, (((1,), (1,)), ((), ())), preferre...]
    dot_general x5 -> x1, matrix products: 23.6 us -> 2.26 us  [multiply(): return jnp.dot(left_side, right_side, preferred_element_type=F32)]
    dynamic_slice x7 -> x3, local copies, waits for them, and re-layouts: 20.7 us -> 2.36 us  [part(): return lax.dynamic_slice_in_dim(array, start, size, axis)]
    dynamic_slice x3 -> x6, local copies, waits for them, and re-layouts: 0.1 us -> 12.3 us  [pick(): return lax.dynamic_index_in_dim(array, index, axis, keepdims=False)]
  transfers between devices with their start and end apart: 54 -> 40, of which waited for: 20 -> 13; matrix products, arithmetic and copies ran while one was open for 12% -> 12% of each run, Pallas kernels for 25% -> 28%
where the time goes in v2:
time: 684 us; the launch traced here: 678 us
  Pallas kernels  435 us (64%)
  waiting for transfers between devices  71.9 us (11%)
  starting transfers between devices  54 us (8%)
  local copies, waits for them, and re-layouts  51.2 us (7%)
  other arithmetic  41.8 us (6%)
  matrix products  22.2 us (3%)
    pallas_call x8, Pallas kernels, exchange(): pl.pallas_call(body, name=name, out_shape=outs, in_specs=[pl.BlockSpec(me...  161 us
    pallas_call x1, Pallas kernels, ffn(): pl.pallas_call(ffn_body, name='ffn', out_shape=[SDS((SUB, D), BF), SDS((S...  135 us
    pallas_call x1, Pallas kernels, gather_weights(): pl.pallas_call(weights_body, name='weights', out_shape=SDS((3, 3, 8, 128,...  127 us
    ppermute x6, waiting for transfers between devices, x_permute(): return lax.ppermute(value, 'wide', [(i, i ^ 1) for i in range(8)])  55.1 us
    ppermute x15, starting transfers between devices, z_permute(): return lax.ppermute(value, 'tok', [(i, (i + 2 * d) % 8) for i in range(8)])  22.8 us
    dot_general x3, matrix products, contract_rows(): lax.dot_general(left_side, right_side, (((0,), (0,)), ((), ())), preferre...  15.3 us
  transfers between devices with their start and end apart: 40, of which 13 were waited for; matrix products, arithmetic and copies ran while one was open for 12% of the time, Pallas kernels for 28%

profile of v2, /device:TPU:0, one launch (start us, length us, event | category | flops | bytes accessed | tf_op | source)
XLA Modules:
  0.0 678.2 jit_solution(4235863621020900365)
XLA Ops:
  7.4 43.7 %enter.1 = (bf16[384,2048]{1,0:T(8,128)(2,1)S(1)}, bf16[2048,768]{1,0:T(8,128)(2,1)S(1)}, f32[16,8,128]{2,1,0:T(8,128)S(1)}) custom-call(bf16[1536,128]{1,0:T(8,128)(2,1)S(1)} %copy-done.2, bf16[2048,128]{1,0:T(8,128)(2,1)S(1)} %copy-done.1, bf16[2048,128]{1,0:T(8,128)(2,1)S(1)} %pad_maximum_fusion.1.refs_2_, f32[8,128]{1,0:T(8,128)S(1)} %broadcast_in_dim.6.refs_3_), custom_call_target="tpu_custom_call" | custom-call | tf_op jit(solution)/shard_map/enter/pallas_call | solution.py:136
  74.4 9.9 %to_heads.1 = (bf16[1536,128]{1,0:T(8,128)(2,1)S(1)}, bf16[1536,128]{1,0:T(8,128)(2,1)S(1)}) custom-call(bf16[384,768]{1,0:T(8,128)(2,1)S(1)} %concatenate.73.refs_0_), custom_call_target="tpu_custom_call" | custom-call | tf_op jit(solution)/shard_map/to_heads/pallas_call | solution.py:136
  86.5 126.7 %weights.1.whole = bf16[3,3,8,128,1024]{4,3,2,1,0:T(8,128)(2,1)} custom-call(bf16[3,128,1024]{2,1,0:T(8,128)(2,1)} %pad_maximum_fusion.pieces), custom_call_target="tpu_custom_call" | custom-call | tf_op jit(solution)/shard_map/weights/pallas_call | solution.py:615
  215.5 4.7 attend.1.refs_0_
  220.2 11.3 %heads_out.1 = (bf16[384,512]{1,0:T(8,128)(2,1)S(1)}, bf16[2048,512]{1,0:T(8,128)(2,1)S(1)}) custom-call(bf16[1536,128]{1,0:T(8,128)(2,1)S(1)} %attend.1.refs_0_, bf16[2048,128]{1,0:T(8,128)(2,1)S(1)} %copy-done, bf16[1024,128]{1,0:T(8,128)(2,1)S(1)} %collective-permute-done.refs_2_, bf16[1024,128]{1,0:T(8,128)(2,1)S(1)} %collective-permute-done.1.refs_3_, ...), custom_call_target="tpu_custom_call" | custom-call | tf_op jit(solution)/shard_map/heads_out/pallas_call | solution.py:136
  234.0 40.6 %out_sum.1 = (bf16[4,96,2048]{2,1,0:T(8,128)(2,1)S(1)}, bf16[384,2048]{1,0:T(8,128)(2,1)S(1)}) custom-call(bf16[384,2048]{1,0:T(8,128)(2,1)S(1)} %convolution_convert_fusion.2.refs_0_, bf16[1536,128]{1,0:T(8,128)(2,1)S(1)} %copy-done.4), custom_call_target="tpu_custom_call" | custom-call | tf_op jit(solution)/shard_map/out_sum/pallas_call | solution.py:136
  277.5 134.6 %ffn.1 = (bf16[96,2048]{1,0:T(8,128)(2,1)}, f32[96,2048]{1,0:T(8,128)}, f32[1,2048]{1,0:T(1,128)}, bf16[384,2048]{1,0:T(8,128)(2,1)}, bf16[1536,128]{1,0:T(8,128...) custom-call(bf16[96,2048]{1,0:T(8,128)(2,1)} %multiply_convert_fusio, ...), custom_call_target="tpu_custom_call" | custom-call | flops 25999998976 | bytes 41943040 | tf_op jit(solution)/shard_map/ffn/pallas_call | solution.py:879
  413.2 7.7 %attend_back.1 = (bf16[1536,128]{1,0:T(8,128)(2,1)S(1)}, bf16[1536,128]{1,0:T(8,128)(2,1)S(1)}) custom-call(s32[1,2]{1,0:T(1,128)S(1)} %copy-done.17, bf16[1536,128]{1,0:T(8,128)(2,1)S(1)} %copy-done.11, bf16[1536,128]{1,0:T(8,128)(2,1)S(1)} %copy-done.14, bf16[1536,128]{1,0:T(8,128)(2,1)S(1)} %copy-done.20, f32[1024,128]{1,0:T(8,128)S(1)} %copy-done.18, ...), custom_call_target="tpu_custom_call" | custom-call | flops 5000000000 | bytes 1048576 | tf_op jit(solution)/shard_map/attend_back/pallas_call | solution.py:437
  420.9 9.6 %grads_out.1 = bf16[384,1024]{1,0:T(8,128)(2,1)S(1)} custom-call(bf16[1536,128]{1,0:T(8,128)(2,1)S(1)} %get-tuple-element.54.refs_0_, bf16[1536,128]{1,0:T(8,128)(2,1)S(1)} %get-tuple-element.55.refs_1_), custom_call_target="tpu_custom_call" | custom-call | tf_op jit(solution)/shard_map/grads_out/pallas_call | solution.py:136
  430.5 5.8 fusion.28
  444.0 6.8 convolution_convert_fusion
  450.8 6.8 constant_dynamic-slice_fusion.1
  464.5 22.7 %normed_sum.1 = bf16[4,96,2048]{2,1,0:T(8,128)(2,1)S(1)} custom-call(bf16[384,2048]{1,0:T(8,128)(2,1)S(1)} %add_convert_fusion.refs_0_), custom_call_target="tpu_custom_call" | custom-call | tf_op jit(solution)/shard_map/normed_sum/pallas_call | solution.py:136
  488.7 16.8 %leave.1 = (bf16[1536,128]{1,0:T(8,128)(2,1)S(1)}, bf16[1536,128]{1,0:T(8,128)(2,1)S(1)}, f32[16,8,128]{2,1,0:T(8,128)S(1)}) custom-call(bf16[96,2048]{1,0:T(8,128)(2,1)S(1)} %copy-done.3, bf16[96,2048]{1,0:T(8,128)(2,1)S(1)} %fusion.16.refs_1_, f32[8,2048]{1,0:T(8,128)S(1)} %maximum_maximum_fusion.refs_2_), custom_call_target="tpu_custom_call" | custom-call | tf_op jit(solution)/shard_map/leave/pallas_call | solution.py:136
  505.6 6.5 gains.1
  512.1 4.1 fusion.8
  519.5 3.8 slice.498
  550.6 3.4 collective-permute-start.28
  560.0 4.7 collective-permute-done.28
  568.8 3.4 collective-permute-start.18
  585.6 4.8 fusion.9
  601.9 46.6 %collective-permute-done.5 = bf16[4,256,128]{2,1,0:T(8,128)(2,1)S(1)} collective-permute-done((bf16[4,256,128]{2,1,0:T(8,128)(2,1)S(1)}, bf16[4,256,128]{2,1,0:T(8,128)(2,1)S(1)}, u32[]{:S(2)}, u32[]{:S(2)}) %collective-permute-start.5) | collective-permute-done | bytes 262176 | tf_op jit(solution)/shard_map/ppermute | solution.py:475
  658.5 3.6 fusion.7
  670.4 3.8 collective-permute-done.34
  (280 shorter events, 143.8 us)
Async XLA Ops:
  51.1 169.1 %collective-permute-start = (bf16[1024,128]{1,0:T(8,128)(2,1)}, bf16[1024,128]{1,0:T(8,128)(2,1)S(1)}, u32[]{:S(2)}, u32[]{:S(2)}) collective-permute-start(bf16[1024,128]{1,0:T(8,128)(2,1)} %constant_dynamic-slice_fusion.9), channel_id=1, source_target_pairs={{0,8},{8,0},{1,9},{9,1},{2,10},{10,2},{3,11},{11,3},{4,12},{12,4},... | collective-permute-start | bytes 786440 | tf_op jit(solution)/shard_map/ppermute | solution.py:473
  52.0 168.2 %collective-permute-start.1 = (bf16[1024,128]{1,0:T(8,128)(2,1)}, bf16[1024,128]{1,0:T(8,128)(2,1)S(1)}, u32[]{:S(2)}, u32[]{:S(2)}) collective-permute-start(bf16[1024,128]{1,0:T(8,128)(2,1)} %constant_dynamic-slice_fusion.9), channel_id=1, source_target_pairs={{0,1},{1,0},{2,3},{3,2},{4,5},{5,4},{6,7},{7,6},{8,9},{9,8},{10,11... | collective-permute-start | bytes 786440 | tf_op jit(solution)/shard_map/ppermute | solution.py:475
  54.6 165.6 %collective-permute-start.2 = (bf16[1024,128]{1,0:T(8,128)(2,1)}, bf16[1024,128]{1,0:T(8,128)(2,1)S(1)}, u32[]{:S(2)}, u32[]{:S(2)}) collective-permute-start(bf16[1024,128]{1,0:T(8,128)(2,1)} %constant_dynamic-slice_fusion.9), channel_id=1, source_target_pairs={{0,9},{1,8},{2,11},{3,10},{4,13},{5,12},{6,15},{7,14},{8,1},{9,0},... | collective-permute-start | bytes 786440 | tf_op jit(solution)/shard_map/ppermute | solution.py:476
  441.3 114.1 %collective-permute-start.37 = (bf16[8,16,1024]{2,1,0:T(8,128)(2,1)}, bf16[8,16,1024]{2,1,0:T(8,128)(2,1)}, u32[]{:S(2)}, u32[]{:S(2)}) collective-permute-start(bf16[8,16,1024]{2,1,0:T(8,128)(2,1)} %get-tuple-element.122), channel_id=1, source_target_pairs={{0,32},{16,48},{32,64},{48,80},{64,96},{80,112},{96,0},{112,16},{1... | collective-permute-start | bytes 786440 | tf_op jit(solution)/shard_map/ppermute | solution.py:480
  459.9 125.7 %collective-permute-start.30 = (bf16[2,8,4,16,2048]{4,3,1,2,0:T(8,128)(2,1)}, bf16[2,8,4,16,2048]{4,3,1,2,0:T(8,128)(2,1)}, u32[]{:S(2)}, u32[]{:S(2)}) collective-permute-start(bf16[2,8,4,16,2048]{4,3,1,2,0:T(8,128)(2,1)} %bitcast.155), channel_id=1, source_target_pairs={{0,16},{16,0},{32,48},{48,32},{64,80},{80,64},{96,112},{112,96},{1... | collective-permute-start | bytes 12582920 | tf_op jit(solution)/shard_map/ppermute | solution.py:488
  463.4 63.6 %collective-permute-start.10 = (bf16[4,256,256]{2,1,0:T(8,128)(2,1)}, bf16[4,256,256]{2,1,0:T(8,128)(2,1)}, u32[]{:S(2)}, u32[]{:S(2)}) collective-permute-start(bf16[4,256,256]{2,1,0:T(8,128)(2,1)} %get-tuple-element.133), channel_id=1, source_target_pairs={{0,16},{16,0},{32,48},{48,32},{64,80},{80,64},{96,112},{112,96},{1... | collective-permute-start | bytes 1572872 | tf_op jit(solution)/shard_map/ppermute | solution.py:488
  550.6 14.0 %collective-permute-start.28 = (bf16[8,16,1024]{2,1,0:T(8,128)(2,1)S(1)}, bf16[8,16,1024]{2,1,0:T(8,128)(2,1)S(1)}, u32[]{:S(2)}, u32[]{:S(2)}) collective-permute-start(bf16[8,16,1024]{2,1,0:T(8,128)(2,1)S(1)} %bitcast.172), channel_id=1, source_target_pairs={{0,1},{1,0},{2,3},{3,2},{4,5},{5,4},{6,7},{7,6},{8,9},{9,8},{10,11... | collective-permute-start | bytes 786440 | tf_op jit(solution)/shard_map/ppermute | solution.py:475
  554.0 13.2 %collective-permute-start.29 = (bf16[8,16,1024]{2,1,0:T(8,128)(2,1)S(1)}, bf16[8,16,1024]{2,1,0:T(8,128)(2,1)S(1)}, u32[]{:S(2)}, u32[]{:S(2)}) collective-permute-start(bf16[8,16,1024]{2,1,0:T(8,128)(2,1)S(1)} %bitcast.171), channel_id=1, source_target_pairs={{0,9},{1,8},{2,11},{3,10},{4,13},{5,12},{6,15},{7,14},{8,1},{9,0},... | collective-permute-start | bytes 786440 | tf_op jit(solution)/shard_map/ppermute | solution.py:476
  555.4 13.4 %collective-permute-start.38 = (bf16[8,16,1024]{2,1,0:T(8,128)(2,1)S(1)}, bf16[8,16,1024]{2,1,0:T(8,128)(2,1)S(1)}, u32[]{:S(2)}, u32[]{:S(2)}) collective-permute-start(bf16[8,16,1024]{2,1,0:T(8,128)(2,1)S(1)} %copy-done.45), channel_id=1, source_target_pairs={{0,64},{16,80},{32,96},{48,112},{64,0},{80,16},{96,32},{112,48},{1... | collective-permute-start | bytes 786440 | tf_op jit(solution)/shard_map/ppermute | solution.py:480
  564.6 11.7 %collective-permute-start.20 = (bf16[4,256,512]{2,1,0:T(8,128)(2,1)}, bf16[4,256,512]{2,1,0:T(8,128)(2,1)}, u32[]{:S(2)}, u32[]{:S(2)}) collective-permute-start(bf16[4,256,512]{2,1,0:T(8,128)(2,1)} %get-tuple-element.88), channel_id=1, source_target_pairs={{0,16},{16,0},{32,48},{48,32},{64,80},{80,64},{96,112},{112,96},{1... | collective-permute-start | bytes 3145736 | tf_op jit(solution)/shard_map/ppermute | solution.py:488
  568.8 14.5 %collective-permute-start.3 = (bf16[4,256,512]{2,1,0:T(8,128)(2,1)}, bf16[4,256,512]{2,1,0:T(8,128)(2,1)}, u32[]{:S(2)}, u32[]{:S(2)}) collective-permute-start(bf16[4,256,512]{2,1,0:T(8,128)(2,1)} %get-tuple-element.93), channel_id=1, source_target_pairs={{0,16},{16,0},{32,48},{48,32},{64,80},{80,64},{96,112},{112,96},{1... | collective-permute-start | bytes 3145736 | tf_op jit(solution)/shard_map/ppermute | solution.py:488
  578.5 13.8 %collective-permute-start.21 = (bf16[4,256,128]{2,1,0:T(8,128)(2,1)S(1)}, bf16[4,256,128]{2,1,0:T(8,128)(2,1)S(1)}, u32[]{:S(2)}, u32[]{:S(2)}) collective-permute-start(bf16[4,256,128]{2,1,0:T(8,128)(2,1)S(1)} %get-tuple-element.84), channel_id=1, source_target_pairs={{0,8},{8,0},{1,9},{9,1},{2,10},{10,2},{3,11},{11,3},{4,12},{12,4},... | collective-permute-start | bytes 786440 | tf_op jit(solution)/shard_map/ppermute | solution.py:473
  578.5 15.7 %collective-permute-start.22 = (bf16[4,256,128]{2,1,0:T(8,128)(2,1)S(1)}, bf16[4,256,128]{2,1,0:T(8,128)(2,1)S(1)}, u32[]{:S(2)}, u32[]{:S(2)}) collective-permute-start(bf16[4,256,128]{2,1,0:T(8,128)(2,1)S(1)} %get-tuple-element.86), channel_id=1, source_target_pairs={{0,1},{1,0},{2,3},{3,2},{4,5},{5,4},{6,7},{7,6},{8,9},{9,8},{10,11... | collective-permute-start | bytes 786440 | tf_op jit(solution)/shard_map/ppermute | solution.py:475
  581.3 16.5 %collective-permute-start.23 = (bf16[4,256,128]{2,1,0:T(8,128)(2,1)}, bf16[4,256,128]{2,1,0:T(8,128)(2,1)}, u32[]{:S(2)}, u32[]{:S(2)}) collective-permute-start(bf16[4,256,128]{2,1,0:T(8,128)(2,1)} %get-tuple-element.85), channel_id=1, source_target_pairs={{0,9},{1,8},{2,11},{3,10},{4,13},{5,12},{6,15},{7,14},{8,1},{9,0},... | collective-permute-start | bytes 786440 | tf_op jit(solution)/shard_map/ppermute | solution.py:476
  585.5 13.6 %collective-permute-start.4 = (bf16[4,256,128]{2,1,0:T(8,128)(2,1)}, bf16[4,256,128]{2,1,0:T(8,128)(2,1)}, u32[]{:S(2)}, u32[]{:S(2)}) collective-permute-start(bf16[4,256,128]{2,1,0:T(8,128)(2,1)} %get-tuple-element.89), channel_id=1, source_target_pairs={{0,8},{8,0},{1,9},{9,1},{2,10},{10,2},{3,11},{11,3},{4,12},{12,4},... | collective-permute-start | bytes 786440 | tf_op jit(solution)/shard_map/ppermute | solution.py:473
  590.3 63.6 %collective-permute-start.31 = (bf16[8,4,16,1024]{3,2,0,1:T(8,128)(2,1)}, bf16[8,4,16,1024]{3,2,0,1:T(8,128)(2,1)}, u32[]{:S(2)}, u32[]{:S(2)}) collective-permute-start(bf16[8,4,16,1024]{3,2,0,1:T(8,128)(2,1)} %get-tuple-element.73), channel_id=1, source_target_pairs={{0,8},{8,0},{1,9},{9,1},{2,10},{10,2},{3,11},{11,3},{4,12},{12,4},... | collective-permute-start | bytes 3145736 | tf_op jit(solution)/shard_map/ppermute | solution.py:473
  592.3 63.7 %collective-permute-start.32 = (bf16[8,4,16,1024]{3,2,0,1:T(8,128)(2,1)}, bf16[8,4,16,1024]{3,2,0,1:T(8,128)(2,1)}, u32[]{:S(2)}, u32[]{:S(2)}) collective-permute-start(bf16[8,4,16,1024]{3,2,0,1:T(8,128)(2,1)} %get-tuple-element.75), channel_id=1, source_target_pairs={{0,1},{1,0},{2,3},{3,2},{4,5},{5,4},{6,7},{7,6},{8,9},{9,8},{10,11... | collective-permute-start | bytes 3145736 | tf_op jit(solution)/shard_map/ppermute | solution.py:475
  594.2 61.8 %collective-permute-start.33 = (bf16[8,4,16,1024]{3,2,0,1:T(8,128)(2,1)S(1)}, bf16[8,4,16,1024]{3,2,0,1:T(8,128)(2,1)}, u32[]{:S(2)}, u32[]{:S(2)}) collective-permute-start(bf16[8,4,16,1024]{3,2,0,1:T(8,128)(2,1)S(1)} %get-tuple-element.74), channel_id=1, source_target_pairs={{0,9},{1,8},{2,11},{3,10},{4,13},{5,12},{6,15},{7,14},{8,1},{9,0},... | collective-permute-start | bytes 3145736 | tf_op jit(solution)/shard_map/ppermute | solution.py:476
  597.8 50.7 %collective-permute-start.5 = (bf16[4,256,128]{2,1,0:T(8,128)(2,1)S(1)}, bf16[4,256,128]{2,1,0:T(8,128)(2,1)S(1)}, u32[]{:S(2)}, u32[]{:S(2)}) collective-permute-start(bf16[4,256,128]{2,1,0:T(8,128)(2,1)S(1)} %get-tuple-element.91), channel_id=1, source_target_pairs={{0,1},{1,0},{2,3},{3,2},{4,5},{5,4},{6,7},{7,6},{8,9},{9,8},{10,11... | collective-permute-start | bytes 786440 | tf_op jit(solution)/shard_map/ppermute | solution.py:475
  599.2 52.0 %collective-permute-start.6 = (bf16[4,256,128]{2,1,0:T(8,128)(2,1)S(1)}, bf16[4,256,128]{2,1,0:T(8,128)(2,1)S(1)}, u32[]{:S(2)}, u32[]{:S(2)}) collective-permute-start(bf16[4,256,128]{2,1,0:T(8,128)(2,1)S(1)} %get-tuple-element.90), channel_id=1, source_target_pairs={{0,9},{1,8},{2,11},{3,10},{4,13},{5,12},{6,15},{7,14},{8,1},{9,0},... | collective-permute-start | bytes 786440 | tf_op jit(solution)/shard_map/ppermute | solution.py:476
  648.5 13.7 %collective-permute-start.24 = (bf16[256,128]{1,0:T(8,128)(2,1)S(1)}, bf16[256,128]{1,0:T(8,128)(2,1)S(1)}, u32[]{:S(2)}, u32[]{:S(2)}) collective-permute-start(bf16[256,128]{1,0:T(8,128)(2,1)S(1)} %get-tuple-element.142), channel_id=1, source_target_pairs={{0,32},{16,48},{32,64},{48,80},{64,96},{80,112},{96,0},{112,16},{1... | collective-permute-start | bytes 196616 | tf_op jit(solution)/shard_map/ppermute | solution.py:480
  651.2 12.2 %collective-permute-start.25 = (bf16[256,128]{1,0:T(8,128)(2,1)S(1)}, bf16[256,128]{1,0:T(8,128)(2,1)S(1)}, u32[]{:S(2)}, u32[]{:S(2)}) collective-permute-start(bf16[256,128]{1,0:T(8,128)(2,1)S(1)} %get-tuple-element.144), channel_id=1, source_target_pairs={{0,64},{16,80},{32,96},{48,112},{64,0},{80,16},{96,32},{112,48},{1... | collective-permute-start | bytes 196616 | tf_op jit(solution)/shard_map/ppermute | solution.py:480
  656.0 13.6 %collective-permute-start.8 = (bf16[256,128]{1,0:T(8,128)(2,1)S(1)}, bf16[256,128]{1,0:T(8,128)(2,1)S(1)}, u32[]{:S(2)}, u32[]{:S(2)}) collective-permute-start(bf16[256,128]{1,0:T(8,128)(2,1)S(1)} %get-tuple-element.147), channel_id=1, source_target_pairs={{0,64},{16,80},{32,96},{48,112},{64,0},{80,16},{96,32},{112,48},{1... | collective-permute-start | bytes 196616 | tf_op jit(solution)/shard_map/ppermute | solution.py:480
  663.4 10.7 %collective-permute-start.34 = (bf16[8,16,1024]{2,1,0:T(8,128)(2,1)S(1)}, bf16[8,16,1024]{2,1,0:T(8,128)(2,1)S(1)}, u32[]{:S(2)}, u32[]{:S(2)}) collective-permute-start(bf16[8,16,1024]{2,1,0:T(8,128)(2,1)S(1)} %get-tuple-element.125), channel_id=1, source_target_pairs={{0,32},{16,48},{32,64},{48,80},{64,96},{80,112},{96,0},{112,16},{1... | collective-permute-start | bytes 786440 | tf_op jit(solution)/shard_map/ppermute | solution.py:480
  (73 other events, 899.4 us)

commit v3 on v2

--- a/solution.py
+++ b/solution.py
@@ -447,6 +447,378 @@
     )(*ins)
 
 
+def back_body(
+    dq_ref,
+    dkv_ref,
+    w_attn,
+    heads_cat,
+    out_mine,
+    in_mine,
+    resid_back,
+    scale_ref,
+    gain_ref,
+    ffn_gain_part,
+    normed_in,
+    mix_in,
+    ffn_in,
+    up_in,
+    down_own,
+    down_came,
+    gate_own,
+    gate_came,
+    layer_output,
+    input_grad,
+    query_grad,
+    kv_grad,
+    out_grad,
+    gate_grad,
+    up_grad,
+    down_grad,
+    gain_grad,
+    left_buf,
+    right_buf,
+    down_in,
+    gate_in,
+    down_sum,
+    gate_sum,
+    down_z,
+    gate_x,
+    up_terms,
+    up_core,
+    up_z,
+    up_sum,
+    up_x,
+    cat_back,
+    norm_send,
+    norm_recv,
+    in_grad,
+    gain_parts,
+    gain_plane,
+    gain_mine,
+    gain_toks,
+    o_terms,
+    o_core,
+    o_x,
+    o_sum,
+    o_z,
+    q_terms,
+    q_core,
+    q_x,
+    q_sum,
+    q_z,
+    k_terms,
+    k_core,
+    k_x,
+    k_sum,
+    k_z,
+    k_last,
+    send_sem,
+    recv_sem,
+    core_send,
+    core_recv,
+    local_sem,
+):
+    me = whereami()
+    wire = Wire(me, send_sem, recv_sem)
+    load_left = pltpu.make_async_copy(ffn_in, left_buf, local_sem.at[0])
+    load_right = pltpu.make_async_copy(up_in, right_buf, local_sem.at[1])
+    load_left.start()
+    load_right.start()
+
+    def halves(own, came, buf, h, sem):
+        part_of = pl.ds(h * (own.shape[0] // 2), own.shape[0] // 2)
+        return [
+            pltpu.make_async_copy(own.at[part_of], buf.at[0], local_sem.at[sem]),
+            pltpu.make_async_copy(came.at[:, part_of], buf.at[1:4], local_sem.at[sem + 1]),
+        ]
+
+    def start(copies):
+        for copy in copies:
+            copy.start()
+
+    start(halves(gate_own, gate_came, gate_in, 0, 2))
+    start(halves(down_own, down_came, down_in, 0, 4))
+    meet(me, PLANE[1:] + TOKS[1:])
+    sent = []
+
+    spot = rows(me.chunk * CHUNK, CHUNK)
+    moves = []
+    for k in (1, 2, 3):
+        there = rows(me.at(XOFF[k]).chunk * CHUNK, CHUNK)
+        for ref, col in ((dq_ref, 0), (dkv_ref, 512)):
+            moves.append(
+                wire.send(
+                    XOFF[k], ref.at[there, :], cat_back.at[:, col + k * 128 : col + k * 128 + 128]
+                )
+            )
+    cat_back[:, 0:128] = dq_ref[spot, :]
+    cat_back[:, 512:640] = dkv_ref[spot, :]
+
+    mine = rows(me.chunk * CHUNK + me.y * SUB, SUB)
+    leaving = [
+        wire.send(off, out_mine.at[:, lanes(me.at(off).block)], layer_output.at[mine, :])
+        for off in PLANE[1:]
+    ]
+    layer_output[mine, :] = out_mine[:, lanes(me.block)]
+
+    load_left.wait()
+    load_right.wait()
+    up_pair = PairSum(me, left_buf, right_buf, up_terms, up_core, core_send, core_recv)
+    up_pair.multiply(0, 8)
+    load_left = pltpu.make_async_copy(normed_in, left_buf, local_sem.at[0])
+    load_right = pltpu.make_async_copy(mix_in, right_buf, local_sem.at[1])
+    load_left.start()
+    load_right.start()
+    up_pair.add(0, 8)
+    up_moves = [
+        wire.send(ZOFF[d], up_terms.at[:, :, (me.z + d) % 4, me.core], up_z.at[d - 1])
+        for d in (1, 2, 3)
+    ]
+
+    finish(moves)
+    for h in range(4):
+        cols = slice(h * 512, h * 512 + 512)
+        term = contract_cols(cat_back[:, 0:768], w_attn[cols, :]) + contract_cols(
+            cat_back[:, 768:1024], w_attn[cols, 512:768]
+        )
+        norm_send[:, cols] = term.astype(BF)
+    norm_moves = [
+        wire.send(YOFF[d], norm_send.at[rows(me.at(YOFF[d]).y * SUB, SUB), :], norm_recv.at[d - 1])
+        for d in (1, 2, 3)
+    ]
+
+    load_left.wait()
+    load_right.wait()
+    for z in range(4):
+        block = contract_rows(left_buf[:, z * 512 : z * 512 + 512], cat_back[:, 0:512])
+        q_terms[z] = block.astype(BF).reshape(2, 256, 512)
+    q_pair = wire.send(SIBLING, q_terms.at[:, 1 - me.core], q_core)
+    for z in range(4):
+        left = left_buf[:, z * 512 : z * 512 + 512]
+        block = contract_rows(left, cat_back[:, 512:768]) + contract_rows(
+            left, cat_back[:, 768:1024]
+        )
+        k_terms[z] = block.astype(BF).reshape(2, 4, 2, 32, 256)
+    k_pair = wire.send(SIBLING, k_terms.at[:, 1 - me.core], k_core)
+    for z in range(4):
+        block = contract_rows(right_buf[:, z * 512 : z * 512 + 512], heads_cat[...])
+        o_terms[z] = block.astype(BF).reshape(2, 256, 512)
+    o_pair = wire.send(SIBLING, o_terms.at[:, 1 - me.core], o_core)
+
+    def fold(own, came, buf, out, sem):
+        size = buf.shape[1]
+        for h in range(2):
+            copies = halves(own, came, buf, h, sem)
+            for copy in copies:
+                copy.wait()
+
+            def step(i, _, h=h):
+                value = buf[0, i].astype(F32)
+                for k in (1, 2, 3):
+                    value = value + buf[k, i].astype(F32)
+                out[h * size + i] = value.astype(BF)
+                return 0
+
+            lax.fori_loop(0, size, step, 0)
+            if h == 0:
+                start(halves(own, came, buf, 1, sem))
+
+    def gate_block(k):
+        e, dxl = XOFF[k][4], XOFF[k][2]
+        return gate_sum.at[dxl * 4 : dxl * 4 + 4, :, :, e * 1024 : e * 1024 + 1024]
+
+    fold(gate_own, gate_came, gate_in, gate_sum, 2)
+    gate_moves = [wire.send(XOFF[k], gate_block(k), gate_x.at[k - 1]) for k in (1, 2, 3)]
+    fold(down_own, down_came, down_in, down_sum, 4)
+    down_moves = [
+        wire.send(ZOFF[d], down_sum.at[:, :, (me.z + d) % 4], down_z.at[d - 1]) for d in (1, 2, 3)
+    ]
+
+    def add_core(copy, terms, came):
+        copy.wait_recv()
+        terms[:, me.core] = (terms[:, me.core].astype(F32) + came[...].astype(F32)).astype(BF)
+
+    def kv_block(k):
+        e, dxl = XOFF[k][4], XOFF[k][2]
+        return k_terms.at[:, me.core, :, (me.xh + e) % 2, :, dxl * 128 : dxl * 128 + 128]
+
+    add_core(k_pair, k_terms, k_core)
+    k_moves = [wire.send(XOFF[k], kv_block(k), k_x.at[k - 1]) for k in (1, 2, 3)]
+    add_core(q_pair, q_terms, q_core)
+    q_moves = [
+        wire.send(XOFF[k], q_terms.at[:, me.core, :, k * 128 : k * 128 + 128], q_x.at[k - 1])
+        for k in (1, 2, 3)
+    ]
+    add_core(o_pair, o_terms, o_core)
+    o_moves = [
+        wire.send(XOFF[k], o_terms.at[:, me.core, :, k * 128 : k * 128 + 128], o_x.at[k - 1])
+        for k in (1, 2, 3)
+    ]
+
+    finish(norm_moves)
+    here = rows(me.y * SUB, SUB)
+    back = norm_send[here, :].astype(F32)
+    for d in range(3):
+        back = back + norm_recv[d].astype(F32)
+    scale = scale_ref[...]
+    enter = in_mine[...].astype(F32)
+    weighed = back * enter
+    inner = jnp.sum(weighed * gain_ref[...], axis=1, keepdims=True)
+    gain_parts[0:1, :] = jnp.sum(weighed * scale, axis=0, keepdims=True)
+    gain_parts[1:2, :] = ffn_gain_part[...]
+    gain_parts[2:8, :] = jnp.zeros((6, D), F32)
+    pull = scale * scale * scale * inner / D
+    in_grad[...] = (resid_back[...] + scale * gain_ref[...] * back - enter * pull).astype(BF)
+    for off in PLANE[1:]:
+        there = lanes(me.at(off).block)
+        leaving.append(wire.send(off, in_grad.at[:, there], input_grad.at[mine, :]))
+        leaving.append(wire.send(off, gain_parts.at[:, there], gain_plane.at[me.block]))
+    input_grad[mine, :] = in_grad[:, lanes(me.block)]
+    gain_plane[me.block] = gain_parts[:, lanes(me.block)]
+
+    def over_x(moves, own, came, out):
+        for copy in moves:
+            copy.wait_recv()
+        value = own.astype(F32)
+        for k in range(3):
+            value = value + came[k].astype(F32)
+        out[...] = value.astype(BF)
+        sent.extend(moves)
+
+    over_x(o_moves, o_terms[:, me.core, :, 0:128], o_x, o_sum)
+    over_x(q_moves, q_terms[:, me.core, :, 0:128], q_x, q_sum)
+    over_x(k_moves, k_terms[:, me.core, :, me.xh, :, 0:128], k_x, k_sum)
+    late = []
+    for summed, came in ((o_sum, o_z), (q_sum, q_z), (k_sum, k_z)):
+        late.append(
+            [wire.send(ZOFF[d], summed.at[(me.z + d) % 4], came.at[d - 1]) for d in (1, 2, 3)]
+        )
+
+    def over_z(moves, own, came):
+        for copy in moves:
+            copy.wait_recv()
+        sent.extend(moves)
+        value = own.astype(F32)
+        for d in range(3):
+            value = value + came[d].astype(F32)
+        return value
+
+    down_grad[...] = over_z(down_moves, down_sum[:, :, me.z].reshape(8, 16, 1024), down_z.reshape(3, 8, 16, 1024))
+    gate_grad[...] = over_z(gate_moves, gate_sum[0:4, :, :, 0:1024].reshape(8, 16, 1024), gate_x.reshape(3, 8, 16, 1024))
+    for copy in up_moves:
+        copy.wait_recv()
+    sent.extend(up_moves)
+
+    def up_step(i, _):
+        value = up_terms[i, :, me.z, me.core].astype(F32)
+        for d in range(3):
+            value = value + up_z[d, i].astype(F32)
+        up_sum[i] = value.astype(BF)
+        return 0
+
+    lax.fori_loop(0, 8, up_step, 0)
+
+    def up_block(k):
+        e, dxl = XOFF[k][4], XOFF[k][2]
+        return up_sum.at[dxl * 4 : dxl * 4 + 4, :, :, e * 1024 : e * 1024 + 1024]
+
+    up_moves = [wire.send(XOFF[k], up_block(k), up_x.at[k - 1]) for k in (1, 2, 3)]
+
+    out_grad[...] = over_z(late[0], o_sum[me.z], o_z)
+    query_grad[...] = over_z(late[1], q_sum[me.z], q_z)
+    k_last[...] = over_z(late[2], k_sum[me.z], k_z)
+    y_moves = [wire.send(YOFF[d], k_last.at[me.at(YOFF[d]).y], kv_grad.at[me.y]) for d in (1, 2, 3)]
+    kv_grad[me.y] = k_last[me.y]
+    for copy in leaving:
+        copy.wait_recv()
+    sent.extend(leaving)
+    gain_mine[...] = jnp.sum(gain_plane[...], axis=0)
+    tok_moves = [wire.send(off, gain_mine, gain_toks.at[me.tok]) for off in TOKS[1:]]
+    gain_toks[me.tok] = gain_mine[...]
+    up_grad[...] = over_z(up_moves, up_sum[0:4, :, :, 0:1024].reshape(8, 16, 1024), up_x.reshape(3, 8, 16, 1024))
+    finish(y_moves + tok_moves)
+    gain_grad[...] = jnp.sum(gain_toks[...], axis=0)
+    for copy in sent:
+        copy.wait_send()
+    up_pair.sent()
+    o_pair.wait_send()
+    q_pair.wait_send()
+    k_pair.wait_send()
+
+
+def back(vmem_ins, hbm_ins):
+    vm = pl.BlockSpec(memory_space=pltpu.VMEM)
+    hbm = pl.BlockSpec(memory_space=pl.ANY)
+    outs = [
+        SDS((ROWS, 128), BF),
+        SDS((ROWS, 128), BF),
+        SDS((256, 128), F32),
+        SDS((4, 32, 128), F32),
+        SDS((256, 128), F32),
+        SDS((8, 16, 1024), F32),
+        SDS((8, 16, 1024), F32),
+        SDS((8, 16, 1024), F32),
+        SDS((8, 128), F32),
+    ]
+    v = pltpu.VMEM
+    heads_sum = [
+        v((4, 2, 256, 512), BF),
+        v((4, 256, 512), BF),
+        v((3, 4, 256, 128), BF),
+        v((4, 256, 128), BF),
+        v((3, 256, 128), BF),
+    ]
+    return pl.pallas_call(
+        back_body,
+        name="back",
+        out_shape=outs,
+        in_specs=[vm] * len(vmem_ins) + [hbm] * len(hbm_ins),
+        out_specs=[vm] * len(outs),
+        scratch_shapes=[
+            v((CHUNK, D), BF),
+            v((CHUNK, D), BF),
+            v((4, 2, 2, 4, 16, 1024), BF),
+            v((4, 4, 2, 16, 2048), BF),
+            v((4, 2, 4, 16, 1024), BF),
+            v((8, 2, 16, 2048), BF),
+            v((3, 4, 2, 16, 1024), BF),
+            v((3, 4, 2, 16, 1024), BF),
+            v((8, 2, 4, 2, 16, 2048), BF),
+            v((8, 2, 4, 16, 2048), BF),
+            v((3, 8, 2, 16, 2048), BF),
+            v((8, 2, 16, 2048), BF),
+            v((3, 4, 2, 16, 1024), BF),
+            v((CHUNK, 1024), BF),
+            v((CHUNK, D), BF),
+            v((3, SUB, D), BF),
+            v((SUB, D), BF),
+            v((8, D), F32),
+            v((16, 8, 128), F32),
+            v((8, 128), F32),
+            v((8, 8, 128), F32),
+        ]
+        + heads_sum
+        + heads_sum
+        + [
+            v((4, 2, 4, 2, 32, 256), BF),
+            v((4, 4, 2, 32, 256), BF),
+            v((3, 4, 4, 32, 128), BF),
+            v((4, 4, 32, 128), BF),
+            v((3, 4, 32, 128), BF),
+            v((4, 32, 128), F32),
+            pltpu.SemaphoreType.DMA((104,)),
+            pltpu.SemaphoreType.DMA((104,)),
+            pltpu.SemaphoreType.DMA((8,)),
+            pltpu.SemaphoreType.DMA((8,)),
+            pltpu.SemaphoreType.DMA((6,)),
+        ],
+        compiler_params=pltpu.CompilerParams(
+            collective_id=15, has_side_effects=True, vmem_limit_bytes=56 * 2**20
+        ),
+        cost_estimate=pl.CostEstimate(flops=10**10, bytes_accessed=30 * 2**20, transcendentals=0),
+    )(*vmem_ins, *hbm_ins)
+
+
 def rope_table():
     halfway = HEAD_DIM // 2
     k = np.arange(halfway, dtype=np.float32)
@@ -501,40 +873,6 @@
     for term in terms[1:]:
         out = out + term.astype(F32)
     return out
-
-
-def reduce_ffn(me, partial):
-    view = partial.reshape(2, 8, 4, 2, 16, 2048)
-    mine = pick(view, me.core, 3)
-    came = core_permute(pick(view, 1 - me.core, 3))
-
-    def quarter(k):
-        r, c = XOFF[k][2], XOFF[k][4]
-        return total([a[r, ..., c * 1024 : c * 1024 + 1024] for a in (mine, came)])
-
-    own = quarter(0)
-    got = [x_permute(quarter(k).astype(BF), k) for k in (1, 2, 3)]
-    summed = total([own] + got).astype(BF)
-    own = pick(summed, me.z, 1)
-    got = [z_permute(pick(summed, (me.z + d) % 4, 1), d) for d in (1, 2, 3)]
-    return total([own] + got)
-
-
-def reduce_core(me, partial):
-    view = partial.reshape(4, 2, 256, partial.shape[1])
-    return pick(view, me.core, 1), core_permute(pick(view, 1 - me.core, 1))
-
-
-def reduce_z(me, summed):
-    own = pick(summed, me.z, 0)
-    got = [z_permute(pick(summed, (me.z + d) % 4, 0), d) for d in (1, 2, 3)]
-    return total([own] + got)
-
-
-def reduce_heads(me, pair):
-    pieces = [total([a[:, :, k * 128 : k * 128 + 128] for a in pair]) for k in range(4)]
-    got = [x_permute(pieces[k].astype(BF), k) for k in (1, 2, 3)]
-    return reduce_z(me, total([pieces[0]] + got).astype(BF))
 
 
 def contract_rows(left_side, right_side):
@@ -959,7 +1297,6 @@
     table_start = jnp.where(long_first, SHORT, 0) + me.chunk * CHUNK
     cos_here = part(cos_all, table_start, CHUNK, 0)
     sin_here = part(sin_all, table_start, CHUNK, 0)
-    cos_doc, sin_doc = cos_all[512:1536], sin_all[512:1536]
 
     w_kv = jnp.concatenate(
         [part(w_key, me.y * 64, 64, 1), part(w_value, me.y * 64, 64, 1)], axis=1
@@ -1038,77 +1375,43 @@
         ffn_mine, grad_full, resid, scale_two, ffn_gain_all, w_out, w_gate, w_up, w_down, whole
     )
 
-    down_sum = (down_own.astype(F32) + total(list(down_came))).astype(BF).reshape(8, 4, 16, 1024)
-    down_grad = reduce_z(me, jnp.moveaxis(down_sum, 1, 0))
-    gate_sum = (gate_own.astype(F32) + total(list(gate_came))).astype(BF)
-    gate_sum = gate_sum.reshape(2, 8, 16, 2, 1024)
-
-    def gate_piece(k):
-        return gate_sum[XOFF[k][2], :, :, XOFF[k][4], :]
-
-    gate_grad = total([gate_piece(0)] + [x_permute(gate_piece(k), k) for k in (1, 2, 3)])
-    up_partial = contract_rows(ffn_input, up_back).astype(BF)
-    up_grad = reduce_ffn(me, up_partial)
-    out_pair = reduce_core(me, contract_rows(mix_full, heads_cat).astype(BF))
-    output_proj_grad = reduce_heads(me, out_pair)
-
     query_back, kv_back = vmem_call(
         "attend_back",
         attend_back_body,
-        [doc_lengths, queries, kv, heads_back, cos_doc, sin_doc],
+        [doc_lengths, queries, kv, heads_back, cos_all[512:1536], sin_all[512:1536]],
         [SDS((ROWS, 128), BF), SDS((ROWS, 128), BF)],
         scratch=[pltpu.VMEM((1024, 128), F32)],
         flops=5 * 10**9,
     )
-    (cat_back,) = exchange(
-        "grads_out", 9, grads_out_plan, [query_back, kv_back], [SDS((CHUNK, 1024), BF)]
-    )
-    normed_term = (
-        contract_cols(cat_back[:, :768], w_attn) + contract_cols(cat_back[:, 768:], w_attn[:, 512:])
-    ).astype(BF)
-    (normed_terms,) = exchange(
-        "normed_sum", 10, sum_plan, [normed_term], [SDS((4, SUB, D), BF)]
-    )
-    attn_partial = contract_rows(normed, cat_back)
-    kv_partial = attn_partial[:, 512:768] + attn_partial[:, 768:]
-    query_grad = reduce_heads(me, reduce_core(me, attn_partial[:, :512].astype(BF)))
-
-    kv_pair = reduce_core(me, kv_partial.astype(BF))
-    kv_pair = [a.reshape(4, 4, 2, 32, 256) for a in kv_pair]
-
-    def kv_piece(k):
-        return total([pick(a, me.at(XOFF[k]).xh, 2)[..., 128 * XOFF[k][2] : 128 * XOFF[k][2] + 128] for a in kv_pair])
-
-    got = [x_permute(kv_piece(k).astype(BF), k) for k in (1, 2, 3)]
-    kv_sum = reduce_z(me, total([kv_piece(0)] + got).astype(BF))
-    kv_cols = jnp.stack(
-        [pick(kv_sum, me.y, 0)] + [y_permute(pick(kv_sum, (me.y + d) % 4, 0), d) for d in (1, 2, 3)]
-    )
-    kv_cols = jnp.concatenate([pick(kv_cols, (me.y - h) % 4, 0) for h in range(4)], axis=1)
-    kv_cols = kv_cols.reshape(32, 4, 2, 64)
+    (
+        layer_output,
+        input_grad,
+        query_grad,
+        kv_grad,
+        output_proj_grad,
+        gate_grad,
+        up_grad,
+        down_grad,
+        gain_grads,
+    ) = back(
+        [
+            query_back,
+            kv_back,
+            w_attn,
+            heads_cat,
+            out_mine,
+            part(full_in, me.y * SUB, SUB, 0),
+            resid_back,
+            part(scale_one, me.y * SUB, SUB, 0),
+            attn_gain[None, :],
+            ffn_gain_part,
+        ],
+        [normed, mix_full, ffn_input, up_back, down_own, down_came, gate_own, gate_came],
+    )
+    kv_cols = jnp.moveaxis(kv_grad, 0, 1).reshape(32, 4, 2, 64)
     key_grad = kv_cols[:, :, 0, :].reshape(32, 256)
     value_grad = kv_cols[:, :, 1, :].reshape(32, 256)
-
-    normed_back = jnp.sum(normed_terms.astype(F32), axis=0)
-    scale_mine = part(scale_one, me.y * SUB, SUB, 0)
-    scaled_back = normed_back * attn_gain[None, :]
-    inner_one = jnp.sum(scaled_back * in_mine, axis=1, keepdims=True)
-    in_grad_mine = (
-        resid_back + scale_mine * scaled_back - in_mine * scale_mine**3 * inner_one / D
-    ).astype(BF)
-    attn_gain_part = jnp.sum(normed_back * in_mine * scale_mine, axis=0, keepdims=True)
-    gain_parts = jnp.concatenate([attn_gain_part, ffn_gain_part, jnp.zeros((6, D), F32)], axis=0)
-    layer_output, input_grad, gain_terms = exchange(
-        "leave",
-        11,
-        leave_plan,
-        [out_mine, in_grad_mine, gain_parts],
-        [SDS((ROWS, 128), BF), SDS((ROWS, 128), BF), SDS((16, 8, 128), F32)],
-    )
-    (gain_toks,) = exchange(
-        "gains", 12, gains_plan, [jnp.sum(gain_terms, axis=0)], [SDS((8, 8, 128), F32)]
-    )
-    gain_grads = part(jnp.sum(gain_toks, axis=0), me.tok * 16, 16, 1)
+    gain_grads = part(gain_grads, me.tok * 16, 16, 1)
     return (
         layer_output,
         input_grad,

time: 684 us -> 534 us (0.78)
  waiting for transfers between devices: 71.9 us -> 0.01 us
  starting transfers between devices: 54 us -> 4.78 us
  Pallas kernels: 435 us -> 472 us
  other arithmetic: 41.8 us -> 12.9 us
  matrix products: 22.2 us -> 3.26 us
  local copies, waits for them, and re-layouts: 51.2 us -> 33.3 us
    pallas_call x0 -> x1, Pallas kernels: none -> 92.9 us  [back(): pl.pallas_call(back_body, name='back', out_shape=outs, in_specs=[vm] * le...]
    pallas_call x8 -> x4, Pallas kernels: 161 us -> 105 us  [exchange(): pl.pallas_call(body, name=name, out_shape=outs, in_specs=[pl.BlockSpec(me...]
    ppermute x6 -> x1, waiting for transfers between devices: 55.1 us -> 0.01 us  [x_permute(): return lax.ppermute(value, 'wide', [(i, i ^ 1) for i in range(8)])]
    ppermute x22 -> x0, starting transfers between devices: 28.4 us -> none  [the longest x15 22.8 us: z_permute(): return lax.ppermute(value, 'tok', [(i, (i + 2 * d) % 8) for i in range(8)])]
    convert_element_type x13 -> x1, other arithmetic: 23.8 us -> 0.43 us  [per_device(): normed = (in_f * scale_one * attn_gain[None, :]).astype(BF)]
    dot_general x3 -> x0, matrix products: 15.3 us -> none  [contract_rows(): lax.dot_general(left_side, right_side, (((0,), (0,)), ((), ())), preferre...]
    dynamic_slice x6 -> x0, local copies, waits for them, and re-layouts: 12.3 us -> none  [pick(): return lax.dynamic_index_in_dim(array, index, axis, keepdims=False)]
    ppermute x6 -> x1, starting transfers between devices: 12.5 us -> 2.63 us  [x_permute(): return lax.ppermute(value, 'wide', [(i, i ^ 1) for i in range(8)])]
  transfers between devices with their start and end apart: 40 -> 3, of which waited for: 13 -> 0; matrix products, arithmetic and copies ran while one was open for 12% -> 4% of each run, Pallas kernels for 28% -> 27%
where the time goes in v3:
time: 534 us; the launch traced here: 528 us
  Pallas kernels  472 us (88%)
  local copies, waits for them, and re-layouts  33.3 us (6%)
  other arithmetic  12.9 us (2%)
    pallas_call x1, Pallas kernels, ffn(): pl.pallas_call(ffn_body, name='ffn', out_shape=[SDS((SUB, D), BF), SDS((S...  135 us
    pallas_call x1, Pallas kernels, gather_weights(): pl.pallas_call(weights_body, name='weights', out_shape=SDS((3, 3, 8, 128,...  127 us
    pallas_call x4, Pallas kernels, exchange(): pl.pallas_call(body, name=name, out_shape=outs, in_specs=[pl.BlockSpec(me...  105 us
    pallas_call x1, Pallas kernels, back(): pl.pallas_call(back_body, name='back', out_shape=outs, in_specs=[vm] * le...  92.9 us
    unnamed x95, local copies, waits for them, and re-layouts  15.8 us
    pallas_call x2, Pallas kernels, vmem_call(): pl.pallas_call(body, name=name, out_shape=outs, in_specs=[pl.BlockSpec(me...  12.4 us
  transfers between devices with their start and end apart: 3, of which 0 were waited for; matrix products, arithmetic and copies ran while one was open for 4% of the time, Pallas kernels for 27%

profile of v3, /device:TPU:0, one launch (start us, length us, event | category | flops | bytes accessed | tf_op | source)
XLA Modules:
  0.0 527.9 jit_solution(1570662959071960839)
XLA Ops:
  0.7 1.6 constant_dynamic-slice_fusion.3
  7.4 43.7 %enter.1 = (bf16[384,2048]{1,0:T(8,128)(2,1)S(1)}, bf16[2048,768]{1,0:T(8,128)(2,1)S(1)}, f32[16,8,128]{2,1,0:T(8,128)S(1)}) custom-call(bf16[1536,128]{1,0:T(8,128)(2,1)S(1)} %copy-done.2, bf16[2048,128]{1,0:T(8,128)(2,1)S(1)} %copy-done.1, bf16[2048,128]{1,0:T(8,128)(2,1)S(1)} %pad_maximum_fusion.1.refs_2_, f32[8,128]{1,0:T(8,128)S(1)} %broadcast_in_dim.4.refs_3_), custom_call_target="tpu_custom_call" | custom-call | tf_op jit(solution)/shard_map/enter/pallas_call | solution.py:136
  52.0 2.6 collective-permute-start.1
  54.6 1.3 collective-permute-start.2
  56.8 2.3 fusion.30
  59.0 1.6 fusion.25
  60.6 1.8 fusion.24
  63.0 1.7 fusion.27
  65.6 2.8 fusion.26
  68.5 2.4 fusion.12
  71.0 2.0 fusion.6
  73.0 1.8 concatenate.58.refs_0_
  74.7 9.9 %to_heads.1 = (bf16[1536,128]{1,0:T(8,128)(2,1)S(1)}, bf16[1536,128]{1,0:T(8,128)(2,1)S(1)}) custom-call(bf16[384,768]{1,0:T(8,128)(2,1)S(1)} %concatenate.58.refs_0_), custom_call_target="tpu_custom_call" | custom-call | tf_op jit(solution)/shard_map/to_heads/pallas_call | solution.py:136
  86.8 126.7 %weights.1.whole = bf16[3,3,8,128,1024]{4,3,2,1,0:T(8,128)(2,1)} custom-call(bf16[3,128,1024]{2,1,0:T(8,128)(2,1)} %pad_maximum_fusion.pieces), custom_call_target="tpu_custom_call" | custom-call | tf_op jit(solution)/shard_map/weights/pallas_call | solution.py:953
  216.3 4.7 attend.1.refs_0_
  221.1 11.3 %heads_out.1 = (bf16[384,512]{1,0:T(8,128)(2,1)S(1)}, bf16[2048,512]{1,0:T(8,128)(2,1)S(1)}) custom-call(bf16[1536,128]{1,0:T(8,128)(2,1)S(1)} %attend.1.refs_0_, bf16[2048,128]{1,0:T(8,128)(2,1)S(1)} %copy-done, bf16[1024,128]{1,0:T(8,128)(2,1)S(1)} %collective-permute-done.refs_2_, bf16[1024,128]{1,0:T(8,128)(2,1)S(1)} %collective-permute-done.1.refs_3_, ...), custom_call_target="tpu_custom_call" | custom-call | tf_op jit(solution)/shard_map/heads_out/pallas_call | solution.py:136
  232.4 1.3 copy-done.5
  234.8 40.6 %out_sum.1 = (bf16[4,96,2048]{2,1,0:T(8,128)(2,1)S(1)}, bf16[384,2048]{1,0:T(8,128)(2,1)S(1)}) custom-call(bf16[384,2048]{1,0:T(8,128)(2,1)S(1)} %convolution_convert_fusion.refs_0_, bf16[1536,128]{1,0:T(8,128)(2,1)S(1)} %copy-done.3), custom_call_target="tpu_custom_call" | custom-call | tf_op jit(solution)/shard_map/out_sum/pallas_call | solution.py:136
  275.7 1.1 multiply_reduce_fusion
  278.6 134.5 %ffn.1 = (bf16[96,2048]{1,0:T(8,128)(2,1)}, f32[96,2048]{1,0:T(8,128)}, f32[1,2048]{1,0:T(1,128)}, bf16[384,2048]{1,0:T(8,128)(2,1)}, bf16[1536,128]{1,0:T(8,128...) custom-call(bf16[96,2048]{1,0:T(8,128)(2,1)} %multiply_convert_fusio, ...), custom_call_target="tpu_custom_call" | custom-call | flops 25999998976 | bytes 41943040 | tf_op jit(solution)/shard_map/ffn/pallas_call | solution.py:1217
  414.2 7.7 %attend_back.1 = (bf16[1536,128]{1,0:T(8,128)(2,1)S(1)}, bf16[1536,128]{1,0:T(8,128)(2,1)S(1)}) custom-call(s32[1,2]{1,0:T(1,128)S(1)} %copy-done.14, bf16[1536,128]{1,0:T(8,128)(2,1)S(1)} %copy-done.9, bf16[1536,128]{1,0:T(8,128)(2,1)S(1)} %copy-done.12, bf16[1536,128]{1,0:T(8,128)(2,1)S(1)} %copy-done.19, f32[1024,128]{1,0:T(8,128)S(1)} %copy-done.15, ...), custom_call_target="tpu_custom_call" | custom-call | flops 5000000000 | bytes 1048576 | tf_op jit(solution)/shard_map/attend_back/pallas_call | solution.py:437
  423.3 92.9 %back.1 = (bf16[1536,128]{1,0:T(8,128)(2,1)}, bf16[1536,128]{1,0:T(8,128)(2,1)}, f32[256,128]{1,0:T(8,128)}, f32[4,32,128]{2,1,0:T(8,128)}, f32[256,128]{1,0:T(8...) custom-call(bf16[1536,128]{1,0:T(8,128)(2,1)} %copy-done.17, ...), custom_call_target="tpu_custom_call" | custom-call | flops 10000000000 | bytes 31457280 | tf_op jit(solution)/shard_map/back/pallas_call | solution.py:771
  520.3 1.8 copy.36
  522.1 1.8 copy.37
  (124 shorter events, 26.4 us)
Async XLA Ops:
  2.6 3.9 copy-start.43
  2.6 3.9 copy-start.1
  5.4 50.9 %copy-start.41 = (f32[2048]{0:T(1024)S(1)}, f32[2048]{0:T(1024)}, u32[]{:S(2)}) copy-start(f32[2048]{0:T(1024)} %param.16) | copy-start | bytes 24580
  51.1 5.6 %copy-start.4 = (bf16[2048,768]{1,0:T(8,128)(2,1)}, bf16[2048,768]{1,0:T(8,128)(2,1)S(1)}, u32[]{:S(2)}) copy-start(bf16[2048,768]{1,0:T(8,128)(2,1)S(1)} %get-tuple-element.47.w_attn) | copy-start | bytes 9437188
  51.1 169.9 %collective-permute-start = (bf16[1024,128]{1,0:T(8,128)(2,1)}, bf16[1024,128]{1,0:T(8,128)(2,1)S(1)}, u32[]{:S(2)}, u32[]{:S(2)}) collective-permute-start(bf16[1024,128]{1,0:T(8,128)(2,1)} %constant_dynamic-slice_fusion.2), channel_id=1, source_target_pairs={{0,8},{8,0},{1,9},{9,1},{2,10},{10,2},{3,11},{11,3},{4,12},{12,4},... | collective-permute-start | bytes 786440 | tf_op jit(solution)/shard_map/ppermute | solution.py:845
  52.0 169.1 %collective-permute-start.1 = (bf16[1024,128]{1,0:T(8,128)(2,1)}, bf16[1024,128]{1,0:T(8,128)(2,1)S(1)}, u32[]{:S(2)}, u32[]{:S(2)}) collective-permute-start(bf16[1024,128]{1,0:T(8,128)(2,1)} %constant_dynamic-slice_fusion.2), channel_id=1, source_target_pairs={{0,1},{1,0},{2,3},{3,2},{4,5},{5,4},{6,7},{7,6},{8,9},{9,8},{10,11... | collective-permute-start | bytes 786440 | tf_op jit(solution)/shard_map/ppermute | solution.py:847
  54.6 166.4 %collective-permute-start.2 = (bf16[1024,128]{1,0:T(8,128)(2,1)}, bf16[1024,128]{1,0:T(8,128)(2,1)S(1)}, u32[]{:S(2)}, u32[]{:S(2)}) collective-permute-start(bf16[1024,128]{1,0:T(8,128)(2,1)} %constant_dynamic-slice_fusion.2), channel_id=1, source_target_pairs={{0,9},{1,8},{2,11},{3,10},{4,13},{5,12},{6,15},{7,14},{8,1},{9,0},... | collective-permute-start | bytes 786440 | tf_op jit(solution)/shard_map/ppermute | solution.py:848
  64.7 3.7 copy-start.29
  64.7 3.7 copy-start.30
  64.7 3.8 copy-start.31
  64.7 3.8 copy-start.32
  64.7 3.8 copy-start.33
  64.8 3.8 copy-start.34
  64.8 3.8 copy-start.35
  64.8 3.8 copy-start.42
  278.6 134.5 %copy-start.9 = (bf16[1536,128]{1,0:T(8,128)(2,1)S(1)}, bf16[1536,128]{1,0:T(8,128)(2,1)}, u32[]{:S(2)}) copy-start(bf16[1536,128]{1,0:T(8,128)(2,1)} %copy-done.7) | copy-start | bytes 1179652
  278.6 134.6 %copy-start.12 = (bf16[1536,128]{1,0:T(8,128)(2,1)S(1)}, bf16[1536,128]{1,0:T(8,128)(2,1)}, u32[]{:S(2)}) copy-start(bf16[1536,128]{1,0:T(8,128)(2,1)} %copy-done.10) | copy-start | bytes 1179652
  278.6 134.6 %copy-start.15 = (f32[1024,128]{1,0:T(8,128)S(1)}, f32[1024,128]{1,0:T(8,128)}, u32[]{:S(2)}) copy-start(f32[1024,128]{1,0:T(8,128)} %constant.118.cos_ref) | copy-start | bytes 1572868
  278.6 134.6 %copy-start.16 = (f32[1024,128]{1,0:T(8,128)S(1)}, f32[1024,128]{1,0:T(8,128)}, u32[]{:S(2)}) copy-start(f32[1024,128]{1,0:T(8,128)} %constant.119.sin_ref) | copy-start | bytes 1572868
  516.3 7.6 %copy-start.40 = (f32[256,128]{1,0:T(8,128)S(1)}, f32[256,128]{1,0:T(8,128)}, u32[]{:S(2)}) copy-start(f32[256,128]{1,0:T(8,128)} %get-tuple-element.148) | copy-start | bytes 393220
  516.3 8.3 %copy-start.39 = (f32[256,128]{1,0:T(8,128)S(1)}, f32[256,128]{1,0:T(8,128)}, u32[]{:S(2)}) copy-start(f32[256,128]{1,0:T(8,128)} %get-tuple-element.151) | copy-start | bytes 393220
  516.3 8.9 %copy-start.38 = (f32[8,16,1024]{2,1,0:T(8,128)S(1)}, f32[8,16,1024]{2,1,0:T(8,128)}, u32[]{:S(2)}) copy-start(f32[8,16,1024]{2,1,0:T(8,128)} %get-tuple-element.153) | copy-start | bytes 1572868
  516.3 9.7 %copy-start.37 = (f32[8,16,1024]{2,1,0:T(8,128)S(1)}, f32[8,16,1024]{2,1,0:T(8,128)}, u32[]{:S(2)}) copy-start(f32[8,16,1024]{2,1,0:T(8,128)} %get-tuple-element.154) | copy-start | bytes 1572868
  520.3 6.5 %copy-start.36 = (f32[8,16,1024]{2,1,0:T(8,128)S(1)}, f32[8,16,1024]{2,1,0:T(8,128)}, u32[]{:S(2)}) copy-start(f32[8,16,1024]{2,1,0:T(8,128)} %get-tuple-element.155) | copy-start | bytes 1572868
  (23 other events, 38.4 us)

commit v4 on v3

--- a/solution.py
+++ b/solution.py
@@ -70,281 +70,8 @@
     return pl.ds(pl.multiple_of(start, size), size)
 
 
-def exchange(name, number, plan, ins, outs):
-    n_in, n_out = len(ins), len(outs)
-
-    def count():
-        fake = Place(0, 0, 0, 0, 0)
-        probe = [_Any() for _ in range(n_in)], [_Any() for _ in range(n_out)]
-        local, sends = plan(fake, *probe)
-        return len(local), sum(1 + len(s[3]) for s in sends)
-
-    n_local, n_send = count()
-
-    def body(*refs):
-        sources, targets = refs[:n_in], refs[n_in : n_in + n_out]
-        send_sem, recv_sem, local_sem = refs[n_in + n_out :]
-        me = whereami()
-        local, sends = plan(me, sources, targets)
-        offsets = []
-        for off, _, _, forwards in sends:
-            for o in [off] + [f[0] for f in forwards]:
-                if o not in offsets:
-                    offsets.append(o)
-        barrier = pltpu.get_barrier_semaphore()
-        for off in offsets:
-            back = tuple(-v for v in off)
-            pl.semaphore_signal(
-                barrier, inc=1, device_id=me.at(back).device(), device_id_type=MESH
-            )
-        near = []
-        for i, (src, dst) in enumerate(local):
-            near.append(pltpu.make_async_copy(src, dst, local_sem.at[i]))
-            near[-1].start()
-        pl.semaphore_wait(barrier, len(offsets))
-        slot = 0
-
-        def launch(off, src, dst):
-            nonlocal slot
-            copy = pltpu.make_async_remote_copy(
-                src_ref=src,
-                dst_ref=dst,
-                send_sem=send_sem.at[slot],
-                recv_sem=recv_sem.at[slot],
-                device_id=me.at(off).device(),
-                device_id_type=MESH,
-            )
-            copy.start()
-            slot += 1
-            return copy
-
-        first = [(launch(off, src, dst), forwards) for off, src, dst, forwards in sends]
-        second = []
-        for copy, forwards in first:
-            if forwards:
-                copy.wait_recv()
-                second += [launch(*f) for f in forwards]
-        for copy, forwards in first:
-            copy.wait_send()
-            if not forwards:
-                copy.wait_recv()
-        for copy in second:
-            copy.wait()
-        for copy in near:
-            copy.wait()
-
-    return pl.pallas_call(
-        body,
-        name=name,
-        out_shape=outs,
-        in_specs=[pl.BlockSpec(memory_space=pl.ANY)] * n_in,
-        out_specs=[pl.BlockSpec(memory_space=pltpu.VMEM)] * n_out,
-        scratch_shapes=[
-            pltpu.SemaphoreType.DMA((n_send,)),
-            pltpu.SemaphoreType.DMA((n_send,)),
-            pltpu.SemaphoreType.DMA((max(n_local, 1),)),
-        ],
-        compiler_params=pltpu.CompilerParams(
-            collective_id=number, has_side_effects=True, vmem_limit_bytes=40 * 2**20
-        ),
-    )(*ins)
-
-
-class _Any:
-    @property
-    def at(self):
-        return self
-
-    def __getitem__(self, key):
-        return self
-
-
 def lanes(index, size=128):
     return pl.ds(pl.multiple_of(index * size, size), size)
-
-
-def spread_plan(me, src, dst, own_first=False):
-    def block(off):
-        return lanes(off[2] * 8 + me.wide if own_first else me.block)
-
-    local = [(src.at[rows(me.chunk * CHUNK, CHUNK), :], dst.at[:, block(HERE)])]
-    sends = [
-        (off, src.at[rows(me.at(off).chunk * CHUNK, CHUNK), :], dst.at[:, block(off)], [])
-        for off in PLANE[1:]
-    ]
-    return local, sends
-
-
-def enter_plan(me, ins, outs):
-    hidden, w_q, w_kv, gain = ins
-    full, w_attn, gains = outs
-    half = rows(me.core * 1024, 1024)
-    local, sends = spread_plan(me, hidden, full)
-    local += [
-        (w_q, w_attn.at[:, 0:128]),
-        (w_kv, w_attn.at[:, 512:640]),
-        (gain, gains.at[me.block]),
-    ]
-    head = []
-    for k in (1, 2, 3):
-        cols = slice(k * 128, k * 128 + 128)
-        block = w_attn.at[half, cols]
-        head.append((XOFF[k], w_q.at[half, :], block, [(SIBLING, block, block)]))
-    block = w_attn.at[half, 640:768]
-    head.append((XOFF[1], w_kv.at[half, :], block, [(SIBLING, block, block)]))
-    sends = head + sends
-    sends += [(off, gain, gains.at[me.block], []) for off in PLANE[1:]]
-    return local, sends
-
-
-def to_heads_plan(me, ins, outs):
-    (lin,) = ins
-    q, kv = outs
-    mine = rows(me.chunk * CHUNK, CHUNK)
-    local, sends = [], []
-    for k, off in enumerate(XOFF):
-        kv_col = 512 + 128 * off[2]
-        pairs = [
-            (lin.at[:, k * 128 : k * 128 + 128], q.at[mine, :]),
-            (lin.at[:, kv_col : kv_col + 128], kv.at[mine, :]),
-        ]
-        if k == 0:
-            local += pairs
-        else:
-            sends += [(off, s, d, []) for s, d in pairs]
-    return local, sends
-
-
-def from_heads_moves(me, src, dst, first_col=0):
-    local, sends = [], []
-    for k, off in enumerate(XOFF):
-        col = first_col + k * 128
-        pair = (src.at[rows(me.at(off).chunk * CHUNK, CHUNK), :], dst.at[:, col : col + 128])
-        if k == 0:
-            local.append(pair)
-        else:
-            sends.append((off, *pair, []))
-    return local, sends
-
-
-def heads_out_plan(me, ins, outs):
-    heads, w_out, half1, half2, half3 = ins
-    cat, w_cat = outs
-    local, sends = from_heads_moves(me, heads, cat)
-    half = rows(me.core * 1024, 1024)
-    local.append((w_out, w_cat.at[:, 0:128]))
-    for k, part in ((1, half1), (2, half2), (3, half3)):
-        block = w_cat.at[half, k * 128 : k * 128 + 128]
-        local.append((part, block))
-        sends.append((SIBLING, part, block, []))
-    return local, sends
-
-
-def heads_back_plan(me, ins, outs):
-    (cat,) = ins
-    (heads,) = outs
-    mine = rows(me.chunk * CHUNK, CHUNK)
-    local, sends = [], []
-    for k, off in enumerate(XOFF):
-        pair = (cat.at[:, k * 128 : k * 128 + 128], heads.at[mine, :])
-        if k == 0:
-            local.append(pair)
-        else:
-            sends.append((off, *pair, []))
-    return local, sends
-
-
-def grads_out_plan(me, ins, outs):
-    q, kv = ins
-    (cat,) = outs
-    local, sends = from_heads_moves(me, q, cat)
-    local2, sends2 = from_heads_moves(me, kv, cat, 512)
-    return local + local2, sends + sends2
-
-
-def scatter_moves(me, src, dst):
-    local = [(src.at[rows(me.y * SUB, SUB), :], dst.at[me.y])]
-    sends = [(off, src.at[rows(me.at(off).y * SUB, SUB), :], dst.at[me.y], []) for off in YOFF[1:]]
-    return local, sends
-
-
-def out_sum_plan(me, ins, outs):
-    local, sends = scatter_moves(me, ins[0], outs[0])
-    local2, sends2 = spread_plan(me, ins[1], outs[1], True)
-    return local + local2, sends + sends2
-
-
-def sum_plan(me, ins, outs):
-    local, sends = [], []
-    for src, dst in zip(ins, outs):
-        a, b = scatter_moves(me, src, dst)
-        local, sends = local + a, sends + b
-    return local, sends
-
-
-def gather_moves(me, src, dst):
-    block = dst.at[rows(me.y * SUB, SUB), :]
-    return [(src, block)], [(off, src, block, []) for off in YOFF[1:]]
-
-
-def gather_plan(me, ins, outs):
-    return gather_moves(me, ins[0], outs[0])
-
-
-def weight_moves(me, own, parts, dst):
-    local = [(own, dst.at[rows(me.xl * 1024, 1024), lanes(me.xh, 1024)])]
-    sends = []
-    for off, part in zip(XOFF[1:], parts):
-        there = me.at(off)
-        block = dst.at[rows(there.xl * 1024 + me.core * 512, 512), lanes(there.xh, 1024)]
-        local.append((part, block))
-        sends.append((SIBLING, part, block, []))
-    return local, sends
-
-
-def weight_moves_t(me, own, parts, dst):
-    local = [(own, dst.at[rows(me.xh * 1024, 1024), lanes(me.xl, 1024)])]
-    sends = []
-    for off, part in zip(XOFF[1:], parts):
-        there = me.at(off)
-        block = dst.at[rows(there.xh * 1024 + me.core * 512, 512), lanes(there.xl, 1024)]
-        local.append((part, block))
-        sends.append((SIBLING, part, block, []))
-    return local, sends
-
-
-def ffn_enter_plan(me, ins, outs):
-    hidden, gate, up, p1, p2, p3 = ins
-    full, w_gate, w_up = outs
-    local, sends = gather_moves(me, hidden, full)
-    for j, (own, dst) in enumerate(((gate, w_gate), (up, w_up))):
-        a, b = weight_moves(me, own, [p.at[j] for p in (p1, p2, p3)], dst)
-        local, sends = local + a, sends + b
-    return local, sends
-
-
-def down_plan(me, ins, outs):
-    return weight_moves_t(me, ins[0], ins[1:], outs[0])
-
-
-def leave_plan(me, ins, outs):
-    local, sends = [], []
-    mine = rows(me.chunk * CHUNK + me.y * SUB, SUB)
-    for k, off in enumerate(PLANE):
-        there = me.at(off)
-        pairs = [(src.at[:, lanes(there.block)], dst.at[mine, :]) for src, dst in zip(ins[:2], outs[:2])]
-        pairs.append((ins[2].at[:, lanes(there.block)], outs[2].at[me.block]))
-        if k == 0:
-            local += pairs
-        else:
-            sends += [(off, s, d, []) for s, d in pairs]
-    return local, sends
-
-
-def gains_plan(me, ins, outs):
-    local = [(ins[0], outs[0].at[me.tok])]
-    sends = [(off, ins[0], outs[0].at[me.tok], []) for off in TOKS[1:]]
-    return local, sends
 
 
 def block_probs(q_ref, kv_ref, start, i, stack):
@@ -852,27 +579,8 @@
     return lax.ppermute(value, "tok", [(i, (i + 2 * d) % 8) for i in range(8)])
 
 
-def y_permute(value, d):
-    return lax.ppermute(value, "wide", [(i, (i + 2 * d) % 8) for i in range(8)])
-
-
-def core_permute(value):
-    return lax.ppermute(value, "tok", [(i, i ^ 1) for i in range(8)])
-
-
-def pick(array, index, axis):
-    return lax.dynamic_index_in_dim(array, index, axis, keepdims=False)
-
-
 def part(array, start, size, axis):
     return lax.dynamic_slice_in_dim(array, start, size, axis)
-
-
-def total(terms):
-    out = terms[0].astype(F32)
-    for term in terms[1:]:
-        out = out + term.astype(F32)
-    return out
 
 
 def contract_rows(left_side, right_side):
@@ -925,40 +633,255 @@
 ZOFF = [(0, d, 0, 0, 0) for d in range(4)]
 
 
-def weights_body(pieces, whole, send_sem, recv_sem):
+def weights_body(pieces, came, send_sem, recv_sem):
     me = whereami()
     wire = Wire(me, send_sem, recv_sem)
-    meet(me, XOFF[1:] + ZOFF[1:] + [SIBLING])
-    over_x = [wire.send(XOFF[k], pieces, whole.at[k - 1, :, me.tok]) for k in (1, 2, 3)]
-    over_z, over_core = [], []
-    for k in (1, 2, 3):
-        over_x[k - 1].wait_recv()
-        block = whole.at[k - 1, :, me.tok]
-        over_core.append(wire.send(SIBLING, block, block))
-        over_z.append([wire.send(ZOFF[d], block, block) for d in (1, 2, 3)])
-    for k in (1, 2, 3):
-        for d in (1, 2, 3):
-            over_z[k - 1][d - 1].wait_recv()
-            block = whole.at[k - 1, :, (me.z - d + 4) % 4 * 2 + me.core]
-            over_core.append(wire.send(SIBLING, block, block))
-    for copy in over_x:
-        copy.wait_send()
-    for copies in over_z:
-        for copy in copies:
-            copy.wait_send()
-    finish(over_core)
-
-
-def gather_weights(pieces):
+    meet(me, XOFF[1:])
+    finish([wire.send(XOFF[k], pieces, came.at[k - 1]) for k in (1, 2, 3)])
+
+
+def weights_over_x(pieces):
     return pl.pallas_call(
         weights_body,
         name="weights",
-        out_shape=SDS((3, 3, 8, 128, 1024), BF),
+        out_shape=SDS((3, 3, 128, 1024), BF),
         in_specs=[pl.BlockSpec(memory_space=pl.ANY)],
         out_specs=pl.BlockSpec(memory_space=pl.ANY),
-        scratch_shapes=[pltpu.SemaphoreType.DMA((24,)), pltpu.SemaphoreType.DMA((24,))],
+        scratch_shapes=[pltpu.SemaphoreType.DMA((3,)), pltpu.SemaphoreType.DMA((3,))],
         compiler_params=pltpu.CompilerParams(collective_id=13, has_side_effects=True),
     )(pieces)
+
+
+def split_rows(count, size):
+    return [slice(i * size, i * size + size) for i in range(count)]
+
+
+def front_body(
+    gain_row,
+    attn_gain,
+    cos_ref,
+    sin_ref,
+    hidden,
+    w_q,
+    w_kv,
+    out_grad,
+    q,
+    kv,
+    w_attn,
+    normed,
+    in_mine,
+    scale_mine,
+    gains,
+    grad_full,
+    full,
+    lin,
+    scales,
+    send_sem,
+    recv_sem,
+    local_sem,
+):
+    me = whereami()
+    wire = Wire(me, send_sem, recv_sem)
+    chunk = rows(me.chunk * CHUNK, CHUNK)
+    near = []
+
+    def take(src, dst):
+        near.append(pltpu.make_async_copy(src, dst, local_sem.at[len(near)]))
+        near[-1].start()
+
+    take(w_q, w_attn.at[:, 0:128])
+    take(w_kv, w_attn.at[:, 512:640])
+    take(hidden.at[chunk, :], full.at[:, lanes(me.block)])
+    take(out_grad.at[chunk, :], grad_full.at[:, lanes(me.wide)])
+    gains[me.block] = gain_row[...]
+    meet(me, PLANE[1:] + [SIBLING])
+
+    half = rows(me.core * 1024, 1024)
+    blocks = [w_attn.at[half, k * 128 : k * 128 + 128] for k in (1, 2, 3)]
+    over_x = [wire.send(XOFF[k], w_q.at[half, :], blocks[k - 1]) for k in (1, 2, 3)]
+    blocks.append(w_attn.at[half, 640:768])
+    over_x.append(wire.send(XOFF[1], w_kv.at[half, :], blocks[3]))
+
+    def chunk_of(off):
+        return rows(me.at(off).chunk * CHUNK, CHUNK)
+
+    enter = [
+        wire.send(off, hidden.at[chunk_of(off), :], full.at[:, lanes(me.block)])
+        for off in PLANE[1:]
+    ]
+    others = [wire.send(off, gain_row, gains.at[me.block]) for off in PLANE[1:]]
+    others += [
+        wire.send(off, out_grad.at[chunk_of(off), :], grad_full.at[:, lanes(off[2] * 8 + me.wide)])
+        for off in PLANE[1:]
+    ]
+    over_core = []
+    for copy, block in zip(over_x, blocks):
+        copy.wait_recv()
+        over_core.append(wire.send(SIBLING, block, block))
+    for copy in enter:
+        copy.wait_recv()
+    for copy in near:
+        copy.wait()
+    for part_rows in split_rows(4, SUB):
+        value = full[part_rows, :].astype(F32)
+        scale = lax.rsqrt(jnp.mean(value * value, axis=1, keepdims=True) + EPS)
+        scales[part_rows, :] = scale
+        normed[part_rows, :] = (value * scale * attn_gain[...]).astype(BF)
+    for copy in over_core:
+        copy.wait_recv()
+    lane = lax.broadcasted_iota(jnp.int32, (CHUNK, 128), 1)
+    for k in range(6):
+        cols = slice(k * 128, k * 128 + 128)
+        block = multiply(normed[...], w_attn[:, cols])
+        swapped = jnp.where(
+            (lane % 64) < 32, -pltpu.roll(block, 96, 1), pltpu.roll(block, 32, 1)
+        )
+        turned = block * cos_ref[...] + swapped * sin_ref[...]
+        if k >= 4:
+            turned = jnp.where(lane < 64, turned, block)
+        lin[:, cols] = turned.astype(BF)
+    moves = []
+    for k in (1, 2, 3):
+        kv_col = 512 + 128 * XOFF[k][2]
+        moves.append(wire.send(XOFF[k], lin.at[:, k * 128 : k * 128 + 128], q.at[chunk, :]))
+        moves.append(wire.send(XOFF[k], lin.at[:, kv_col : kv_col + 128], kv.at[chunk, :]))
+    q[chunk, :] = lin[:, 0:128]
+    kv[chunk, :] = lin[:, 512:640]
+    here = rows(me.y * SUB, SUB)
+    in_mine[...] = full[here, :]
+    scale_mine[...] = scales[here, :]
+    for copy in over_x + enter:
+        copy.wait_send()
+    for copy in over_core:
+        copy.wait_send()
+    finish(others + moves)
+
+
+def front(gain_row, attn_gain, cos_here, sin_here, hidden, w_q, w_kv, out_grad):
+    vm = pl.BlockSpec(memory_space=pltpu.VMEM)
+    hbm = pl.BlockSpec(memory_space=pl.ANY)
+    outs = [
+        SDS((ROWS, 128), BF),
+        SDS((ROWS, 128), BF),
+        SDS((D, 768), BF),
+        SDS((CHUNK, D), BF),
+        SDS((SUB, D), BF),
+        SDS((SUB, 1), F32),
+        SDS((16, 8, 128), F32),
+        SDS((CHUNK, D), BF),
+    ]
+    return pl.pallas_call(
+        front_body,
+        name="front",
+        out_shape=outs,
+        in_specs=[vm] * 4 + [hbm] * 4,
+        out_specs=[vm] * len(outs),
+        scratch_shapes=[
+            pltpu.VMEM((CHUNK, D), BF),
+            pltpu.VMEM((CHUNK, 768), BF),
+            pltpu.VMEM((CHUNK, 1), F32),
+            pltpu.SemaphoreType.DMA((60,)),
+            pltpu.SemaphoreType.DMA((60,)),
+            pltpu.SemaphoreType.DMA((4,)),
+        ],
+        compiler_params=pltpu.CompilerParams(
+            collective_id=0, has_side_effects=True, vmem_limit_bytes=40 * 2**20
+        ),
+        cost_estimate=pl.CostEstimate(flops=2 * 10**9, bytes_accessed=2**23, transcendentals=0),
+    )(gain_row, attn_gain, cos_here, sin_here, hidden, w_q, w_kv, out_grad)
+
+
+def middle_body(
+    heads,
+    in_mine,
+    gain,
+    w_out,
+    half1,
+    half2,
+    half3,
+    heads_cat,
+    w_cat,
+    resid,
+    scale_out,
+    ffn_mine,
+    term_send,
+    term_recv,
+    send_sem,
+    recv_sem,
+    local_sem,
+):
+    me = whereami()
+    wire = Wire(me, send_sem, recv_sem)
+    half = rows(me.core * 1024, 1024)
+    blocks = [w_cat.at[half, k * 128 : k * 128 + 128] for k in (1, 2, 3)]
+    pairs = [(w_out, w_cat.at[:, 0:128])] + list(zip((half1, half2, half3), blocks))
+    near = []
+    for src, dst in pairs:
+        near.append(pltpu.make_async_copy(src, dst, local_sem.at[len(near)]))
+        near[-1].start()
+    meet(me, XOFF[1:] + YOFF[1:] + [SIBLING])
+    moves = [
+        wire.send(
+            XOFF[k],
+            heads.at[rows(me.at(XOFF[k]).chunk * CHUNK, CHUNK), :],
+            heads_cat.at[:, k * 128 : k * 128 + 128],
+        )
+        for k in (1, 2, 3)
+    ]
+    moves += [wire.send(SIBLING, src, dst) for src, dst in pairs[1:]]
+    heads_cat[:, 0:128] = heads[rows(me.chunk * CHUNK, CHUNK), :]
+    for copy in near:
+        copy.wait()
+    finish(moves)
+    sums = []
+    for h in range(2):
+        for p in range(2):
+            cols = slice(h * 1024 + p * 512, h * 1024 + p * 512 + 512)
+            term_send[:, cols] = contract_cols(heads_cat[...], w_cat[cols, :]).astype(BF)
+        cols = slice(h * 1024, h * 1024 + 1024)
+        for d in (1, 2, 3):
+            there = rows(me.at(YOFF[d]).y * SUB, SUB)
+            sums.append(
+                wire.send(YOFF[d], term_send.at[there, cols], term_recv.at[d - 1, :, cols])
+            )
+    finish(sums)
+    value = in_mine[...].astype(F32) + term_send[rows(me.y * SUB, SUB), :].astype(F32)
+    for d in range(3):
+        value = value + term_recv[d].astype(F32)
+    resid[...] = value
+    scale = lax.rsqrt(jnp.mean(value * value, axis=1, keepdims=True) + EPS)
+    scale_out[...] = scale
+    ffn_mine[...] = (value * scale * gain[...]).astype(BF)
+
+
+def middle(heads, in_mine, gain, w_out, halves):
+    vm = pl.BlockSpec(memory_space=pltpu.VMEM)
+    hbm = pl.BlockSpec(memory_space=pl.ANY)
+    outs = [
+        SDS((CHUNK, 512), BF),
+        SDS((D, 512), BF),
+        SDS((SUB, D), F32),
+        SDS((SUB, 1), F32),
+        SDS((SUB, D), BF),
+    ]
+    return pl.pallas_call(
+        middle_body,
+        name="middle",
+        out_shape=outs,
+        in_specs=[vm] * 3 + [hbm] * 4,
+        out_specs=[vm] * len(outs),
+        scratch_shapes=[
+            pltpu.VMEM((CHUNK, D), BF),
+            pltpu.VMEM((3, SUB, D), BF),
+            pltpu.SemaphoreType.DMA((12,)),
+            pltpu.SemaphoreType.DMA((12,)),
+            pltpu.SemaphoreType.DMA((4,)),
+        ],
+        compiler_params=pltpu.CompilerParams(
+            collective_id=1, has_side_effects=True, vmem_limit_bytes=32 * 2**20
+        ),
+        cost_estimate=pl.CostEstimate(flops=10**9, bytes_accessed=2**23, transcendentals=0),
+    )(heads, in_mine, gain, w_out, *halves)
 
 
 class PairSum:
@@ -1014,7 +937,10 @@
     own_gate,
     own_up,
     own_down,
-    whole,
+    piece0,
+    piece1,
+    piece2,
+    piece3,
     out_mine,
     resid_back,
     gain_part,
@@ -1026,6 +952,7 @@
     down_came,
     gate_own,
     gate_came,
+    other_core,
     turned,
     act,
     gate_back,
@@ -1056,41 +983,75 @@
     half = [lanes(me.xl, 1024), lanes(1 - me.xl, 1024)]
     here = rows(me.y * SUB, SUB)
 
+    pieces = (piece0, piece1, piece2, piece3)
+
     def tile_copies(e, q, slot):
-        copies = []
+        copies, groups = [], []
         cols = pl.ds(pl.multiple_of(q * 256, 256), 256)
+
+        def copy(src, dst):
+            sem = tile_sem.at[slot, len(copies) + len(groups)]
+            return pltpu.make_async_copy(src, dst, sem)
+
         for dxl in range(2):
             k = e * 2 + dxl
-            for j, (own, tile) in enumerate(
-                ((own_gate, gate_tile), (own_up, up_tile), (own_down, down_tile))
-            ):
-                block = own if k == 0 else whole.at[k - 1, j]
-                if j < 2:
-                    src, dst = block.at[:, :, cols], tile.at[slot, dxl]
-                else:
-                    src = block.at[pl.ds(q * 2, 2)]
-                    dst = tile.at[slot, :, :, dxl * 1024 : dxl * 1024 + 1024]
-                copies.append(pltpu.make_async_copy(src, dst, tile_sem.at[slot, dxl * 3 + j]))
-        return copies
+            for j, (own, tile) in enumerate(((own_gate, gate_tile), (own_up, up_tile))):
+                if k == 0:
+                    copies.append(copy(own.at[:, :, :, cols], tile.at[slot, dxl]))
+                    continue
+                for d, piece in enumerate(pieces):
+                    spot = tile.at[slot, dxl, (me.z - d + 4) % 4, me.core]
+                    copies.append(copy(piece.at[k - 1, j, :, cols], spot))
+                spot = tile.at[slot, dxl, :, 1 - me.core]
+                copies.append(copy(other_core.at[:, k - 1, j, :, cols], spot))
+            here = slice(dxl * 1024, dxl * 1024 + 1024)
+            if k == 0:
+                copies.append(copy(own_down.at[q], down_tile.at[slot, :, :, here]))
+                continue
+            spot = down_tile.at[slot, 1 - me.core, :, here]
+            copies.append(copy(other_core.at[q, k - 1, 2], spot))
+            spot = down_tile.at[slot, me.core, :, here]
+            groups.append([copy(piece.at[k - 1, 2], spot) for piece in pieces])
+        return copies, groups
 
     def fetch(e, q, slot):
-        for copy in tile_copies(e, q, slot):
+        copies, groups = tile_copies(e, q, slot)
+        for copy in copies:
             copy.start()
+        for group in groups:
+            for d, copy in enumerate(group):
+                pl.when((me.z - q + 4) % 4 == d)(copy.start)
+
+    def arrive(e, q, slot):
+        copies, groups = tile_copies(e, q, slot)
+        for copy in copies + [group[0] for group in groups]:
+            copy.wait()
 
     meet(me, YOFF[1:] + XOFF[1:] + ZOFF[1:] + [SIBLING])
     for h in range(2):
         turned[:, h * 1024 : h * 1024 + 1024] = mine_ref[:, half[h]]
     gathers = [wire.send(off, turned, ffn_in.at[here, :]) for off in YOFF[1:]]
-    fetch(0, 0, 0)
+    shares = [
+        [
+            wire.send(SIBLING, piece.at[k], other_core.at[(me.z - d + 4) % 4, k])
+            for d, piece in enumerate(pieces)
+        ]
+        for k in range(3)
+    ]
     ffn_in[here, :] = turned[...]
     down_acc[...] = jnp.zeros(down_acc.shape, F32)
     ffn_acc[...] = jnp.zeros(ffn_acc.shape, F32)
+    finish(shares[0])
+    fetch(0, 0, 0)
     finish(gathers)
 
     down_sum = PairSum(me, act, grad_ref, down_terms, came, core_send.at[0], core_recv.at[0])
     gate_sum = PairSum(me, ffn_in, gate_back, gate_terms, came, core_send.at[1], core_recv.at[1])
 
     for e in range(2):
+
+        if e == 0:
+            finish(shares[1] + shares[2])
 
         def step(q, _, e=e):
             slot = q % 2
@@ -1105,8 +1066,7 @@
                 def _():
                     fetch(1, 0, 0)
 
-            for copy in tile_copies(e, q, slot):
-                copy.wait()
+            arrive(e, q, slot)
             cols = pl.ds(pl.multiple_of(e * 1024 + q * 256, 256), 256)
             w_g = gate_tile[slot].reshape(2048, 256)
             w_u = up_tile[slot].reshape(2048, 256)
@@ -1211,7 +1171,7 @@
     gate_sum.sent()
 
 
-def ffn(ffn_mine, grad_full, resid, scale_two, gain, w_out, w_gate, w_up, w_down, whole):
+def ffn(ffn_mine, grad_full, resid, scale_two, gain, w_out, w_gate, w_up, w_down, pieces):
     vm = pl.BlockSpec(memory_space=pltpu.VMEM)
     hbm = pl.BlockSpec(memory_space=pl.ANY)
     return pl.pallas_call(
@@ -1229,15 +1189,16 @@
             SDS((3, 4, 2, 4, 16, 1024), BF),
             SDS((8, 2, 16, 2048), BF),
             SDS((3, 8, 2, 16, 2048), BF),
+            SDS((4, 3, 3, 128, 1024), BF),
         ],
-        in_specs=[vm] * 6 + [hbm] * 4,
-        out_specs=[vm] * 7 + [hbm] * 4,
+        in_specs=[vm] * 6 + [hbm] * 7,
+        out_specs=[vm] * 7 + [hbm] * 5,
         scratch_shapes=[
             pltpu.VMEM((SUB, D), BF),
             pltpu.VMEM((CHUNK, D), BF),
             pltpu.VMEM((CHUNK, D), BF),
-            pltpu.VMEM((2, 2, 8, 128, 256), BF),
-            pltpu.VMEM((2, 2, 8, 128, 256), BF),
+            pltpu.VMEM((2, 2, 4, 2, 128, 256), BF),
+            pltpu.VMEM((2, 2, 4, 2, 128, 256), BF),
             pltpu.VMEM((2, 2, 128, 2048), BF),
             pltpu.VMEM((CHUNK, D), F32),
             pltpu.VMEM((CHUNK, D), F32),
@@ -1250,11 +1211,11 @@
             pltpu.VMEM((8, 2, 4, 2, 16, 2048), BF),
             pltpu.VMEM((8, 2, 4, 2, 16, 2048), BF),
             pltpu.VMEM((8, 2, 4, 16, 2048), BF),
-            pltpu.SemaphoreType.DMA((24,)),
-            pltpu.SemaphoreType.DMA((24,)),
+            pltpu.SemaphoreType.DMA((36,)),
+            pltpu.SemaphoreType.DMA((36,)),
             pltpu.SemaphoreType.DMA((2, 8)),
             pltpu.SemaphoreType.DMA((2, 8)),
-            pltpu.SemaphoreType.DMA((2, 6)),
+            pltpu.SemaphoreType.DMA((2, 24)),
             pltpu.SemaphoreType.DMA((2,)),
             pltpu.SemaphoreType.REGULAR,
         ],
@@ -1269,10 +1230,10 @@
         scale_two,
         gain,
         w_out,
-        w_gate.reshape(8, 128, 1024),
-        w_up.reshape(8, 128, 1024),
-        w_down.reshape(8, 128, 1024),
-        whole,
+        w_gate.reshape(4, 2, 128, 1024),
+        w_up.reshape(4, 2, 128, 1024),
+        w_down.reshape(4, 2, 128, 1024),
+        *pieces,
     )
 
 
@@ -1301,64 +1262,29 @@
     w_kv = jnp.concatenate(
         [part(w_key, me.y * 64, 64, 1), part(w_value, me.y * 64, 64, 1)], axis=1
     )
-    full_in, w_attn, gains = exchange(
-        "enter",
-        0,
-        enter_plan,
-        [layer_input, w_query, w_kv, jnp.broadcast_to(ffn_gain[None, :], (8, 128))],
-        [SDS((CHUNK, D), BF), SDS((D, 768), BF), SDS((16, 8, 128), F32)],
+    pieces = jnp.stack([part(w, me.tok * 128, 128, 0) for w in (w_gate, w_up, w_down)])
+    pieces = [weights_over_x(pieces)]
+    pieces += [z_permute(pieces[0], d) for d in (1, 2, 3)]
+    queries, kv, w_attn, normed, in_mine, scale_mine, gains, grad_full = front(
+        jnp.broadcast_to(ffn_gain[None, :], (8, 128)),
+        attn_gain[None, :],
+        cos_here,
+        sin_here,
+        layer_input,
+        w_query,
+        w_kv,
+        output_grad,
     )
     ffn_gain_all = gains[:, 0, :].reshape(1, D)
-
     half_out = part(w_output, me.core * 1024, 1024, 0)
-    pieces = jnp.stack([part(w, me.tok * 128, 128, 0) for w in (w_gate, w_up, w_down)])
-    full_in, half_out, pieces = lax.optimization_barrier((full_in, half_out, pieces))
-    whole = gather_weights(pieces)
+    queries, half_out = lax.optimization_barrier((queries, half_out))
     got_out = [x_permute(half_out, k) for k in (1, 2, 3)]
-
-    in_f = full_in.astype(F32)
-    scale_one = lax.rsqrt(jnp.mean(in_f * in_f, axis=1, keepdims=True) + EPS)
-    normed = (in_f * scale_one * attn_gain[None, :]).astype(BF)
-    lin = multiply(normed, w_attn)
-
-    def turn(block):
-        lane = lax.broadcasted_iota(jnp.int32, block.shape, 1)
-        swapped = jnp.where(
-            (lane % 64) < 32, -jnp.roll(block, -32, axis=1), jnp.roll(block, 32, axis=1)
-        )
-        return block * cos_here + swapped * sin_here
-
-    turned = [turn(lin[:, k * 128 : k * 128 + 128]) for k in range(6)]
-    for k in (4, 5):
-        turned[k] = jnp.concatenate(
-            [turned[k][:, :64], lin[:, k * 128 + 64 : k * 128 + 128]], axis=1
-        )
-    lin = jnp.concatenate(turned, axis=1).astype(BF)
-    queries, kv = exchange(
-        "to_heads", 1, to_heads_plan, [lin], [SDS((ROWS, 128), BF), SDS((ROWS, 128), BF)]
-    )
     (heads_out,) = vmem_call(
         "attend", attend_body, [doc_lengths, queries, kv], [SDS((ROWS, 128), BF)], flops=2 * 10**9
     )
-    heads_cat, w_out = exchange(
-        "heads_out",
-        2,
-        heads_out_plan,
-        [heads_out, w_output] + got_out,
-        [SDS((CHUNK, 512), BF), SDS((D, 512), BF)],
-    )
-    attn_term = contract_cols(heads_cat, w_out).astype(BF)
-    attn_terms, grad_full = exchange(
-        "out_sum",
-        3,
-        out_sum_plan,
-        [attn_term, output_grad],
-        [SDS((4, SUB, D), BF), SDS((CHUNK, D), BF)],
-    )
-    in_mine = part(full_in, me.y * SUB, SUB, 0).astype(F32)
-    resid = in_mine + jnp.sum(attn_terms.astype(F32), axis=0)
-    scale_two = lax.rsqrt(jnp.mean(resid * resid, axis=1, keepdims=True) + EPS)
-    ffn_mine = (resid * scale_two * ffn_gain_all).astype(BF)
+    heads_cat, w_out, resid, scale_two, ffn_mine = middle(
+        heads_out, in_mine, ffn_gain_all, w_output, got_out
+    )
     (
         out_mine,
         resid_back,
@@ -1371,8 +1297,9 @@
         down_came,
         gate_own,
         gate_came,
+        _,
     ) = ffn(
-        ffn_mine, grad_full, resid, scale_two, ffn_gain_all, w_out, w_gate, w_up, w_down, whole
+        ffn_mine, grad_full, resid, scale_two, ffn_gain_all, w_out, w_gate, w_up, w_down, pieces
     )
 
     query_back, kv_back = vmem_call(
@@ -1400,9 +1327,9 @@
             w_attn,
             heads_cat,
             out_mine,
-            part(full_in, me.y * SUB, SUB, 0),
+            in_mine,
             resid_back,
-            part(scale_one, me.y * SUB, SUB, 0),
+            scale_mine,
             attn_gain[None, :],
             ffn_gain_part,
         ],

time: 534 us -> 432 us (0.81)
  Pallas kernels: 472 us -> 377 us
  other arithmetic: 12.9 us -> 1.28 us
  waiting for transfers between devices: 0.01 us -> 10.8 us
  local copies, waits for them, and re-layouts: 33.3 us -> 26.4 us
    pallas_call x5 -> x3, Pallas kernels: 232 us -> 135 us  [the longest x1 66.3 us: front(): pl.pallas_call(front_body, name='front', out_shape=outs, in_specs=[vm] *...]
    ppermute x1, waiting for transfers between devices: 0.01 us -> 9.23 us  [x_permute(): lax.ppermute(value, ('narrow', 'wide'), [(i, i ^ 9) for i in range(16)])]
    ppermute x0 -> x3, starting transfers between devices: none -> 5.37 us  [z_permute(): return lax.ppermute(value, 'tok', [(i, (i + 2 * d) % 8) for i in range(8)])]
    unnamed x95 -> x67, local copies, waits for them, and re-layouts: 15.8 us -> 18.8 us
  transfers between devices with their start and end apart: 3 -> 6, of which waited for: 0 -> 2; matrix products, arithmetic and copies ran while one was open for 4% -> 0% of each run, Pallas kernels for 27% -> 24%
where the time goes in v4:
time: 432 us; the launch traced here: 425 us
  Pallas kernels  377 us (87%)
  local copies, waits for them, and re-layouts  26.4 us (6%)
  waiting for transfers between devices  10.8 us (2%)
  starting transfers between devices  8.55 us (2%)
    pallas_call x1, Pallas kernels, ffn(): pl.pallas_call(ffn_body, name='ffn', out_shape=[SDS((SUB, D), BF), SDS((S...  138 us
    pallas_call x1, Pallas kernels, back(): pl.pallas_call(back_body, name='back', out_shape=outs, in_specs=[vm] * le...  91.4 us
    pallas_call x1, Pallas kernels, front(): pl.pallas_call(front_body, name='front', out_shape=outs, in_specs=[vm] *...  66.3 us
    pallas_call x1, Pallas kernels, weights_over_x(): pl.pallas_call(weights_body, name='weights', out_shape=SDS((3, 3, 128, 10...  38.8 us
    pallas_call x1, Pallas kernels, middle(): pl.pallas_call(middle_body, name='middle', out_shape=outs, in_specs=[vm]...  30 us
    unnamed x67, local copies, waits for them, and re-layouts  18.8 us
    pallas_call x2, Pallas kernels, vmem_call(): pl.pallas_call(body, name=name, out_shape=outs, in_specs=[pl.BlockSpec(me...  12.4 us
    ppermute x1, waiting for transfers between devices, x_permute(): lax.ppermute(value, ('narrow', 'wide'), [(i, i ^ 9) for i in range(16)])  9.23 us
  transfers between devices with their start and end apart: 6, of which 2 were waited for; matrix products, arithmetic and copies ran while one was open for 0% of the time, Pallas kernels for 24%

profile of v4, /device:TPU:0, one launch (start us, length us, event | category | flops | bytes accessed | tf_op | source)
XLA Modules:
  0.0 425.1 jit_solution(15062491641038151449)
XLA Ops:
  0.7 1.0 dynamic-slice_bitcast_fusion.2
  1.6 1.1 dynamic-slice_bitcast_fusion
  2.7 1.0 pad_maximum_fusion.pieces
  3.7 38.8 %weights.1.piece0 = bf16[3,3,128,1024]{3,2,1,0:T(8,128)(2,1)} custom-call(bf16[3,128,1024]{2,1,0:T(8,128)(2,1)} %pad_maximum_fusion.pieces), custom_call_target="tpu_custom_call" | custom-call | tf_op jit(solution)/shard_map/weights/pallas_call | solution.py:644
  42.5 4.1 collective-permute-start.5
  46.6 1.3 collective-permute-start.3
  48.1 1.2 constant_dynamic-slice_fusion.4
  50.0 66.3 %front.1 = (bf16[1536,128]{1,0:T(8,128)(2,1)S(1)}, bf16[1536,128]{1,0:T(8,128)(2,1)S(1)}, bf16[2048,768]{1,0:T(8,128)(2,1)S(1)}, bf16[384,2048]{1,0:T(8,128)(2,1...) custom-call(f32[8,128]{1,0:T(8,128)S(1)} %broadcast_in_dim.4.gain_ro, ...), custom_call_target="tpu_custom_call" | custom-call | flops 2000000000 | bytes 8388608 | tf_op jit(solution)/shard_map/front/pallas_call | solution.py:773
  116.3 1.7 copy-done.14
  118.0 1.1 copy-done.15
  119.2 1.1 copy-done.16
  120.9 2.0 collective-permute-start.2
  123.6 9.2 %collective-permute-done.2.half3 = bf16[1024,128]{1,0:T(8,128)(2,1)S(1)} collective-permute-done((bf16[1024,128]{1,0:T(8,128)(2,1)S(1)}, bf16[1024,128]{1,0:T(8,128)(2,1)S(1)}, u32[]{:S(2)}, u32[]{:S(2)}) %collective-permute-start.2) | collective-permute-done | bytes 262176 | tf_op jit(solution)/shard_map/ppermute | solution.py:575
  133.4 4.7 %attend.1.heads = bf16[1536,128]{1,0:T(8,128)(2,1)S(1)} custom-call(s32[1,2]{1,0:T(1,128)S(1)} %copy-done.6, bf16[1536,128]{1,0:T(8,128)(2,1)S(1)} %get-tuple-element.49.q_ref, bf16[1536,128]{1,0:T(8,128)(2,1)S(1)} %get-tuple-element.50.kv_ref), custom_call_target="tpu_custom_call" | custom-call | flops 2000000000 | bytes 1048576 | tf_op jit(solution)/shard_map/attend/pallas_call | solution.py:164
  138.1 1.6 collective-permute-done.half1
  139.7 30.0 %middle.1 = (bf16[384,512]{1,0:T(8,128)(2,1)S(1)}, bf16[2048,512]{1,0:T(8,128)(2,1)S(1)}, f32[96,2048]{1,0:T(8,128)S(1)}, f32[96,1]{1,0:T(8,128)S(1)}, bf16[96,2048]{1,0:T(8,128)(2,1)S(1)}) custom-call(bf16[1536,128]{1,0:T(8,128)(2,1)S(1)} %attend.1.heads, bf16[96,2048]{1,0:T(8,128)(2,1)S(1)} %get-tuple-element.51.in_mine, ...), custom_call_target="tpu_custom_call" | custom-call | flops 1000000000 | bytes 8388608 | tf_op jit(solution)/shard_map/middle/pallas_call | solution.py:867
  169.7 1.3 copy-done.9
  174.1 137.7 %ffn.1 = (bf16[96,2048]{1,0:T(8,128)(2,1)}, f32[96,2048]{1,0:T(8,128)}, f32[1,2048]{1,0:T(1,128)}, bf16[384,2048]{1,0:T(8,128)(2,1)}, bf16[1536,128]{1,0:T(8,128...) custom-call(bf16[96,2048]{1,0:T(8,128)(2,1)} %copy-done.13, ...), custom_call_target="tpu_custom_call" | custom-call | flops 25999998976 | bytes 41943040 | tf_op jit(solution)/shard_map/ffn/pallas_call | solution.py:1177
  311.8 1.0 copy-done.21
  312.8 7.7 %attend_back.1 = (bf16[1536,128]{1,0:T(8,128)(2,1)S(1)}, bf16[1536,128]{1,0:T(8,128)(2,1)S(1)}) custom-call(s32[1,2]{1,0:T(1,128)S(1)} %copy-done.6, bf16[1536,128]{1,0:T(8,128)(2,1)S(1)} %get-tuple-element.49.q_ref, bf16[1536,128]{1,0:T(8,128)(2,1)S(1)} %get-tuple-element.50.kv_ref, bf16[1536,128]{1,0:T(8,128)(2,1)S(1)} %copy-done.21, ...), custom_call_target="tpu_custom_call" | custom-call | flops 5000000000 | bytes 1048576 | tf_op jit(solution)/shard_map/attend_back/pallas_call | solution.py:164
  322.0 91.4 %back.1 = (bf16[1536,128]{1,0:T(8,128)(2,1)}, bf16[1536,128]{1,0:T(8,128)(2,1)}, f32[256,128]{1,0:T(8,128)}, f32[4,32,128]{2,1,0:T(8,128)}, f32[256,128]{1,0:T(8...) custom-call(bf16[1536,128]{1,0:T(8,128)(2,1)} %copy-done.19, ...), custom_call_target="tpu_custom_call" | custom-call | flops 10000000000 | bytes 31457280 | tf_op jit(solution)/shard_map/back/pallas_call | solution.py:498
  414.9 1.0 reshape.43
  417.5 1.8 copy.34
  419.3 1.8 copy.35
  (79 shorter events, 13.8 us)
Async XLA Ops:
  2.7 45.2 %copy-start.6 = (s32[1,2]{1,0:T(1,128)S(1)}, s32[1,2]{1,0:T(1,128)}, u32[]{:S(2)}) copy-start(s32[1,2]{1,0:T(1,128)} %len_ref.3) | copy-start | bytes 28
  2.7 45.2 %copy-start = (bf16[2048,128]{1,0:T(8,128)(2,1)S(1)}, bf16[2048,128]{1,0:T(8,128)(2,1)}, u32[]{:S(2)}) copy-start(bf16[2048,128]{1,0:T(8,128)(2,1)} %w_out.1) | copy-start | bytes 1572868
  3.7 45.5 %copy-start.25 = (bf16[2048,256]{1,0:T(8,128)(2,1)S(1)}, bf16[2048,256]{1,0:T(8,128)(2,1)}, u32[]{:S(2)}) copy-start(bf16[2048,256]{1,0:T(8,128)(2,1)} %param.19) | copy-start | bytes 3145732
  3.7 45.5 %copy-start.26 = (bf16[2048,256]{1,0:T(8,128)(2,1)S(1)}, bf16[2048,256]{1,0:T(8,128)(2,1)}, u32[]{:S(2)}) copy-start(bf16[2048,256]{1,0:T(8,128)(2,1)} %param.18) | copy-start | bytes 3145732
  42.5 131.5 %collective-permute-start.5 = (bf16[3,3,128,1024]{3,2,1,0:T(8,128)(2,1)}, bf16[3,3,128,1024]{3,2,1,0:T(8,128)(2,1)}, u32[]{:S(2)}, u32[]{:S(2)}) collective-permute-start(bf16[3,3,128,1024]{3,2,1,0:T(8,128)(2,1)} %weights.1.piece0), channel_id=1, source_target_pairs={{0,96},{16,112},{32,0},{48,16},{64,32},{80,48},{96,64},{112,80},{1... | collective-permute-start | bytes 7077896 | tf_op jit(solution)/shard_map/ppermute | solution.py:579
  46.6 127.4 %collective-permute-start.4 = (bf16[3,3,128,1024]{3,2,1,0:T(8,128)(2,1)}, bf16[3,3,128,1024]{3,2,1,0:T(8,128)(2,1)}, u32[]{:S(2)}, u32[]{:S(2)}) collective-permute-start(bf16[3,3,128,1024]{3,2,1,0:T(8,128)(2,1)} %weights.1.piece0), channel_id=1, source_target_pairs={{0,64},{16,80},{32,96},{48,112},{64,0},{80,16},{96,32},{112,48},{1... | collective-permute-start | bytes 7077896 | tf_op jit(solution)/shard_map/ppermute | solution.py:579
  46.6 127.4 %collective-permute-start.3 = (bf16[3,3,128,1024]{3,2,1,0:T(8,128)(2,1)}, bf16[3,3,128,1024]{3,2,1,0:T(8,128)(2,1)}, u32[]{:S(2)}, u32[]{:S(2)}) collective-permute-start(bf16[3,3,128,1024]{3,2,1,0:T(8,128)(2,1)} %weights.1.piece0), channel_id=1, source_target_pairs={{0,32},{16,48},{32,64},{48,80},{64,96},{80,112},{96,0},{112,16},{1... | collective-permute-start | bytes 7077896 | tf_op jit(solution)/shard_map/ppermute | solution.py:579
  48.0 1.9 copy-start.29
  48.0 1.9 copy-start.2
  48.0 1.9 copy-start.3
  48.1 1.9 copy-start.4
  48.1 1.9 copy-start.5
  120.9 18.8 %copy-start.11 = (bf16[96,2048]{1,0:T(8,128)(2,1)}, bf16[96,2048]{1,0:T(8,128)(2,1)S(1)}, u32[]{:S(2)}) copy-start(bf16[96,2048]{1,0:T(8,128)(2,1)S(1)} %get-tuple-element.51.in_mine) | copy-start | bytes 1179652
  120.9 11.9 %collective-permute-start.2 = (bf16[1024,128]{1,0:T(8,128)(2,1)S(1)}, bf16[1024,128]{1,0:T(8,128)(2,1)S(1)}, u32[]{:S(2)}, u32[]{:S(2)}) collective-permute-start(bf16[1024,128]{1,0:T(8,128)(2,1)S(1)} %constant_dynamic-slice_fusion.1), channel_id=1, source_target_pairs={{0,9},{1,8},{2,11},{3,10},{4,13},{5,12},{6,15},{7,14},{8,1},{9,0},... | collective-permute-start | bytes 786440 | tf_op jit(solution)/shard_map/ppermute | solution.py:575
  122.9 15.2 %collective-permute-start.1 = (bf16[1024,128]{1,0:T(8,128)(2,1)S(1)}, bf16[1024,128]{1,0:T(8,128)(2,1)S(1)}, u32[]{:S(2)}, u32[]{:S(2)}) collective-permute-start(bf16[1024,128]{1,0:T(8,128)(2,1)S(1)} %constant_dynamic-slice_fusion.1), channel_id=1, source_target_pairs={{0,1},{1,0},{2,3},{3,2},{4,5},{5,4},{6,7},{7,6},{8,9},{9,8},{10,11... | collective-permute-start | bytes 786440 | tf_op jit(solution)/shard_map/ppermute | solution.py:574
  132.8 6.9 %collective-permute-start = (bf16[1024,128]{1,0:T(8,128)(2,1)S(1)}, bf16[1024,128]{1,0:T(8,128)(2,1)S(1)}, u32[]{:S(2)}, u32[]{:S(2)}) collective-permute-start(bf16[1024,128]{1,0:T(8,128)(2,1)S(1)} %constant_dynamic-slice_fusion.1), channel_id=1, source_target_pairs={{0,8},{8,0},{1,9},{9,1},{2,10},{10,2},{3,11},{11,3},{4,12},{12,4},... | collective-permute-start | bytes 786440 | tf_op jit(solution)/shard_map/ppermute | solution.py:572
  133.3 6.3 %copy-start.1 = (f32[1,2048]{1,0:T(1,128)}, f32[1,2048]{1,0:T(1,128)S(1)}, u32[]{:S(2)}) copy-start(f32[1,2048]{1,0:T(1,128)S(1)} %slice_bitcast_fusion.gain.gain_ref) | copy-start | bytes 24580
  174.0 137.8 %copy-start.7 = (f32[1024,128]{1,0:T(8,128)S(1)}, f32[1024,128]{1,0:T(8,128)}, u32[]{:S(2)}) copy-start(f32[1024,128]{1,0:T(8,128)} %constant.77.sin_ref) | copy-start | bytes 1572868
  174.0 137.7 %copy-start.8 = (f32[1024,128]{1,0:T(8,128)S(1)}, f32[1024,128]{1,0:T(8,128)}, u32[]{:S(2)}) copy-start(f32[1024,128]{1,0:T(8,128)} %constant.76.cos_ref) | copy-start | bytes 1572868
  413.5 7.6 %copy-start.28 = (f32[256,128]{1,0:T(8,128)S(1)}, f32[256,128]{1,0:T(8,128)}, u32[]{:S(2)}) copy-start(f32[256,128]{1,0:T(8,128)} %get-tuple-element.109) | copy-start | bytes 393220
  413.5 8.3 %copy-start.27 = (f32[256,128]{1,0:T(8,128)S(1)}, f32[256,128]{1,0:T(8,128)}, u32[]{:S(2)}) copy-start(f32[256,128]{1,0:T(8,128)} %get-tuple-element.112) | copy-start | bytes 393220
  413.5 8.9 %copy-start.24 = (f32[8,16,1024]{2,1,0:T(8,128)S(1)}, f32[8,16,1024]{2,1,0:T(8,128)}, u32[]{:S(2)}) copy-start(f32[8,16,1024]{2,1,0:T(8,128)} %get-tuple-element.114) | copy-start | bytes 1572868
  413.5 9.7 %copy-start.23 = (f32[8,16,1024]{2,1,0:T(8,128)S(1)}, f32[8,16,1024]{2,1,0:T(8,128)}, u32[]{:S(2)}) copy-start(f32[8,16,1024]{2,1,0:T(8,128)} %get-tuple-element.115) | copy-start | bytes 1572868
  417.5 6.5 %copy-start.22 = (f32[8,16,1024]{2,1,0:T(8,128)S(1)}, f32[8,16,1024]{2,1,0:T(8,128)}, u32[]{:S(2)}) copy-start(f32[8,16,1024]{2,1,0:T(8,128)} %get-tuple-element.116) | copy-start | bytes 1572868
  (12 other events, 11.5 us)

commit v5 on v4

--- a/solution.py
+++ b/solution.py
@@ -292,9 +292,14 @@
     load_right.wait()
     up_pair = PairSum(me, left_buf, right_buf, up_terms, up_core, core_send, core_recv)
     up_pair.multiply(0, 8)
-    load_left = pltpu.make_async_copy(normed_in, left_buf, local_sem.at[0])
-    load_right = pltpu.make_async_copy(mix_in, right_buf, local_sem.at[1])
+    load_left = pltpu.make_async_copy(mix_in, left_buf, local_sem.at[0])
     load_left.start()
+    load_left.wait()
+    for z in range(4):
+        block = contract_rows(left_buf[:, z * 512 : z * 512 + 512], heads_cat[...])
+        o_terms[z] = block.astype(BF).reshape(2, 256, 512)
+    o_pair = wire.send(SIBLING, o_terms.at[:, 1 - me.core], o_core)
+    load_right = pltpu.make_async_copy(normed_in, right_buf, local_sem.at[1])
     load_right.start()
     up_pair.add(0, 8)
     up_moves = [
@@ -314,23 +319,28 @@
         for d in (1, 2, 3)
     ]
 
-    load_left.wait()
+    def add_core(copy, terms, came):
+        copy.wait_recv()
+        terms[:, me.core] = (terms[:, me.core].astype(F32) + came[...].astype(F32)).astype(BF)
+
+    add_core(o_pair, o_terms, o_core)
+    o_moves = [
+        wire.send(XOFF[k], o_terms.at[:, me.core, :, k * 128 : k * 128 + 128], o_x.at[k - 1])
+        for k in (1, 2, 3)
+    ]
+
     load_right.wait()
     for z in range(4):
-        block = contract_rows(left_buf[:, z * 512 : z * 512 + 512], cat_back[:, 0:512])
+        block = contract_rows(right_buf[:, z * 512 : z * 512 + 512], cat_back[:, 0:512])
         q_terms[z] = block.astype(BF).reshape(2, 256, 512)
     q_pair = wire.send(SIBLING, q_terms.at[:, 1 - me.core], q_core)
     for z in range(4):
-        left = left_buf[:, z * 512 : z * 512 + 512]
+        left = right_buf[:, z * 512 : z * 512 + 512]
         block = contract_rows(left, cat_back[:, 512:768]) + contract_rows(
             left, cat_back[:, 768:1024]
         )
         k_terms[z] = block.astype(BF).reshape(2, 4, 2, 32, 256)
     k_pair = wire.send(SIBLING, k_terms.at[:, 1 - me.core], k_core)
-    for z in range(4):
-        block = contract_rows(right_buf[:, z * 512 : z * 512 + 512], heads_cat[...])
-        o_terms[z] = block.astype(BF).reshape(2, 256, 512)
-    o_pair = wire.send(SIBLING, o_terms.at[:, 1 - me.core], o_core)
 
     def fold(own, came, buf, out, sem):
         size = buf.shape[1]
@@ -361,10 +371,6 @@
         wire.send(ZOFF[d], down_sum.at[:, :, (me.z + d) % 4], down_z.at[d - 1]) for d in (1, 2, 3)
     ]
 
-    def add_core(copy, terms, came):
-        copy.wait_recv()
-        terms[:, me.core] = (terms[:, me.core].astype(F32) + came[...].astype(F32)).astype(BF)
-
     def kv_block(k):
         e, dxl = XOFF[k][4], XOFF[k][2]
         return k_terms.at[:, me.core, :, (me.xh + e) % 2, :, dxl * 128 : dxl * 128 + 128]
@@ -374,11 +380,6 @@
     add_core(q_pair, q_terms, q_core)
     q_moves = [
         wire.send(XOFF[k], q_terms.at[:, me.core, :, k * 128 : k * 128 + 128], q_x.at[k - 1])
-        for k in (1, 2, 3)
-    ]
-    add_core(o_pair, o_terms, o_core)
-    o_moves = [
-        wire.send(XOFF[k], o_terms.at[:, me.core, :, k * 128 : k * 128 + 128], o_x.at[k - 1])
         for k in (1, 2, 3)
     ]
 
@@ -567,14 +568,6 @@
     )
 
 
-def x_permute(value, k):
-    if k == 1:
-        return lax.ppermute(value, "narrow", [(0, 1), (1, 0)])
-    if k == 2:
-        return lax.ppermute(value, "wide", [(i, i ^ 1) for i in range(8)])
-    return lax.ppermute(value, ("narrow", "wide"), [(i, i ^ 9) for i in range(16)])
-
-
 def z_permute(value, d):
     return lax.ppermute(value, "tok", [(i, (i + 2 * d) % 8) for i in range(8)])
 
@@ -636,18 +629,25 @@
 def weights_body(pieces, came, send_sem, recv_sem):
     me = whereami()
     wire = Wire(me, send_sem, recv_sem)
-    meet(me, XOFF[1:])
-    finish([wire.send(XOFF[k], pieces, came.at[k - 1]) for k in (1, 2, 3)])
+    meet(me, [XOFF[1], XOFF[3]])
+    first = [wire.send(XOFF[k], pieces, came.at[:, k - 1]) for k in (1, 3)]
+    first[0].wait_recv()
+    second = [wire.send(XOFF[3], came.at[0, 0], came.at[0, 1])]
+    first[1].wait_recv()
+    second.append(wire.send(XOFF[1], came.at[1, 2], came.at[1, 1]))
+    for copy in first:
+        copy.wait_send()
+    finish(second)
 
 
 def weights_over_x(pieces):
     return pl.pallas_call(
         weights_body,
         name="weights",
-        out_shape=SDS((3, 3, 128, 1024), BF),
+        out_shape=SDS((2, 3, 3, 64, 1024), BF),
         in_specs=[pl.BlockSpec(memory_space=pl.ANY)],
         out_specs=pl.BlockSpec(memory_space=pl.ANY),
-        scratch_shapes=[pltpu.SemaphoreType.DMA((3,)), pltpu.SemaphoreType.DMA((3,))],
+        scratch_shapes=[pltpu.SemaphoreType.DMA((4,)), pltpu.SemaphoreType.DMA((4,))],
         compiler_params=pltpu.CompilerParams(collective_id=13, has_side_effects=True),
     )(pieces)
 
@@ -665,6 +665,7 @@
     w_q,
     w_kv,
     out_grad,
+    w_o,
     q,
     kv,
     w_attn,
@@ -673,6 +674,7 @@
     scale_mine,
     gains,
     grad_full,
+    w_cat,
     full,
     lin,
     scales,
@@ -691,37 +693,50 @@
 
     take(w_q, w_attn.at[:, 0:128])
     take(w_kv, w_attn.at[:, 512:640])
+    take(w_o, w_cat.at[:, 0:128])
     take(hidden.at[chunk, :], full.at[:, lanes(me.block)])
     take(out_grad.at[chunk, :], grad_full.at[:, lanes(me.wide)])
     gains[me.block] = gain_row[...]
     meet(me, PLANE[1:] + [SIBLING])
 
+    def chunk_of(off):
+        return rows(me.at(off).chunk * CHUNK, CHUNK)
+
+    def spread(src, dst, column):
+        return [wire.send(XOFF[k], src.at[chunk_of(XOFF[k]), :], dst.at[:, column(k)]) for k in (1, 2, 3)]
+
+    enter = spread(hidden, full, lambda k: lanes(me.block))
     half = rows(me.core * 1024, 1024)
     blocks = [w_attn.at[half, k * 128 : k * 128 + 128] for k in (1, 2, 3)]
     over_x = [wire.send(XOFF[k], w_q.at[half, :], blocks[k - 1]) for k in (1, 2, 3)]
     blocks.append(w_attn.at[half, 640:768])
     over_x.append(wire.send(XOFF[1], w_kv.at[half, :], blocks[3]))
-
-    def chunk_of(off):
-        return rows(me.at(off).chunk * CHUNK, CHUNK)
-
-    enter = [
-        wire.send(off, hidden.at[chunk_of(off), :], full.at[:, lanes(me.block)])
-        for off in PLANE[1:]
-    ]
     others = [wire.send(off, gain_row, gains.at[me.block]) for off in PLANE[1:]]
-    others += [
-        wire.send(off, out_grad.at[chunk_of(off), :], grad_full.at[:, lanes(off[2] * 8 + me.wide)])
-        for off in PLANE[1:]
-    ]
+    grads = spread(out_grad, grad_full, lambda k: lanes(XOFF[k][2] * 8 + me.wide))
+    out_blocks = [w_cat.at[half, k * 128 : k * 128 + 128] for k in (1, 2, 3)]
+    out_x = [wire.send(XOFF[k], w_o.at[half, :], out_blocks[k - 1]) for k in (1, 2, 3)]
+
+    def pass_on(ref):
+        out = []
+        for h in range(2):
+            cols = lanes(h * 4 + me.y, 256)
+            out += [wire.send(off, ref.at[:, cols], ref.at[:, cols]) for off in YOFF[1:]]
+        return out
+
+    for copy in near:
+        copy.wait()
+    for copy in enter:
+        copy.wait_recv()
+    over_y = pass_on(full)
     over_core = []
     for copy, block in zip(over_x, blocks):
         copy.wait_recv()
         over_core.append(wire.send(SIBLING, block, block))
-    for copy in enter:
+    for copy in grads:
         copy.wait_recv()
-    for copy in near:
-        copy.wait()
+    others += pass_on(grad_full)
+    for copy in over_y:
+        copy.wait_recv()
     for part_rows in split_rows(4, SUB):
         value = full[part_rows, :].astype(F32)
         scale = lax.rsqrt(jnp.mean(value * value, axis=1, keepdims=True) + EPS)
@@ -747,17 +762,19 @@
         moves.append(wire.send(XOFF[k], lin.at[:, kv_col : kv_col + 128], kv.at[chunk, :]))
     q[chunk, :] = lin[:, 0:128]
     kv[chunk, :] = lin[:, 512:640]
+    for copy, block in zip(out_x, out_blocks):
+        copy.wait_recv()
+        over_core.append(wire.send(SIBLING, block, block))
+        others.append(over_core[-1])
     here = rows(me.y * SUB, SUB)
     in_mine[...] = full[here, :]
     scale_mine[...] = scales[here, :]
-    for copy in over_x + enter:
-        copy.wait_send()
-    for copy in over_core:
+    for copy in over_x + enter + grads + over_y + out_x + over_core[:4]:
         copy.wait_send()
     finish(others + moves)
 
 
-def front(gain_row, attn_gain, cos_here, sin_here, hidden, w_q, w_kv, out_grad):
+def front(gain_row, attn_gain, cos_here, sin_here, hidden, w_q, w_kv, out_grad, w_o):
     vm = pl.BlockSpec(memory_space=pltpu.VMEM)
     hbm = pl.BlockSpec(memory_space=pl.ANY)
     outs = [
@@ -769,38 +786,35 @@
         SDS((SUB, 1), F32),
         SDS((16, 8, 128), F32),
         SDS((CHUNK, D), BF),
+        SDS((D, 512), BF),
     ]
     return pl.pallas_call(
         front_body,
         name="front",
         out_shape=outs,
-        in_specs=[vm] * 4 + [hbm] * 4,
+        in_specs=[vm] * 4 + [hbm] * 5,
         out_specs=[vm] * len(outs),
         scratch_shapes=[
             pltpu.VMEM((CHUNK, D), BF),
             pltpu.VMEM((CHUNK, 768), BF),
             pltpu.VMEM((CHUNK, 1), F32),
-            pltpu.SemaphoreType.DMA((60,)),
-            pltpu.SemaphoreType.DMA((60,)),
-            pltpu.SemaphoreType.DMA((4,)),
+            pltpu.SemaphoreType.DMA((64,)),
+            pltpu.SemaphoreType.DMA((64,)),
+            pltpu.SemaphoreType.DMA((5,)),
         ],
         compiler_params=pltpu.CompilerParams(
             collective_id=0, has_side_effects=True, vmem_limit_bytes=40 * 2**20
         ),
         cost_estimate=pl.CostEstimate(flops=2 * 10**9, bytes_accessed=2**23, transcendentals=0),
-    )(gain_row, attn_gain, cos_here, sin_here, hidden, w_q, w_kv, out_grad)
+    )(gain_row, attn_gain, cos_here, sin_here, hidden, w_q, w_kv, out_grad, w_o)
 
 
 def middle_body(
     heads,
     in_mine,
     gain,
-    w_out,
-    half1,
-    half2,
-    half3,
+    w_cat,
     heads_cat,
-    w_cat,
     resid,
     scale_out,
     ffn_mine,
@@ -808,18 +822,10 @@
     term_recv,
     send_sem,
     recv_sem,
-    local_sem,
 ):
     me = whereami()
     wire = Wire(me, send_sem, recv_sem)
-    half = rows(me.core * 1024, 1024)
-    blocks = [w_cat.at[half, k * 128 : k * 128 + 128] for k in (1, 2, 3)]
-    pairs = [(w_out, w_cat.at[:, 0:128])] + list(zip((half1, half2, half3), blocks))
-    near = []
-    for src, dst in pairs:
-        near.append(pltpu.make_async_copy(src, dst, local_sem.at[len(near)]))
-        near[-1].start()
-    meet(me, XOFF[1:] + YOFF[1:] + [SIBLING])
+    meet(me, XOFF[1:] + YOFF[1:])
     moves = [
         wire.send(
             XOFF[k],
@@ -828,10 +834,7 @@
         )
         for k in (1, 2, 3)
     ]
-    moves += [wire.send(SIBLING, src, dst) for src, dst in pairs[1:]]
     heads_cat[:, 0:128] = heads[rows(me.chunk * CHUNK, CHUNK), :]
-    for copy in near:
-        copy.wait()
     finish(moves)
     sums = []
     for h in range(2):
@@ -854,34 +857,26 @@
     ffn_mine[...] = (value * scale * gain[...]).astype(BF)
 
 
-def middle(heads, in_mine, gain, w_out, halves):
+def middle(heads, in_mine, gain, w_cat):
     vm = pl.BlockSpec(memory_space=pltpu.VMEM)
-    hbm = pl.BlockSpec(memory_space=pl.ANY)
-    outs = [
-        SDS((CHUNK, 512), BF),
-        SDS((D, 512), BF),
-        SDS((SUB, D), F32),
-        SDS((SUB, 1), F32),
-        SDS((SUB, D), BF),
-    ]
+    outs = [SDS((CHUNK, 512), BF), SDS((SUB, D), F32), SDS((SUB, 1), F32), SDS((SUB, D), BF)]
     return pl.pallas_call(
         middle_body,
         name="middle",
         out_shape=outs,
-        in_specs=[vm] * 3 + [hbm] * 4,
+        in_specs=[vm] * 4,
         out_specs=[vm] * len(outs),
         scratch_shapes=[
             pltpu.VMEM((CHUNK, D), BF),
             pltpu.VMEM((3, SUB, D), BF),
-            pltpu.SemaphoreType.DMA((12,)),
-            pltpu.SemaphoreType.DMA((12,)),
-            pltpu.SemaphoreType.DMA((4,)),
+            pltpu.SemaphoreType.DMA((9,)),
+            pltpu.SemaphoreType.DMA((9,)),
         ],
         compiler_params=pltpu.CompilerParams(
             collective_id=1, has_side_effects=True, vmem_limit_bytes=32 * 2**20
         ),
         cost_estimate=pl.CostEstimate(flops=10**9, bytes_accessed=2**23, transcendentals=0),
-    )(heads, in_mine, gain, w_out, *halves)
+    )(heads, in_mine, gain, w_cat)
 
 
 class PairSum:
@@ -939,7 +934,8 @@
     own_down,
     piece0,
     piece1,
-    piece2,
+    piece2_first,
+    piece2_second,
     piece3,
     out_mine,
     resid_back,
@@ -983,7 +979,8 @@
     half = [lanes(me.xl, 1024), lanes(1 - me.xl, 1024)]
     here = rows(me.y * SUB, SUB)
 
-    pieces = (piece0, piece1, piece2, piece3)
+    pieces = (piece0, piece1, None, piece3)
+    opposite = (piece2_first, piece2_second)
 
     def tile_copies(e, q, slot):
         copies, groups = [], []
@@ -997,21 +994,31 @@
             k = e * 2 + dxl
             for j, (own, tile) in enumerate(((own_gate, gate_tile), (own_up, up_tile))):
                 if k == 0:
-                    copies.append(copy(own.at[:, :, :, cols], tile.at[slot, dxl]))
+                    copies.append(copy(own.at[:, :, :, :, cols], tile.at[slot, dxl]))
                     continue
                 for d, piece in enumerate(pieces):
                     spot = tile.at[slot, dxl, (me.z - d + 4) % 4, me.core]
-                    copies.append(copy(piece.at[k - 1, j, :, cols], spot))
+                    if piece is not None:
+                        copies.append(copy(piece.at[:, k - 1, j, :, cols], spot))
+                        continue
+                    for h in range(2):
+                        copies.append(copy(opposite[h].at[k - 1, j, :, cols], spot.at[h]))
                 spot = tile.at[slot, dxl, :, 1 - me.core]
-                copies.append(copy(other_core.at[:, k - 1, j, :, cols], spot))
+                copies.append(copy(other_core.at[:, :, k - 1, j, :, cols], spot))
             here = slice(dxl * 1024, dxl * 1024 + 1024)
             if k == 0:
-                copies.append(copy(own_down.at[q], down_tile.at[slot, :, :, here]))
+                copies.append(copy(own_down.at[q], down_tile.at[slot, :, :, :, here]))
                 continue
-            spot = down_tile.at[slot, 1 - me.core, :, here]
-            copies.append(copy(other_core.at[q, k - 1, 2], spot))
-            spot = down_tile.at[slot, me.core, :, here]
-            groups.append([copy(piece.at[k - 1, 2], spot) for piece in pieces])
+            spot = down_tile.at[slot, 1 - me.core, :, :, here]
+            copies.append(copy(other_core.at[q, :, k - 1, 2], spot))
+            for h in range(2):
+                spot = down_tile.at[slot, me.core, h, :, here]
+                groups.append(
+                    [
+                        copy(opposite[h].at[k - 1, 2] if p is None else p.at[h, k - 1, 2], spot)
+                        for p in pieces
+                    ]
+                )
         return copies, groups
 
     def fetch(e, q, slot):
@@ -1031,13 +1038,16 @@
     for h in range(2):
         turned[:, h * 1024 : h * 1024 + 1024] = mine_ref[:, half[h]]
     gathers = [wire.send(off, turned, ffn_in.at[here, :]) for off in YOFF[1:]]
-    shares = [
-        [
-            wire.send(SIBLING, piece.at[k], other_core.at[(me.z - d + 4) % 4, k])
-            for d, piece in enumerate(pieces)
-        ]
-        for k in range(3)
-    ]
+    shares = []
+    for k in range(3):
+        shares.append([])
+        for d, piece in enumerate(pieces):
+            spot = other_core.at[(me.z - d + 4) % 4, :, k]
+            if piece is not None:
+                shares[k].append(wire.send(SIBLING, piece.at[:, k], spot))
+                continue
+            for h in range(2):
+                shares[k].append(wire.send(SIBLING, opposite[h].at[k], spot.at[h]))
     ffn_in[here, :] = turned[...]
     down_acc[...] = jnp.zeros(down_acc.shape, F32)
     ffn_acc[...] = jnp.zeros(ffn_acc.shape, F32)
@@ -1096,15 +1106,11 @@
         for d in (1, 2, 3)
     ]
     down_sum.multiply(4, 8)
-    down_send[...] = down_acc[...].astype(BF)
-    down_moves = [
-        wire.send(YOFF[d], down_send.at[rows(me.at(YOFF[d]).y * SUB, SUB), :], down_recv.at[d - 1])
-        for d in (1, 2, 3)
-    ]
 
     def down_block(k):
         e, dxl = XOFF[k][4], XOFF[k][2]
-        return down_terms.at[e * 4 : e * 4 + 4, :, :, me.core, :, dxl * 1024 : dxl * 1024 + 1024]
+        here = slice(dxl * 1024, dxl * 1024 + 1024)
+        return down_terms.at[e * 4 : e * 4 + 4, :, :, me.core, :, here]
 
     down_sum.add(0, 4)
     x_moves = [wire.send(XOFF[1], down_block(1), down_came.at[0])]
@@ -1112,7 +1118,20 @@
     x_moves += [wire.send(XOFF[k], down_block(k), down_came.at[k - 1]) for k in (2, 3)]
     near = [pltpu.make_async_copy(down_block(0), down_own, local_sem.at[0])]
     near[0].start()
+
     pl.semaphore_signal(ack, inc=1, device_id=me.at(SIBLING).device(), device_id_type=MESH)
+    pl.semaphore_wait(ack, 1)
+    gate_sum.multiply(0, 8)
+    gate_sum.add(0, 8)
+
+    def gate_block(z):
+        return gate_terms.at[:, :, z, me.core]
+
+    z_moves = [
+        wire.send(ZOFF[d], gate_block((me.z + d) % 4), gate_came.at[d - 1]) for d in (1, 2, 3)
+    ]
+    near.append(pltpu.make_async_copy(gate_block(me.z), gate_own, local_sem.at[1]))
+    near[1].start()
 
     finish(ffn_moves)
 
@@ -1140,22 +1159,11 @@
     mix_full[here, :] = mix_mine[...]
     mix_moves = [wire.send(off, mix_mine, mix_full.at[here, :]) for off in YOFF[1:]]
 
-    pl.semaphore_wait(ack, 1)
-    gate_sum.multiply(0, 8)
-    finish(down_moves)
-    for h in range(2):
-        out_mine[:, half[h]] = (resid_ref[:, half[h]] + summed(down_send, down_recv, h)).astype(BF)
-    gate_sum.add(0, 8)
-
-    def gate_block(z):
-        return gate_terms.at[:, :, z, me.core]
-
-    z_moves = [
-        wire.send(ZOFF[d], gate_block((me.z + d) % 4), gate_came.at[d - 1]) for d in (1, 2, 3)
+    down_send[...] = down_acc[...].astype(BF)
+    down_moves = [
+        wire.send(YOFF[d], down_send.at[rows(me.at(YOFF[d]).y * SUB, SUB), :], down_recv.at[d - 1])
+        for d in (1, 2, 3)
     ]
-    near.append(pltpu.make_async_copy(gate_block(me.z), gate_own, local_sem.at[1]))
-    near[1].start()
-
     finish(mix_moves)
     back_cat[...] = multiply(mix_full[...], w_out_ref[...]).astype(BF)
     spot = rows(me.chunk * CHUNK, CHUNK)
@@ -1164,6 +1172,9 @@
         for k in (1, 2, 3)
     ]
     heads_back[spot, :] = back_cat[:, 0:128]
+    finish(down_moves)
+    for h in range(2):
+        out_mine[:, half[h]] = (resid_ref[:, half[h]] + summed(down_send, down_recv, h)).astype(BF)
     finish(head_moves + x_moves + z_moves)
     for copy in near:
         copy.wait()
@@ -1189,17 +1200,17 @@
             SDS((3, 4, 2, 4, 16, 1024), BF),
             SDS((8, 2, 16, 2048), BF),
             SDS((3, 8, 2, 16, 2048), BF),
-            SDS((4, 3, 3, 128, 1024), BF),
+            SDS((4, 2, 3, 3, 64, 1024), BF),
         ],
-        in_specs=[vm] * 6 + [hbm] * 7,
+        in_specs=[vm] * 6 + [hbm] * 8,
         out_specs=[vm] * 7 + [hbm] * 5,
         scratch_shapes=[
             pltpu.VMEM((SUB, D), BF),
             pltpu.VMEM((CHUNK, D), BF),
             pltpu.VMEM((CHUNK, D), BF),
-            pltpu.VMEM((2, 2, 4, 2, 128, 256), BF),
-            pltpu.VMEM((2, 2, 4, 2, 128, 256), BF),
-            pltpu.VMEM((2, 2, 128, 2048), BF),
+            pltpu.VMEM((2, 2, 4, 2, 2, 64, 256), BF),
+            pltpu.VMEM((2, 2, 4, 2, 2, 64, 256), BF),
+            pltpu.VMEM((2, 2, 2, 64, 2048), BF),
             pltpu.VMEM((CHUNK, D), F32),
             pltpu.VMEM((CHUNK, D), F32),
             pltpu.VMEM((CHUNK, D), BF),
@@ -1215,7 +1226,7 @@
             pltpu.SemaphoreType.DMA((36,)),
             pltpu.SemaphoreType.DMA((2, 8)),
             pltpu.SemaphoreType.DMA((2, 8)),
-            pltpu.SemaphoreType.DMA((2, 24)),
+            pltpu.SemaphoreType.DMA((2, 32)),
             pltpu.SemaphoreType.DMA((2,)),
             pltpu.SemaphoreType.REGULAR,
         ],
@@ -1230,9 +1241,9 @@
         scale_two,
         gain,
         w_out,
-        w_gate.reshape(4, 2, 128, 1024),
-        w_up.reshape(4, 2, 128, 1024),
-        w_down.reshape(4, 2, 128, 1024),
+        w_gate.reshape(4, 2, 2, 64, 1024),
+        w_up.reshape(4, 2, 2, 64, 1024),
+        w_down.reshape(4, 2, 2, 64, 1024),
         *pieces,
     )
 
@@ -1263,9 +1274,9 @@
         [part(w_key, me.y * 64, 64, 1), part(w_value, me.y * 64, 64, 1)], axis=1
     )
     pieces = jnp.stack([part(w, me.tok * 128, 128, 0) for w in (w_gate, w_up, w_down)])
-    pieces = [weights_over_x(pieces)]
-    pieces += [z_permute(pieces[0], d) for d in (1, 2, 3)]
-    queries, kv, w_attn, normed, in_mine, scale_mine, gains, grad_full = front(
+    piece0 = weights_over_x(jnp.moveaxis(pieces.reshape(3, 2, 64, 1024), 1, 0))
+    piece1, piece3 = z_permute(piece0, 1), z_permute(piece0, 3)
+    queries, kv, w_attn, normed, in_mine, scale_mine, gains, grad_full, w_out = front(
         jnp.broadcast_to(ffn_gain[None, :], (8, 128)),
         attn_gain[None, :],
         cos_here,
@@ -1274,17 +1285,15 @@
         w_query,
         w_kv,
         output_grad,
+        w_output,
     )
     ffn_gain_all = gains[:, 0, :].reshape(1, D)
-    half_out = part(w_output, me.core * 1024, 1024, 0)
-    queries, half_out = lax.optimization_barrier((queries, half_out))
-    got_out = [x_permute(half_out, k) for k in (1, 2, 3)]
+    queries, second, first = lax.optimization_barrier((queries, piece1[0], piece3[1]))
+    pieces = [piece0, piece1, z_permute(second, 1), z_permute(first, 3), piece3]
     (heads_out,) = vmem_call(
-        "attend", attend_body, [doc_lengths, queries, kv], [SDS((ROWS, 128), BF)], flops=2 * 10**9
+        "attend", attend_body, [doc_lengths, queries, kv], [SDS((ROWS, 128), BF)], flops=2 * 10**10
     )
-    heads_cat, w_out, resid, scale_two, ffn_mine = middle(
-        heads_out, in_mine, ffn_gain_all, w_output, got_out
-    )
+    heads_cat, resid, scale_two, ffn_mine = middle(heads_out, in_mine, ffn_gain_all, w_out)
     (
         out_mine,
         resid_back,

time: 432 us -> 372 us (0.86)
  Pallas kernels: 377 us -> 328 us
  waiting for transfers between devices: 10.8 us -> 0.01 us
    pallas_call x1, Pallas kernels: 138 us -> 113 us  [ffn(): pl.pallas_call(ffn_body, name='ffn', out_shape=[SDS((SUB, D), BF), SDS((S...]
    pallas_call x1, Pallas kernels: 66.3 us -> 52.2 us  [front(): pl.pallas_call(front_body, name='front', out_shape=outs, in_specs=[vm] *...]
    ppermute x3 -> x0, waiting for transfers between devices: 10.8 us -> none  [the longest x1 9.23 us: x_permute(): lax.ppermute(value, ('narrow', 'wide'), [(i, i ^ 9) for i in range(16)])]
    pallas_call x1, Pallas kernels: 38.8 us -> 31.1 us  [weights_over_x(): pl.pallas_call(weights_body, name='weights', out_shape=SDS((2, 3, 3, 64,...]
    unnamed x67 -> x75, local copies, waits for them, and re-layouts: 18.8 us -> 17.1 us
  transfers between devices with their start and end apart: 6 -> 4, of which waited for: 2 -> 0; matrix products, arithmetic and copies ran while one was open for 0% -> 1% of each run, Pallas kernels for 24% -> 23%
where the time goes in v5:
time: 372 us; the launch traced here: 366 us
  Pallas kernels  328 us (88%)
  local copies, waits for them, and re-layouts  28 us (8%)
  starting transfers between devices  7.91 us (2%)
    pallas_call x1, Pallas kernels, ffn(): pl.pallas_call(ffn_body, name='ffn', out_shape=[SDS((SUB, D), BF), SDS((S...  113 us
    pallas_call x1, Pallas kernels, back(): pl.pallas_call(back_body, name='back', out_shape=outs, in_specs=[vm] * le...  92.5 us
    pallas_call x1, Pallas kernels, front(): pl.pallas_call(front_body, name='front', out_shape=outs, in_specs=[vm] *...  52.2 us
    pallas_call x1, Pallas kernels, weights_over_x(): pl.pallas_call(weights_body, name='weights', out_shape=SDS((2, 3, 3, 64,...  31.1 us
    pallas_call x1, Pallas kernels, middle(): pl.pallas_call(middle_body, name='middle', out_shape=outs, in_specs=[vm]...  25.9 us
    unnamed x75, local copies, waits for them, and re-layouts  17.1 us
    pallas_call x2, Pallas kernels, vmem_call(): pl.pallas_call(body, name=name, out_shape=outs, in_specs=[pl.BlockSpec(me...  12.4 us
    ppermute x4, starting transfers between devices, z_permute(): return lax.ppermute(value, 'tok', [(i, (i + 2 * d) % 8) for i in range(8)])  7.91 us
  transfers between devices with their start and end apart: 4, of which 0 were waited for; matrix products, arithmetic and copies ran while one was open for 1% of the time, Pallas kernels for 23%

profile of v5, /device:TPU:0, one launch (start us, length us, event | category | flops | bytes accessed | tf_op | source)
XLA Modules:
  0.0 366.2 jit_solution(6233263017365899851)
XLA Ops:
  0.7 1.0 constant_dynamic-slice_fusion.3
  1.6 1.1 constant_dynamic-slice_fusion.1
  2.7 1.0 maximum_bitcast_fusion.pieces
  3.7 31.1 %weights.1.piece0 = bf16[2,3,3,64,1024]{4,3,2,1,0:T(8,128)(2,1)} custom-call(bf16[2,3,64,1024]{3,2,1,0:T(8,128)(2,1)} %maximum_bitcast_fusion.pieces), custom_call_target="tpu_custom_call" | custom-call | tf_op jit(solution)/shard_map/weights/pallas_call | solution.py:644
  34.8 4.1 %collective-permute-start.1 = (bf16[2,3,3,64,1024]{4,3,2,1,0:T(8,128)(2,1)}, bf16[2,3,3,64,1024]{4,3,2,1,0:T(8,128)(2,1)S(1)}, u32[]{:S(2)}, u32[]{:S(2)}) collective-permute-start(bf16[2,3,3,64,1024]{4,3,2,1,0:T(8,128)(2,1)} %weights.1.piece0), channel_id=1, source_target_pairs={{0,96},{16,112},{32,0},{48,16},{64,32},{80,48},{96,64},{112,80},{1... | collective-permute-start | bytes 7077896 | tf_op jit(solution)/shard_map/ppermute | solution.py:572
  39.0 1.2 constant_dynamic-slice_fusion.6
  40.2 1.4 constant_dynamic-slice_fusion.4
  42.0 52.2 %front.1 = (bf16[1536,128]{1,0:T(8,128)(2,1)S(1)}, bf16[1536,128]{1,0:T(8,128)(2,1)S(1)}, bf16[2048,768]{1,0:T(8,128)(2,1)S(1)}, bf16[384,2048]{1,0:T(8,128)(2,1...) custom-call(f32[8,128]{1,0:T(8,128)S(1)} %broadcast_in_dim.4.gain_ro, ...), custom_call_target="tpu_custom_call" | custom-call | flops 2000000000 | bytes 8388608 | tf_op jit(solution)/shard_map/front/pallas_call | solution.py:791
  94.2 1.7 copy-done.14
  96.0 1.1 copy-done.17
  97.3 2.2 slice_bitcast_fusion.1
  99.6 3.7 %collective-permute-start.3 = (bf16[3,3,64,1024]{3,2,1,0:T(8,128)(2,1)S(1)}, bf16[3,3,64,1024]{3,2,1,0:T(8,128)(2,1)S(1)}, u32[]{:S(2)}, u32[]{:S(2)}) collective-permute-start(bf16[3,3,64,1024]{3,2,1,0:T(8,128)(2,1)S(1)} %slice_bitcast_fusion), channel_id=1, source_target_pairs={{0,96},{16,112},{32,0},{48,16},{64,32},{80,48},{96,64},{112,80},{1... | collective-permute-start | bytes 3538952 | tf_op jit(solution)/shard_map/ppermute | solution.py:572
  103.3 4.7 %attend.1.heads = bf16[1536,128]{1,0:T(8,128)(2,1)S(1)} custom-call(s32[1,2]{1,0:T(1,128)S(1)} %copy-done.6, bf16[1536,128]{1,0:T(8,128)(2,1)S(1)} %get-tuple-element.50.q_ref, bf16[1536,128]{1,0:T(8,128)(2,1)S(1)} %get-tuple-element.51.kv_ref), custom_call_target="tpu_custom_call" | custom-call | flops 20000000000 | bytes 1048576 | tf_op jit(solution)/shard_map/attend/pallas_call | solution.py:164
  108.0 25.9 %middle.1 = (bf16[384,512]{1,0:T(8,128)(2,1)S(1)}, f32[96,2048]{1,0:T(8,128)S(1)}, f32[96,1]{1,0:T(8,128)S(1)}, bf16[96,2048]{1,0:T(8,128)(2,1)S(1)}) custom-call(bf16[1536,128]{1,0:T(8,128)(2,1)S(1)} %attend.1.heads, bf16[96,2048]{1,0:T(8,128)(2,1)S(1)} %get-tuple-element.52.in_mine, f32[1,2048]{1,0:T(1,128)S(1)} %slice_bitcast_fusion.2.gain.gain_ref, ...), custom_call_target="tpu_custom_call" | custom-call | flops 1000000000 | bytes 8388608 | tf_op jit(solution)/shard_map/middle/pallas_call | solution.py:863
  133.9 0.9 copy-done.10
  136.9 1.0 copy-done.33
  138.4 113.5 %ffn.1 = (bf16[96,2048]{1,0:T(8,128)(2,1)}, f32[96,2048]{1,0:T(8,128)}, f32[1,2048]{1,0:T(1,128)}, bf16[384,2048]{1,0:T(8,128)(2,1)}, bf16[1536,128]{1,0:T(8,128...) custom-call(bf16[96,2048]{1,0:T(8,128)(2,1)} %copy-done.13, ...), custom_call_target="tpu_custom_call" | custom-call | flops 25999998976 | bytes 41943040 | tf_op jit(solution)/shard_map/ffn/pallas_call | solution.py:1188
  251.9 1.0 copy-done.23
  252.9 7.8 %attend_back.1 = (bf16[1536,128]{1,0:T(8,128)(2,1)S(1)}, bf16[1536,128]{1,0:T(8,128)(2,1)S(1)}) custom-call(s32[1,2]{1,0:T(1,128)S(1)} %copy-done.6, bf16[1536,128]{1,0:T(8,128)(2,1)S(1)} %get-tuple-element.50.q_ref, bf16[1536,128]{1,0:T(8,128)(2,1)S(1)} %copy-done.19, bf16[1536,128]{1,0:T(8,128)(2,1)S(1)} %copy-done.23, f32[1024,128]{1,0:T(8,128)S(1)} %copy-done.8, ...), custom_call_target="tpu_custom_call" | custom-call | flops 5000000000 | bytes 1048576 | tf_op jit(solution)/shard_map/attend_back/pallas_call | solution.py:164
  262.1 92.5 %back.1 = (bf16[1536,128]{1,0:T(8,128)(2,1)}, bf16[1536,128]{1,0:T(8,128)(2,1)}, f32[256,128]{1,0:T(8,128)}, f32[4,32,128]{2,1,0:T(8,128)}, f32[256,128]{1,0:T(8...) custom-call(bf16[1536,128]{1,0:T(8,128)(2,1)} %copy-done.21, ...), custom_call_target="tpu_custom_call" | custom-call | flops 10000000000 | bytes 31457280 | tf_op jit(solution)/shard_map/back/pallas_call | solution.py:499
  354.7 0.9 constant_dynamic-slice_fusion
  356.0 1.0 reshape.50
  358.7 1.8 copy.34
  360.5 1.8 copy.35
  (84 shorter events, 10.4 us)
Async XLA Ops:
  2.7 36.2 %copy-start.6 = (s32[1,2]{1,0:T(1,128)S(1)}, s32[1,2]{1,0:T(1,128)}, u32[]{:S(2)}) copy-start(s32[1,2]{1,0:T(1,128)} %len_ref.3) | copy-start | bytes 28
  3.7 36.5 %copy-start.28 = (bf16[2048,256]{1,0:T(8,128)(2,1)S(1)}, bf16[2048,256]{1,0:T(8,128)(2,1)}, u32[]{:S(2)}) copy-start(bf16[2048,256]{1,0:T(8,128)(2,1)} %param.19) | copy-start | bytes 3145732
  34.8 62.3 %collective-permute-start.1 = (bf16[2,3,3,64,1024]{4,3,2,1,0:T(8,128)(2,1)}, bf16[2,3,3,64,1024]{4,3,2,1,0:T(8,128)(2,1)S(1)}, u32[]{:S(2)}, u32[]{:S(2)}) collective-permute-start(bf16[2,3,3,64,1024]{4,3,2,1,0:T(8,128)(2,1)} %weights.1.piece0), channel_id=1, source_target_pairs={{0,96},{16,112},{32,0},{48,16},{64,32},{80,48},{96,64},{112,80},{1... | collective-permute-start | bytes 7077896 | tf_op jit(solution)/shard_map/ppermute | solution.py:572
  38.9 58.3 %collective-permute-start = (bf16[2,3,3,64,1024]{4,3,2,1,0:T(8,128)(2,1)}, bf16[2,3,3,64,1024]{4,3,2,1,0:T(8,128)(2,1)}, u32[]{:S(2)}, u32[]{:S(2)}) collective-permute-start(bf16[2,3,3,64,1024]{4,3,2,1,0:T(8,128)(2,1)} %weights.1.piece0), channel_id=1, source_target_pairs={{0,32},{16,48},{32,64},{48,80},{64,96},{80,112},{96,0},{112,16},{1... | collective-permute-start | bytes 7077896 | tf_op jit(solution)/shard_map/ppermute | solution.py:572
  39.0 3.0 copy-start.1
  39.0 3.0 copy-start.2
  39.0 3.0 copy-start.3
  39.0 3.0 copy-start.4
  39.0 3.0 copy-start.5
  97.1 6.2 %copy-start.18 = (bf16[1536,128]{1,0:T(8,128)(2,1)}, bf16[1536,128]{1,0:T(8,128)(2,1)S(1)}, u32[]{:S(2)}) copy-start(bf16[1536,128]{1,0:T(8,128)(2,1)S(1)} %get-tuple-element.51.kv_ref) | copy-start | bytes 1179652
  97.1 10.9 %copy-start.9 = (bf16[2048,512]{1,0:T(8,128)(2,1)}, bf16[2048,512]{1,0:T(8,128)(2,1)S(1)}, u32[]{:S(2)}) copy-start(bf16[2048,512]{1,0:T(8,128)(2,1)S(1)} %get-tuple-element.54.w_cat.w_out_ref) | copy-start | bytes 6291460
  97.1 10.9 %copy-start.11 = (bf16[96,2048]{1,0:T(8,128)(2,1)}, bf16[96,2048]{1,0:T(8,128)(2,1)S(1)}, u32[]{:S(2)}) copy-start(bf16[96,2048]{1,0:T(8,128)(2,1)S(1)} %get-tuple-element.52.in_mine) | copy-start | bytes 1179652
  97.1 10.9 %copy-start = (f32[1,2048]{1,0:T(1,128)}, f32[1,2048]{1,0:T(1,128)S(1)}, u32[]{:S(2)}) copy-start(f32[1,2048]{1,0:T(1,128)S(1)} %slice_bitcast_fusion.2.gain.gain_ref) | copy-start | bytes 24580
  97.1 10.8 %copy-start.24 = (bf16[2,3,3,64,1024]{4,3,2,1,0:T(8,128)(2,1)}, bf16[2,3,3,64,1024]{4,3,2,1,0:T(8,128)(2,1)S(1)}, u32[]{:S(2)}) copy-start(bf16[2,3,3,64,1024]{4,3,2,1,0:T(8,128)(2,1)S(1)} %collective-permute-done.1.piece3) | copy-start | bytes 7077892
  99.5 37.4 %collective-permute-start.2 = (bf16[3,3,64,1024]{3,2,1,0:T(8,128)(2,1)S(1)}, bf16[3,3,64,1024]{3,2,1,0:T(8,128)(2,1)S(1)}, u32[]{:S(2)}, u32[]{:S(2)}) collective-permute-start(bf16[3,3,64,1024]{3,2,1,0:T(8,128)(2,1)S(1)} %slice_bitcast_fusion.1), channel_id=1, source_target_pairs={{0,32},{16,48},{32,64},{48,80},{64,96},{80,112},{96,0},{112,16},{1... | collective-permute-start | bytes 3538952 | tf_op jit(solution)/shard_map/ppermute | solution.py:572
  99.6 37.4 %collective-permute-start.3 = (bf16[3,3,64,1024]{3,2,1,0:T(8,128)(2,1)S(1)}, bf16[3,3,64,1024]{3,2,1,0:T(8,128)(2,1)S(1)}, u32[]{:S(2)}, u32[]{:S(2)}) collective-permute-start(bf16[3,3,64,1024]{3,2,1,0:T(8,128)(2,1)S(1)} %slice_bitcast_fusion), channel_id=1, source_target_pairs={{0,96},{16,112},{32,0},{48,16},{64,32},{80,48},{96,64},{112,80},{1... | collective-permute-start | bytes 3538952 | tf_op jit(solution)/shard_map/ppermute | solution.py:572
  138.3 113.5 %copy-start.7 = (f32[1024,128]{1,0:T(8,128)S(1)}, f32[1024,128]{1,0:T(8,128)}, u32[]{:S(2)}) copy-start(f32[1024,128]{1,0:T(8,128)} %constant.77.sin_ref) | copy-start | bytes 1572868
  138.4 113.5 %copy-start.8 = (f32[1024,128]{1,0:T(8,128)S(1)}, f32[1024,128]{1,0:T(8,128)}, u32[]{:S(2)}) copy-start(f32[1024,128]{1,0:T(8,128)} %constant.76.cos_ref) | copy-start | bytes 1572868
  138.4 113.5 %copy-start.19 = (bf16[1536,128]{1,0:T(8,128)(2,1)S(1)}, bf16[1536,128]{1,0:T(8,128)(2,1)}, u32[]{:S(2)}) copy-start(bf16[1536,128]{1,0:T(8,128)(2,1)} %copy-done.18) | copy-start | bytes 1179652
  354.6 7.6 %copy-start.30 = (f32[256,128]{1,0:T(8,128)S(1)}, f32[256,128]{1,0:T(8,128)}, u32[]{:S(2)}) copy-start(f32[256,128]{1,0:T(8,128)} %get-tuple-element.111) | copy-start | bytes 393220
  354.6 8.3 %copy-start.29 = (f32[256,128]{1,0:T(8,128)S(1)}, f32[256,128]{1,0:T(8,128)}, u32[]{:S(2)}) copy-start(f32[256,128]{1,0:T(8,128)} %get-tuple-element.114) | copy-start | bytes 393220
  354.6 8.9 %copy-start.27 = (f32[8,16,1024]{2,1,0:T(8,128)S(1)}, f32[8,16,1024]{2,1,0:T(8,128)}, u32[]{:S(2)}) copy-start(f32[8,16,1024]{2,1,0:T(8,128)} %get-tuple-element.116) | copy-start | bytes 1572868
  354.7 9.7 %copy-start.26 = (f32[8,16,1024]{2,1,0:T(8,128)S(1)}, f32[8,16,1024]{2,1,0:T(8,128)}, u32[]{:S(2)}) copy-start(f32[8,16,1024]{2,1,0:T(8,128)} %get-tuple-element.117) | copy-start | bytes 1572868
  358.7 6.5 %copy-start.25 = (f32[8,16,1024]{2,1,0:T(8,128)S(1)}, f32[8,16,1024]{2,1,0:T(8,128)}, u32[]{:S(2)}) copy-start(f32[8,16,1024]{2,1,0:T(8,128)} %get-tuple-element.118) | copy-start | bytes 1572868
  (14 other events, 18.6 us)

commit v6 on v5

--- a/solution.py
+++ b/solution.py
@@ -128,38 +128,6 @@
     return tensor * cosine + swapped * sine
 
 
-def attend_back_body(len_ref, q_ref, kv_ref, back_ref, cos_ref, sin_ref, dq_ref, dkv_ref, acc_ref):
-    for start, blocks in starts_of(len_ref):
-        acc_ref[...] = jnp.zeros(acc_ref.shape, F32)
-        for i in range(blocks):
-            n = 256 * (i + 1)
-            mine = rows_256(start + 256 * i, 256)
-            stack = both(q_ref[mine, :])
-            keys, raised, mass = block_probs(q_ref, kv_ref, start, i, stack)
-            soft = raised * (1.0 / mass)
-            values = kv_ref[rows_256(start, n), 64:128]
-            backs = both(back_ref[mine, :])
-            prob_back = lax.dot_general(
-                values, backs, (((1,), (1,)), ((), ())), preferred_element_type=F32
-            )
-            inner = jnp.sum(soft * prob_back, axis=0, keepdims=True)
-            score_back = (soft * (prob_back - inner)).astype(BF)
-            dq = lax.dot_general(
-                score_back, keys, (((0,), (0,)), ((), ())), preferred_element_type=F32
-            ) * (HEAD_DIM**-0.5)
-            dq = jnp.concatenate([dq[:256], dq[256:]], axis=1)
-            pos = slice(256 * i, 256 * i + 256)
-            dq_ref[mine, :] = unrope(dq, cos_ref[pos, :], sin_ref[pos, :]).astype(BF)
-            dk = jnp.dot(score_back, stack, preferred_element_type=F32) * (HEAD_DIM**-0.5)
-            dv = jnp.dot(soft.astype(BF), backs, preferred_element_type=F32)
-            acc_ref[0:n, :] += jnp.concatenate([dk, dv], axis=1)
-        m = 256 * blocks
-        acc = acc_ref[0:m, :]
-        lane = lax.broadcasted_iota(jnp.int32, acc.shape, 1)
-        turned = unrope(acc, cos_ref[0:m, :], sin_ref[0:m, :])
-        dkv_ref[rows_256(start, m), :] = jnp.where(lane < 64, turned, acc).astype(BF)
-
-
 def vmem_call(name, body, ins, outs, scratch=(), flops=0):
     return pl.pallas_call(
         body,
@@ -174,9 +142,29 @@
     )(*ins)
 
 
+def masked_scores(keys, query, i, length):
+    n = keys.shape[0]
+    scores = contract_cols(keys, query) * (HEAD_DIM**-0.5)
+    key_id = lax.broadcasted_iota(jnp.int32, (256, 256), 0)
+    query_id = lax.broadcasted_iota(jnp.int32, (256, 256), 1)
+    parts = [jnp.where(key_id <= query_id, scores[n - 256 :, :], NEG)]
+    middle = 0
+    if i >= 2:
+        cut = SHORT if i < 4 else 2 * SHORT
+        middle = SHORT
+        parts.insert(0, jnp.where(length == cut, NEG, scores[:SHORT, :]))
+    if n - 256 > middle:
+        parts.insert(len(parts) - 1, scores[middle : n - 256, :])
+    return jnp.concatenate(parts, axis=0) if len(parts) > 1 else parts[0]
+
+
 def back_body(
-    dq_ref,
-    dkv_ref,
+    len_ref,
+    q_ref,
+    kv_ref,
+    heads_back,
+    cos_ref,
+    sin_ref,
     w_attn,
     heads_cat,
     out_mine,
@@ -185,14 +173,15 @@
     scale_ref,
     gain_ref,
     ffn_gain_part,
-    normed_in,
-    mix_in,
-    ffn_in,
-    up_in,
+    normed,
+    mix_full,
     down_own,
     down_came,
     gate_own,
     gate_came,
+    up_own,
+    up_late,
+    up_pass,
     layer_output,
     input_grad,
     query_grad,
@@ -202,18 +191,20 @@
     up_grad,
     down_grad,
     gain_grad,
-    left_buf,
-    right_buf,
+    dq_ref,
+    dkv_ref,
+    dkv_acc,
     down_in,
     gate_in,
+    up_in,
+    late_in,
+    pass_in,
+    up_last,
     down_sum,
     gate_sum,
+    up_sum,
     down_z,
     gate_x,
-    up_terms,
-    up_core,
-    up_z,
-    up_sum,
     up_x,
     cat_back,
     norm_send,
@@ -241,32 +232,57 @@
     k_last,
     send_sem,
     recv_sem,
-    core_send,
-    core_recv,
     local_sem,
 ):
     me = whereami()
     wire = Wire(me, send_sem, recv_sem)
-    load_left = pltpu.make_async_copy(ffn_in, left_buf, local_sem.at[0])
-    load_right = pltpu.make_async_copy(up_in, right_buf, local_sem.at[1])
-    load_left.start()
-    load_right.start()
-
-    def halves(own, came, buf, h, sem):
-        part_of = pl.ds(h * (own.shape[0] // 2), own.shape[0] // 2)
-        return [
-            pltpu.make_async_copy(own.at[part_of], buf.at[0], local_sem.at[sem]),
-            pltpu.make_async_copy(came.at[:, part_of], buf.at[1:4], local_sem.at[sem + 1]),
-        ]
-
-    def start(copies):
-        for copy in copies:
-            copy.start()
-
-    start(halves(gate_own, gate_came, gate_in, 0, 2))
-    start(halves(down_own, down_came, down_in, 0, 4))
+    loads = []
+    for src, dst in (
+        (up_late, late_in),
+        (up_pass, pass_in),
+        (gate_own, gate_in.at[0]),
+        (gate_came, gate_in.at[1:3]),
+        (down_own, down_in.at[0]),
+        (down_came, down_in.at[1:3]),
+        (up_own, up_in),
+    ):
+        loads.append(pltpu.make_async_copy(src, dst, local_sem.at[len(loads)]))
+        loads[-1].start()
     meet(me, PLANE[1:] + TOKS[1:])
     sent = []
+
+    for copy in loads[0:2]:
+        copy.wait()
+    up_moves = [
+        wire.send(ZOFF[1], late_in.at[0, 4:8], up_last.at[0, 4:8]),
+        wire.send(ZOFF[3], late_in.at[1, 0:4], up_last.at[1, 0:4]),
+    ]
+
+    length = len_ref[0:1, 0:1]
+    dkv_acc[...] = jnp.zeros(dkv_acc.shape, F32)
+    for i in range(6):
+        low, high = 0 if i < 4 else SHORT, 256 * (i + 1)
+        here = slice(256 * i, high)
+        keys, values = kv_ref[low:high, 0:64], kv_ref[low:high, 64:128]
+        parts = []
+        for head in (slice(0, 64), slice(64, 128)):
+            query, value_back = q_ref[here, head], heads_back[here, head]
+            scores = masked_scores(keys, query, i, length)
+            raised = jnp.exp(scores - jnp.max(scores, axis=0, keepdims=True))
+            soft = raised * (1.0 / jnp.sum(raised, axis=0, keepdims=True))
+            prob_back = contract_cols(values, value_back)
+            inner = jnp.sum(soft * prob_back, axis=0, keepdims=True)
+            score_back = (soft * (prob_back - inner)).astype(BF)
+            parts.append(contract_rows(score_back, keys) * (HEAD_DIM**-0.5))
+            dk = multiply(score_back, query) * (HEAD_DIM**-0.5)
+            dv = multiply(soft.astype(BF), value_back)
+            dkv_acc[low:high, :] += jnp.concatenate([dk, dv], axis=1)
+        dq = jnp.concatenate(parts, axis=1)
+        dq_ref[here, :] = unrope(dq, cos_ref[here, :], sin_ref[here, :]).astype(BF)
+    acc = dkv_acc[...]
+    lane = lax.broadcasted_iota(jnp.int32, acc.shape, 1)
+    turned = unrope(acc, cos_ref[...], sin_ref[...])
+    dkv_ref[...] = jnp.where(lane < 64, turned, acc).astype(BF)
 
     spot = rows(me.chunk * CHUNK, CHUNK)
     moves = []
@@ -288,24 +304,39 @@
     ]
     layer_output[mine, :] = out_mine[:, lanes(me.block)]
 
-    load_left.wait()
-    load_right.wait()
-    up_pair = PairSum(me, left_buf, right_buf, up_terms, up_core, core_send, core_recv)
-    up_pair.multiply(0, 8)
-    load_left = pltpu.make_async_copy(mix_in, left_buf, local_sem.at[0])
-    load_left.start()
-    load_left.wait()
+    add_to(late_in.at[0, 0:4], pass_in.at[0])
+    up_moves.append(wire.send(ZOFF[1], late_in.at[0, 0:4], up_last.at[0, 0:4]))
+    add_to(late_in.at[1, 4:8], pass_in.at[1])
+    up_moves.append(wire.send(ZOFF[3], late_in.at[1, 4:8], up_last.at[1, 4:8]))
+
+    def fold(ref, out):
+        for n in range(out.shape[0]):
+            value = ref[0, n].astype(F32)
+            for k in range(1, ref.shape[0]):
+                value = value + ref[k, n].astype(F32)
+            out[n] = value.astype(BF)
+
+    def x_blocks(ref, came):
+        moves = []
+        for k in (1, 2, 3):
+            e, dxl = XOFF[k][4], XOFF[k][2]
+            src = ref.at[dxl * 4 : dxl * 4 + 4, :, :, e * 1024 : e * 1024 + 1024]
+            moves.append(wire.send(XOFF[k], src, came.at[k - 1]))
+        return moves
+
+    for copy in loads[2:]:
+        copy.wait()
+    fold(gate_in, gate_sum)
+    gate_moves = x_blocks(gate_sum, gate_x)
+
     for z in range(4):
-        block = contract_rows(left_buf[:, z * 512 : z * 512 + 512], heads_cat[...])
+        block = contract_rows(mix_full[:, z * 512 : z * 512 + 512], heads_cat[...])
         o_terms[z] = block.astype(BF).reshape(2, 256, 512)
     o_pair = wire.send(SIBLING, o_terms.at[:, 1 - me.core], o_core)
-    load_right = pltpu.make_async_copy(normed_in, right_buf, local_sem.at[1])
-    load_right.start()
-    up_pair.add(0, 8)
-    up_moves = [
-        wire.send(ZOFF[d], up_terms.at[:, :, (me.z + d) % 4, me.core], up_z.at[d - 1])
-        for d in (1, 2, 3)
-    ]
+
+    def add_core(copy, terms, came):
+        copy.wait_recv()
+        terms[:, me.core] = (terms[:, me.core].astype(F32) + came[...].astype(F32)).astype(BF)
 
     finish(moves)
     for h in range(4):
@@ -319,58 +350,23 @@
         for d in (1, 2, 3)
     ]
 
-    def add_core(copy, terms, came):
-        copy.wait_recv()
-        terms[:, me.core] = (terms[:, me.core].astype(F32) + came[...].astype(F32)).astype(BF)
-
     add_core(o_pair, o_terms, o_core)
     o_moves = [
-        wire.send(XOFF[k], o_terms.at[:, me.core, :, k * 128 : k * 128 + 128], o_x.at[k - 1])
-        for k in (1, 2, 3)
-    ]
-
-    load_right.wait()
+        wire.send(ZOFF[d], o_terms.at[(me.z + d) % 4, me.core], o_z.at[d - 1]) for d in (1, 2, 3)
+    ]
+
     for z in range(4):
-        block = contract_rows(right_buf[:, z * 512 : z * 512 + 512], cat_back[:, 0:512])
+        block = contract_rows(normed[:, z * 512 : z * 512 + 512], cat_back[:, 0:512])
         q_terms[z] = block.astype(BF).reshape(2, 256, 512)
     q_pair = wire.send(SIBLING, q_terms.at[:, 1 - me.core], q_core)
     for z in range(4):
-        left = right_buf[:, z * 512 : z * 512 + 512]
+        left = normed[:, z * 512 : z * 512 + 512]
         block = contract_rows(left, cat_back[:, 512:768]) + contract_rows(
             left, cat_back[:, 768:1024]
         )
         k_terms[z] = block.astype(BF).reshape(2, 4, 2, 32, 256)
     k_pair = wire.send(SIBLING, k_terms.at[:, 1 - me.core], k_core)
 
-    def fold(own, came, buf, out, sem):
-        size = buf.shape[1]
-        for h in range(2):
-            copies = halves(own, came, buf, h, sem)
-            for copy in copies:
-                copy.wait()
-
-            def step(i, _, h=h):
-                value = buf[0, i].astype(F32)
-                for k in (1, 2, 3):
-                    value = value + buf[k, i].astype(F32)
-                out[h * size + i] = value.astype(BF)
-                return 0
-
-            lax.fori_loop(0, size, step, 0)
-            if h == 0:
-                start(halves(own, came, buf, 1, sem))
-
-    def gate_block(k):
-        e, dxl = XOFF[k][4], XOFF[k][2]
-        return gate_sum.at[dxl * 4 : dxl * 4 + 4, :, :, e * 1024 : e * 1024 + 1024]
-
-    fold(gate_own, gate_came, gate_in, gate_sum, 2)
-    gate_moves = [wire.send(XOFF[k], gate_block(k), gate_x.at[k - 1]) for k in (1, 2, 3)]
-    fold(down_own, down_came, down_in, down_sum, 4)
-    down_moves = [
-        wire.send(ZOFF[d], down_sum.at[:, :, (me.z + d) % 4], down_z.at[d - 1]) for d in (1, 2, 3)
-    ]
-
     def kv_block(k):
         e, dxl = XOFF[k][4], XOFF[k][2]
         return k_terms.at[:, me.core, :, (me.xh + e) % 2, :, dxl * 128 : dxl * 128 + 128]
@@ -379,9 +375,38 @@
     k_moves = [wire.send(XOFF[k], kv_block(k), k_x.at[k - 1]) for k in (1, 2, 3)]
     add_core(q_pair, q_terms, q_core)
     q_moves = [
-        wire.send(XOFF[k], q_terms.at[:, me.core, :, k * 128 : k * 128 + 128], q_x.at[k - 1])
-        for k in (1, 2, 3)
-    ]
+        wire.send(ZOFF[d], q_terms.at[(me.z + d) % 4, me.core], q_z.at[d - 1]) for d in (1, 2, 3)
+    ]
+
+    fold(down_in, down_sum)
+    down_moves = [
+        wire.send(ZOFF[d], down_sum.at[:, :, (me.z + d) % 4], down_z.at[d - 1]) for d in (1, 2, 3)
+    ]
+
+    def gathered(moves, own, came):
+        for copy in moves:
+            copy.wait_recv()
+        sent.extend(moves)
+        value = own.astype(F32)
+        for d in range(came.shape[0]):
+            value = value + came[d].astype(F32)
+        return value
+
+    for copy in up_moves:
+        copy.wait_recv()
+    sent.extend(up_moves)
+    for n in range(8):
+        value = up_in[n].astype(F32) + up_last[0, n].astype(F32)
+        up_sum[n] = (value + up_last[1, n].astype(F32)).astype(BF)
+    up_moves = x_blocks(up_sum, up_x)
+
+    def over_x(ref, came):
+        return [
+            wire.send(XOFF[k], ref.at[:, k * 128 : k * 128 + 128], came.at[k - 1]) for k in (1, 2, 3)
+        ]
+
+    o_sum[...] = gathered(o_moves, o_terms[me.z, me.core], o_z).astype(BF)
+    o_moves = over_x(o_sum, o_x)
 
     finish(norm_moves)
     here = rows(me.y * SUB, SUB)
@@ -404,57 +429,20 @@
     input_grad[mine, :] = in_grad[:, lanes(me.block)]
     gain_plane[me.block] = gain_parts[:, lanes(me.block)]
 
-    def over_x(moves, own, came, out):
-        for copy in moves:
-            copy.wait_recv()
-        value = own.astype(F32)
-        for k in range(3):
-            value = value + came[k].astype(F32)
-        out[...] = value.astype(BF)
-        sent.extend(moves)
-
-    over_x(o_moves, o_terms[:, me.core, :, 0:128], o_x, o_sum)
-    over_x(q_moves, q_terms[:, me.core, :, 0:128], q_x, q_sum)
-    over_x(k_moves, k_terms[:, me.core, :, me.xh, :, 0:128], k_x, k_sum)
-    late = []
-    for summed, came in ((o_sum, o_z), (q_sum, q_z), (k_sum, k_z)):
-        late.append(
-            [wire.send(ZOFF[d], summed.at[(me.z + d) % 4], came.at[d - 1]) for d in (1, 2, 3)]
-        )
-
-    def over_z(moves, own, came):
-        for copy in moves:
-            copy.wait_recv()
-        sent.extend(moves)
-        value = own.astype(F32)
-        for d in range(3):
-            value = value + came[d].astype(F32)
-        return value
-
-    down_grad[...] = over_z(down_moves, down_sum[:, :, me.z].reshape(8, 16, 1024), down_z.reshape(3, 8, 16, 1024))
-    gate_grad[...] = over_z(gate_moves, gate_sum[0:4, :, :, 0:1024].reshape(8, 16, 1024), gate_x.reshape(3, 8, 16, 1024))
-    for copy in up_moves:
-        copy.wait_recv()
-    sent.extend(up_moves)
-
-    def up_step(i, _):
-        value = up_terms[i, :, me.z, me.core].astype(F32)
-        for d in range(3):
-            value = value + up_z[d, i].astype(F32)
-        up_sum[i] = value.astype(BF)
-        return 0
-
-    lax.fori_loop(0, 8, up_step, 0)
-
-    def up_block(k):
-        e, dxl = XOFF[k][4], XOFF[k][2]
-        return up_sum.at[dxl * 4 : dxl * 4 + 4, :, :, e * 1024 : e * 1024 + 1024]
-
-    up_moves = [wire.send(XOFF[k], up_block(k), up_x.at[k - 1]) for k in (1, 2, 3)]
-
-    out_grad[...] = over_z(late[0], o_sum[me.z], o_z)
-    query_grad[...] = over_z(late[1], q_sum[me.z], q_z)
-    k_last[...] = over_z(late[2], k_sum[me.z], k_z)
+    k_sum[...] = gathered(k_moves, k_terms[:, me.core, :, me.xh, :, 0:128], k_x).astype(BF)
+    k_moves = [wire.send(ZOFF[d], k_sum.at[(me.z + d) % 4], k_z.at[d - 1]) for d in (1, 2, 3)]
+    q_sum[...] = gathered(q_moves, q_terms[me.z, me.core], q_z).astype(BF)
+    q_moves = over_x(q_sum, q_x)
+
+    shape = (8, 16, 1024)
+    own = down_sum[:, :, me.z].reshape(shape)
+    down_grad[...] = gathered(down_moves, own, down_z.reshape(3, *shape))
+    own = gate_sum[0:4, :, :, 0:1024].reshape(shape)
+    gate_grad[...] = gathered(gate_moves, own, gate_x.reshape(3, *shape))
+
+    out_grad[...] = gathered(o_moves, o_sum[:, 0:128], o_x)
+    query_grad[...] = gathered(q_moves, q_sum[:, 0:128], q_x)
+    k_last[...] = gathered(k_moves, k_sum[me.z], k_z)
     y_moves = [wire.send(YOFF[d], k_last.at[me.at(YOFF[d]).y], kv_grad.at[me.y]) for d in (1, 2, 3)]
     kv_grad[me.y] = k_last[me.y]
     for copy in leaving:
@@ -463,12 +451,12 @@
     gain_mine[...] = jnp.sum(gain_plane[...], axis=0)
     tok_moves = [wire.send(off, gain_mine, gain_toks.at[me.tok]) for off in TOKS[1:]]
     gain_toks[me.tok] = gain_mine[...]
-    up_grad[...] = over_z(up_moves, up_sum[0:4, :, :, 0:1024].reshape(8, 16, 1024), up_x.reshape(3, 8, 16, 1024))
+    own = up_sum[0:4, :, :, 0:1024].reshape(shape)
+    up_grad[...] = gathered(up_moves, own, up_x.reshape(3, *shape))
     finish(y_moves + tok_moves)
     gain_grad[...] = jnp.sum(gain_toks[...], axis=0)
     for copy in sent:
         copy.wait_send()
-    up_pair.sent()
     o_pair.wait_send()
     q_pair.wait_send()
     k_pair.wait_send()
@@ -489,13 +477,6 @@
         SDS((8, 128), F32),
     ]
     v = pltpu.VMEM
-    heads_sum = [
-        v((4, 2, 256, 512), BF),
-        v((4, 256, 512), BF),
-        v((3, 4, 256, 128), BF),
-        v((4, 256, 128), BF),
-        v((3, 256, 128), BF),
-    ]
     return pl.pallas_call(
         back_body,
         name="back",
@@ -503,18 +484,20 @@
         in_specs=[vm] * len(vmem_ins) + [hbm] * len(hbm_ins),
         out_specs=[vm] * len(outs),
         scratch_shapes=[
-            v((CHUNK, D), BF),
-            v((CHUNK, D), BF),
-            v((4, 2, 2, 4, 16, 1024), BF),
-            v((4, 4, 2, 16, 2048), BF),
+            v((ROWS, 128), BF),
+            v((ROWS, 128), BF),
+            v((ROWS, 128), F32),
+            v((3, 4, 2, 4, 16, 1024), BF),
+            v((3, 8, 2, 16, 2048), BF),
+            v((8, 2, 16, 2048), BF),
+            v((2, 8, 2, 16, 2048), BF),
+            v((2, 4, 2, 16, 2048), BF),
+            v((2, 8, 2, 16, 2048), BF),
             v((4, 2, 4, 16, 1024), BF),
+            v((8, 2, 16, 2048), BF),
             v((8, 2, 16, 2048), BF),
             v((3, 4, 2, 16, 1024), BF),
             v((3, 4, 2, 16, 1024), BF),
-            v((8, 2, 4, 2, 16, 2048), BF),
-            v((8, 2, 4, 16, 2048), BF),
-            v((3, 8, 2, 16, 2048), BF),
-            v((8, 2, 16, 2048), BF),
             v((3, 4, 2, 16, 1024), BF),
             v((CHUNK, 1024), BF),
             v((CHUNK, D), BF),
@@ -525,9 +508,17 @@
             v((8, 128), F32),
             v((8, 8, 128), F32),
         ]
-        + heads_sum
-        + heads_sum
         + [
+            v((4, 2, 256, 512), BF),
+            v((4, 256, 512), BF),
+            v((3, 256, 128), BF),
+            v((256, 512), BF),
+            v((3, 256, 512), BF),
+            v((4, 2, 256, 512), BF),
+            v((4, 256, 512), BF),
+            v((3, 256, 128), BF),
+            v((256, 512), BF),
+            v((3, 256, 512), BF),
             v((4, 2, 4, 2, 32, 256), BF),
             v((4, 4, 2, 32, 256), BF),
             v((3, 4, 4, 32, 128), BF),
@@ -536,9 +527,7 @@
             v((4, 32, 128), F32),
             pltpu.SemaphoreType.DMA((104,)),
             pltpu.SemaphoreType.DMA((104,)),
-            pltpu.SemaphoreType.DMA((8,)),
-            pltpu.SemaphoreType.DMA((8,)),
-            pltpu.SemaphoreType.DMA((6,)),
+            pltpu.SemaphoreType.DMA((7,)),
         ],
         compiler_params=pltpu.CompilerParams(
             collective_id=15, has_side_effects=True, vmem_limit_bytes=56 * 2**20
@@ -880,13 +869,13 @@
 
 
 class PairSum:
-    def __init__(self, me, left, right, terms, came, send_sem, recv_sem):
-        self.me, self.left, self.right, self.terms, self.came = me, left, right, terms, came
-        self.send_sem, self.recv_sem = send_sem, recv_sem
+    def __init__(self, me, left, right, own, came, stage, send_sem, recv_sem):
+        self.me, self.left, self.right, self.own, self.came = me, left, right, own, came
+        self.stage, self.send_sem, self.recv_sem = stage, send_sem, recv_sem
 
     def copy(self, i):
         return pltpu.make_async_remote_copy(
-            src_ref=self.terms.at[i, :, :, 1 - self.me.core],
+            src_ref=self.stage.at[i % 3, :, :, 1 - self.me.core],
             dst_ref=self.came.at[i],
             send_sem=self.send_sem.at[i],
             recv_sem=self.recv_sem.at[i],
@@ -897,29 +886,33 @@
     def multiply(self, first, last):
         def step(i, _):
             cols = pl.ds(pl.multiple_of(i * 256, 256), 256)
+
+            @pl.when(i >= first + 3)
+            def _():
+                self.copy(i - 3).wait_send()
+
             block = contract_rows(self.left[:, cols], self.right[...])
-            self.terms[i] = block.astype(BF).reshape(2, 4, 2, 16, 2048)
+            self.stage[i % 3] = block.astype(BF).reshape(2, 4, 2, 16, 2048)
+            self.own[i] = self.stage[i % 3, :, :, self.me.core]
             self.copy(i).start()
             return 0
 
         lax.fori_loop(first, last, step, 0)
+        for i in range(last - 3, last):
+            self.copy(i).wait_send()
 
     def add(self, first, last):
         def step(i, _):
-            copy = self.copy(i)
-            copy.wait_recv()
-            mine = self.terms[i, :, :, self.me.core].astype(F32) + self.came[i].astype(F32)
-            self.terms[i, :, :, self.me.core] = mine.astype(BF)
+            self.copy(i).wait_recv()
+            self.own[i] = (self.own[i].astype(F32) + self.came[i].astype(F32)).astype(BF)
             return 0
 
         lax.fori_loop(first, last, step, 0)
 
-    def sent(self):
-        def step(i, _):
-            self.copy(i).wait_send()
-            return 0
-
-        lax.fori_loop(0, 8, step, 0)
+
+def add_to(target, came):
+    for i in range(came.shape[0]):
+        target[i] = (target[i].astype(F32) + came[i].astype(F32)).astype(BF)
 
 
 def ffn_body(
@@ -942,16 +935,19 @@
     gain_part,
     mix_full,
     heads_back,
-    ffn_in,
-    up_back,
     down_own,
     down_came,
     gate_own,
     gate_came,
+    up_own,
+    up_late,
+    up_pass,
     other_core,
     turned,
+    ffn_in,
     act,
     gate_back,
+    up_back,
     gate_tile,
     up_tile,
     down_tile,
@@ -965,7 +961,11 @@
     back_cat,
     down_terms,
     gate_terms,
+    up_terms,
+    stage,
     came,
+    down_pass,
+    gate_pass,
     send_sem,
     recv_sem,
     core_send,
@@ -1055,8 +1055,19 @@
     fetch(0, 0, 0)
     finish(gathers)
 
-    down_sum = PairSum(me, act, grad_ref, down_terms, came, core_send.at[0], core_recv.at[0])
-    gate_sum = PairSum(me, ffn_in, gate_back, gate_terms, came, core_send.at[1], core_recv.at[1])
+    sums = []
+    for left, right, own in (
+        (act, grad_ref, down_terms),
+        (ffn_in, gate_back, gate_terms),
+        (ffn_in, up_back, up_terms),
+    ):
+        j = len(sums)
+        sums.append(PairSum(me, left, right, own, came, stage, core_send.at[j], core_recv.at[j]))
+    down_sum, gate_sum, up_sum = sums
+
+    def came_free():
+        pl.semaphore_signal(ack, inc=1, device_id=me.at(SIBLING).device(), device_id_type=MESH)
+        pl.semaphore_wait(ack, 1)
 
     for e in range(2):
 
@@ -1107,31 +1118,44 @@
     ]
     down_sum.multiply(4, 8)
 
-    def down_block(k):
+
+    def down_block(k, h=None):
         e, dxl = XOFF[k][4], XOFF[k][2]
-        here = slice(dxl * 1024, dxl * 1024 + 1024)
-        return down_terms.at[e * 4 : e * 4 + 4, :, :, me.core, :, here]
-
-    down_sum.add(0, 4)
-    x_moves = [wire.send(XOFF[1], down_block(1), down_came.at[0])]
-    down_sum.add(4, 8)
-    x_moves += [wire.send(XOFF[k], down_block(k), down_came.at[k - 1]) for k in (2, 3)]
-    near = [pltpu.make_async_copy(down_block(0), down_own, local_sem.at[0])]
-    near[0].start()
-
-    pl.semaphore_signal(ack, inc=1, device_id=me.at(SIBLING).device(), device_id_type=MESH)
-    pl.semaphore_wait(ack, 1)
+        pairs = slice(e * 4, e * 4 + 4) if h is None else slice(e * 4 + h * 2, e * 4 + h * 2 + 2)
+        return down_terms.at[pairs, :, :, :, dxl * 1024 : dxl * 1024 + 1024]
+
+    down_sum.add(0, 8)
+    x_moves = [
+        wire.send(XOFF[1], down_block(2, 0), down_pass.at[0]),
+        wire.send(XOFF[3], down_block(2, 1), down_pass.at[1]),
+        wire.send(XOFF[1], down_block(1, 0), down_came.at[0, 0:2]),
+        wire.send(XOFF[3], down_block(3, 1), down_came.at[1, 2:4]),
+    ]
+    near = []
+
+    def keep(src, dst):
+        near.append(pltpu.make_async_copy(src, dst, local_sem.at[len(near)]))
+        near[-1].start()
+
+    keep(down_block(0), down_own)
+
+    def z_block(terms, d, h=None):
+        pairs = slice(0, 8) if h is None else slice(h * 4, h * 4 + 4)
+        return terms.at[pairs, :, (me.z + d) % 4]
+
+    came_free()
     gate_sum.multiply(0, 8)
-    gate_sum.add(0, 8)
-
-    def gate_block(z):
-        return gate_terms.at[:, :, z, me.core]
-
+    gate_sum.add(0, 4)
     z_moves = [
-        wire.send(ZOFF[d], gate_block((me.z + d) % 4), gate_came.at[d - 1]) for d in (1, 2, 3)
-    ]
-    near.append(pltpu.make_async_copy(gate_block(me.z), gate_own, local_sem.at[1]))
-    near[1].start()
+        wire.send(ZOFF[1], z_block(gate_terms, 2, 0), gate_pass.at[0]),
+        wire.send(ZOFF[3], z_block(gate_terms, 3, 0), gate_came.at[1, 0:4]),
+    ]
+    gate_sum.add(4, 8)
+    z_moves += [
+        wire.send(ZOFF[3], z_block(gate_terms, 2, 1), gate_pass.at[1]),
+        wire.send(ZOFF[1], z_block(gate_terms, 1, 1), gate_came.at[0, 4:8]),
+    ]
+    keep(z_block(gate_terms, 0), gate_own)
 
     finish(ffn_moves)
 
@@ -1164,6 +1188,29 @@
         wire.send(YOFF[d], down_send.at[rows(me.at(YOFF[d]).y * SUB, SUB), :], down_recv.at[d - 1])
         for d in (1, 2, 3)
     ]
+    x_moves[0].wait_recv()
+    add_to(down_block(3, 0), down_pass.at[0])
+    x_late = [wire.send(XOFF[3], down_block(3, 0), down_came.at[1, 0:2])]
+    x_moves[1].wait_recv()
+    add_to(down_block(1, 1), down_pass.at[1])
+    x_late.append(wire.send(XOFF[1], down_block(1, 1), down_came.at[0, 2:4]))
+    came_free()
+    up_sum.multiply(0, 8)
+    z_moves[0].wait_recv()
+    add_to(z_block(gate_terms, 1, 0), gate_pass.at[0])
+    z_late = [wire.send(ZOFF[1], z_block(gate_terms, 1, 0), gate_came.at[0, 0:4])]
+    z_moves[2].wait_recv()
+    add_to(z_block(gate_terms, 3, 1), gate_pass.at[1])
+    z_late.append(wire.send(ZOFF[3], z_block(gate_terms, 3, 1), gate_came.at[1, 4:8]))
+    up_sum.add(0, 8)
+    z_late += [
+        wire.send(ZOFF[1], z_block(up_terms, 2, 0), up_pass.at[0]),
+        wire.send(ZOFF[3], z_block(up_terms, 2, 1), up_pass.at[1]),
+    ]
+    keep(z_block(up_terms, 0), up_own)
+    keep(z_block(up_terms, 1), up_late.at[0])
+    keep(z_block(up_terms, 3), up_late.at[1])
+
     finish(mix_moves)
     back_cat[...] = multiply(mix_full[...], w_out_ref[...]).astype(BF)
     spot = rows(me.chunk * CHUNK, CHUNK)
@@ -1175,11 +1222,11 @@
     finish(down_moves)
     for h in range(2):
         out_mine[:, half[h]] = (resid_ref[:, half[h]] + summed(down_send, down_recv, h)).astype(BF)
-    finish(head_moves + x_moves + z_moves)
+    for move in (x_moves[0], x_moves[1], z_moves[0], z_moves[2]):
+        move.wait_send()
+    finish(head_moves + x_moves[2:] + [z_moves[1], z_moves[3]] + x_late + z_late)
     for copy in near:
         copy.wait()
-    down_sum.sent()
-    gate_sum.sent()
 
 
 def ffn(ffn_mine, grad_full, resid, scale_two, gain, w_out, w_gate, w_up, w_down, pieces):
@@ -1194,18 +1241,21 @@
             SDS((1, D), F32),
             SDS((CHUNK, D), BF),
             SDS((ROWS, 128), BF),
-            SDS((CHUNK, D), BF),
-            SDS((CHUNK, D), BF),
             SDS((4, 2, 4, 16, 1024), BF),
-            SDS((3, 4, 2, 4, 16, 1024), BF),
+            SDS((2, 4, 2, 4, 16, 1024), BF),
             SDS((8, 2, 16, 2048), BF),
-            SDS((3, 8, 2, 16, 2048), BF),
+            SDS((2, 8, 2, 16, 2048), BF),
+            SDS((8, 2, 16, 2048), BF),
+            SDS((2, 8, 2, 16, 2048), BF),
+            SDS((2, 4, 2, 16, 2048), BF),
             SDS((4, 2, 3, 3, 64, 1024), BF),
         ],
         in_specs=[vm] * 6 + [hbm] * 8,
-        out_specs=[vm] * 7 + [hbm] * 5,
+        out_specs=[vm] * 5 + [hbm] * 8,
         scratch_shapes=[
             pltpu.VMEM((SUB, D), BF),
+            pltpu.VMEM((CHUNK, D), BF),
+            pltpu.VMEM((CHUNK, D), BF),
             pltpu.VMEM((CHUNK, D), BF),
             pltpu.VMEM((CHUNK, D), BF),
             pltpu.VMEM((2, 2, 4, 2, 2, 64, 256), BF),
@@ -1219,15 +1269,19 @@
             pltpu.VMEM((3, SUB, D), BF),
             pltpu.VMEM((SUB, D), BF),
             pltpu.VMEM((CHUNK, 512), BF),
-            pltpu.VMEM((8, 2, 4, 2, 16, 2048), BF),
-            pltpu.VMEM((8, 2, 4, 2, 16, 2048), BF),
             pltpu.VMEM((8, 2, 4, 16, 2048), BF),
-            pltpu.SemaphoreType.DMA((36,)),
-            pltpu.SemaphoreType.DMA((36,)),
-            pltpu.SemaphoreType.DMA((2, 8)),
-            pltpu.SemaphoreType.DMA((2, 8)),
+            pltpu.VMEM((8, 2, 4, 16, 2048), BF),
+            pltpu.VMEM((8, 2, 4, 16, 2048), BF),
+            pltpu.VMEM((3, 2, 4, 2, 16, 2048), BF),
+            pltpu.VMEM((8, 2, 4, 16, 2048), BF),
+            pltpu.VMEM((2, 2, 2, 4, 16, 1024), BF),
+            pltpu.VMEM((2, 4, 2, 16, 2048), BF),
+            pltpu.SemaphoreType.DMA((48,)),
+            pltpu.SemaphoreType.DMA((48,)),
+            pltpu.SemaphoreType.DMA((3, 8)),
+            pltpu.SemaphoreType.DMA((3, 8)),
             pltpu.SemaphoreType.DMA((2, 32)),
-            pltpu.SemaphoreType.DMA((2,)),
+            pltpu.SemaphoreType.DMA((6,)),
             pltpu.SemaphoreType.REGULAR,
         ],
         compiler_params=pltpu.CompilerParams(
@@ -1300,25 +1354,13 @@
         ffn_gain_part,
         mix_full,
         heads_back,
-        ffn_input,
-        up_back,
-        down_own,
-        down_came,
-        gate_own,
-        gate_came,
+        *ffn_sums,
         _,
     ) = ffn(
         ffn_mine, grad_full, resid, scale_two, ffn_gain_all, w_out, w_gate, w_up, w_down, pieces
     )
 
-    query_back, kv_back = vmem_call(
-        "attend_back",
-        attend_back_body,
-        [doc_lengths, queries, kv, heads_back, cos_all[512:1536], sin_all[512:1536]],
-        [SDS((ROWS, 128), BF), SDS((ROWS, 128), BF)],
-        scratch=[pltpu.VMEM((1024, 128), F32)],
-        flops=5 * 10**9,
-    )
+    table = jnp.where(long_first, SHORT, 0)
     (
         layer_output,
         input_grad,
@@ -1331,8 +1373,12 @@
         gain_grads,
     ) = back(
         [
-            query_back,
-            kv_back,
+            jnp.broadcast_to(doc_lengths[0, 0], (8, 128)),
+            queries,
+            kv,
+            heads_back,
+            part(cos_all, table, ROWS, 0),
+            part(sin_all, table, ROWS, 0),
             w_attn,
             heads_cat,
             out_mine,
@@ -1341,8 +1387,10 @@
             scale_mine,
             attn_gain[None, :],
             ffn_gain_part,
+            normed,
+            mix_full,
         ],
-        [normed, mix_full, ffn_input, up_back, down_own, down_came, gate_own, gate_came],
+        ffn_sums,
     )
     kv_cols = jnp.moveaxis(kv_grad, 0, 1).reshape(32, 4, 2, 64)
     key_grad = kv_cols[:, :, 0, :].reshape(32, 256)

time: 372 us -> 357 us (0.960)
  Pallas kernels: 328 us -> 312 us
    pallas_call x1, Pallas kernels: 92.5 us -> 81.7 us  [back(): pl.pallas_call(back_body, name='back', out_shape=outs, in_specs=[vm] * le...]
    pallas_call x2 -> x1, Pallas kernels: 12.4 us -> 4.72 us  [vmem_call(): pl.pallas_call(body, name=name, out_shape=outs, in_specs=[pl.BlockSpec(me...]
    unnamed x75 -> x67, local copies, waits for them, and re-layouts: 17.1 us -> 14.6 us
  transfers between devices with their start and end apart: 4 -> 4, of which waited for: 0 -> 0; matrix products, arithmetic and copies ran while one was open for 1% -> 2% of each run, Pallas kernels for 23% -> 24%
where the time goes in v6:
time: 357 us; the launch traced here: 350 us
  Pallas kernels  312 us (87%)
  local copies, waits for them, and re-layouts  27.7 us (8%)
  starting transfers between devices  7.56 us (2%)
    pallas_call x1, Pallas kernels, ffn(): pl.pallas_call(ffn_body, name='ffn', out_shape=[SDS((SUB, D), BF), SDS((S...  117 us
    pallas_call x1, Pallas kernels, back(): pl.pallas_call(back_body, name='back', out_shape=outs, in_specs=[vm] * le...  81.7 us
    pallas_call x1, Pallas kernels, front(): pl.pallas_call(front_body, name='front', out_shape=outs, in_specs=[vm] *...  52.2 us
    pallas_call x1, Pallas kernels, weights_over_x(): pl.pallas_call(weights_body, name='weights', out_shape=SDS((2, 3, 3, 64,...  31.1 us
    pallas_call x1, Pallas kernels, middle(): pl.pallas_call(middle_body, name='middle', out_shape=outs, in_specs=[vm]...  25.9 us
    unnamed x67, local copies, waits for them, and re-layouts  14.6 us
    ppermute x4, starting transfers between devices, z_permute(): return lax.ppermute(value, 'tok', [(i, (i + 2 * d) % 8) for i in range(8)])  7.56 us
  transfers between devices with their start and end apart: 4, of which 0 were waited for; matrix products, arithmetic and copies ran while one was open for 2% of the time, Pallas kernels for 24%

profile of v6, /device:TPU:0, one launch (start us, length us, event | category | flops | bytes accessed | tf_op | source)
XLA Modules:
  0.0 350.2 jit_solution(18222373878967825624)
XLA Ops:
  0.7 1.0 constant_dynamic-slice_fusion.5
  1.6 1.1 constant_dynamic-slice_fusion.3
  2.8 1.0 maximum_bitcast_fusion.pieces
  3.7 31.1 %weights.1.piece0 = bf16[2,3,3,64,1024]{4,3,2,1,0:T(8,128)(2,1)} custom-call(bf16[2,3,64,1024]{3,2,1,0:T(8,128)(2,1)} %maximum_bitcast_fusion.pieces), custom_call_target="tpu_custom_call" | custom-call | tf_op jit(solution)/shard_map/weights/pallas_call | solution.py:633
  34.8 4.1 %collective-permute-start.1 = (bf16[2,3,3,64,1024]{4,3,2,1,0:T(8,128)(2,1)}, bf16[2,3,3,64,1024]{4,3,2,1,0:T(8,128)(2,1)}, u32[]{:S(2)}, u32[]{:S(2)}) collective-permute-start(bf16[2,3,3,64,1024]{4,3,2,1,0:T(8,128)(2,1)} %weights.1.piece0), channel_id=1, source_target_pairs={{0,96},{16,112},{32,0},{48,16},{64,32},{80,48},{96,64},{112,80},{1... | collective-permute-start | bytes 7077896 | tf_op jit(solution)/shard_map/ppermute | solution.py:561
  39.1 1.5 constant_dynamic-slice_fusion.6
  41.0 52.2 %front.1 = (bf16[1536,128]{1,0:T(8,128)(2,1)S(1)}, bf16[1536,128]{1,0:T(8,128)(2,1)S(1)}, bf16[2048,768]{1,0:T(8,128)(2,1)S(1)}, bf16[384,2048]{1,0:T(8,128)(2,1...) custom-call(f32[8,128]{1,0:T(8,128)S(1)} %broadcast_in_dim.14.gain_r, ...), custom_call_target="tpu_custom_call" | custom-call | flops 2000000000 | bytes 8388608 | tf_op jit(solution)/shard_map/front/pallas_call | solution.py:780
  93.3 1.7 copy-done.12
  95.0 1.2 copy-done.15
  96.1 1.4 constant_dynamic-slice_fusion.1
  97.5 2.1 slice_bitcast_fusion
  99.7 1.4 slice_bitcast_fusion.1
  101.1 3.4 collective-permute-start.3
  104.5 4.7 %attend.1.heads = bf16[1536,128]{1,0:T(8,128)(2,1)S(1)} custom-call(s32[1,2]{1,0:T(1,128)S(1)} %copy-done.1, bf16[1536,128]{1,0:T(8,128)(2,1)S(1)} %get-tuple-element.49.q_ref, bf16[1536,128]{1,0:T(8,128)(2,1)S(1)} %get-tuple-element.50.kv_ref), custom_call_target="tpu_custom_call" | custom-call | flops 20000000000 | bytes 1048576 | tf_op jit(solution)/shard_map/attend/pallas_call | solution.py:132
  109.2 25.9 %middle.1 = (bf16[384,512]{1,0:T(8,128)(2,1)S(1)}, f32[96,2048]{1,0:T(8,128)S(1)}, f32[96,1]{1,0:T(8,128)S(1)}, bf16[96,2048]{1,0:T(8,128)(2,1)S(1)}) custom-call(bf16[1536,128]{1,0:T(8,128)(2,1)S(1)} %attend.1.heads, bf16[96,2048]{1,0:T(8,128)(2,1)S(1)} %get-tuple-element.51.in_mine, f32[1,2048]{1,0:T(1,128)S(1)} %slice_bitcast_fusion.2.gain.gain_ref, ...), custom_call_target="tpu_custom_call" | custom-call | flops 1000000000 | bytes 8388608 | tf_op jit(solution)/shard_map/middle/pallas_call | solution.py:852
  135.1 0.9 copy-done.8
  138.1 1.0 copy-done.28
  139.5 116.8 %ffn.1 = (bf16[96,2048]{1,0:T(8,128)(2,1)}, f32[96,2048]{1,0:T(8,128)}, f32[1,2048]{1,0:T(1,128)}, bf16[384,2048]{1,0:T(8,128)(2,1)}, bf16[1536,128]{1,0:T(8,128...) custom-call(bf16[96,2048]{1,0:T(8,128)(2,1)} %copy-done.11, ...), custom_call_target="tpu_custom_call" | custom-call | flops 25999998976 | bytes 41943040 | tf_op jit(solution)/shard_map/ffn/pallas_call | solution.py:1235
  257.0 81.7 %back.1 = (bf16[1536,128]{1,0:T(8,128)(2,1)}, bf16[1536,128]{1,0:T(8,128)(2,1)}, f32[256,128]{1,0:T(8,128)}, f32[4,32,128]{2,1,0:T(8,128)}, f32[256,128]{1,0:T(8...) custom-call(s32[8,128]{1,0:T(8,128)} %broadcast_in_dim.6.len_ref, ...), custom_call_target="tpu_custom_call" | custom-call | flops 10000000000 | bytes 31457280 | tf_op jit(solution)/shard_map/back/pallas_call | solution.py:480
  338.7 0.9 constant_dynamic-slice_fusion
  340.1 1.0 reshape.45
  342.7 1.8 copy.34
  344.6 1.8 copy.35
  347.6 0.8 copy.38
  (77 shorter events, 8.7 us)
Async XLA Ops:
  2.7 36.2 %copy-start.1 = (s32[1,2]{1,0:T(1,128)S(1)}, s32[1,2]{1,0:T(1,128)}, u32[]{:S(2)}) copy-start(s32[1,2]{1,0:T(1,128)} %len_ref.1) | copy-start | bytes 28
  2.7 36.3 %copy-start.19 = (f32[2048,128]{1,0:T(8,128)S(1)}, f32[2048,128]{1,0:T(8,128)}, u32[]{:S(2)}) copy-start(f32[2048,128]{1,0:T(8,128)} %constant.70.clone) | copy-start | bytes 3145732
  2.7 36.3 %copy-start.20 = (f32[2048,128]{1,0:T(8,128)S(1)}, f32[2048,128]{1,0:T(8,128)}, u32[]{:S(2)}) copy-start(f32[2048,128]{1,0:T(8,128)} %constant.71.clone) | copy-start | bytes 3145732
  3.7 35.4 %copy-start.24 = (bf16[2048,256]{1,0:T(8,128)(2,1)S(1)}, bf16[2048,256]{1,0:T(8,128)(2,1)}, u32[]{:S(2)}) copy-start(bf16[2048,256]{1,0:T(8,128)(2,1)} %param.19) | copy-start | bytes 3145732
  34.8 62.7 %collective-permute-start.1 = (bf16[2,3,3,64,1024]{4,3,2,1,0:T(8,128)(2,1)}, bf16[2,3,3,64,1024]{4,3,2,1,0:T(8,128)(2,1)}, u32[]{:S(2)}, u32[]{:S(2)}) collective-permute-start(bf16[2,3,3,64,1024]{4,3,2,1,0:T(8,128)(2,1)} %weights.1.piece0), channel_id=1, source_target_pairs={{0,96},{16,112},{32,0},{48,16},{64,32},{80,48},{96,64},{112,80},{1... | collective-permute-start | bytes 7077896 | tf_op jit(solution)/shard_map/ppermute | solution.py:561
  38.9 60.7 %collective-permute-start = (bf16[2,3,3,64,1024]{4,3,2,1,0:T(8,128)(2,1)}, bf16[2,3,3,64,1024]{4,3,2,1,0:T(8,128)(2,1)}, u32[]{:S(2)}, u32[]{:S(2)}) collective-permute-start(bf16[2,3,3,64,1024]{4,3,2,1,0:T(8,128)(2,1)} %weights.1.piece0), channel_id=1, source_target_pairs={{0,32},{16,48},{32,64},{48,80},{64,96},{80,112},{96,0},{112,16},{1... | collective-permute-start | bytes 7077896 | tf_op jit(solution)/shard_map/ppermute | solution.py:561
  39.0 2.0 copy-start.2
  39.0 2.0 copy-start.3
  39.0 2.0 copy-start.4
  39.1 2.0 copy-start.5
  96.1 3.5 %copy-start.14 = (bf16[384,2048]{1,0:T(8,128)(2,1)}, bf16[384,2048]{1,0:T(8,128)(2,1)S(1)}, u32[]{:S(2)}) copy-start(bf16[384,2048]{1,0:T(8,128)(2,1)S(1)} %get-tuple-element.67.normed) | copy-start | bytes 4718596
  96.1 3.5 %copy-start.18 = (f32[96,1]{1,0:T(8,128)}, f32[96,1]{1,0:T(8,128)S(1)}, u32[]{:S(2)}) copy-start(f32[96,1]{1,0:T(8,128)S(1)} %get-tuple-element.65.scale_ref) | copy-start | bytes 1156
  96.1 8.4 %copy-start.16 = (bf16[1536,128]{1,0:T(8,128)(2,1)}, bf16[1536,128]{1,0:T(8,128)(2,1)S(1)}, u32[]{:S(2)}) copy-start(bf16[1536,128]{1,0:T(8,128)(2,1)S(1)} %get-tuple-element.49.q_ref) | copy-start | bytes 1179652
  96.1 8.4 %copy-start.17 = (bf16[1536,128]{1,0:T(8,128)(2,1)}, bf16[1536,128]{1,0:T(8,128)(2,1)S(1)}, u32[]{:S(2)}) copy-start(bf16[1536,128]{1,0:T(8,128)(2,1)S(1)} %get-tuple-element.50.kv_ref) | copy-start | bytes 1179652
  96.1 13.1 %copy-start.7 = (bf16[2048,512]{1,0:T(8,128)(2,1)}, bf16[2048,512]{1,0:T(8,128)(2,1)S(1)}, u32[]{:S(2)}) copy-start(bf16[2048,512]{1,0:T(8,128)(2,1)S(1)} %get-tuple-element.53.w_cat.w_out_ref) | copy-start | bytes 6291460
  96.1 13.1 %copy-start.9 = (bf16[96,2048]{1,0:T(8,128)(2,1)}, bf16[96,2048]{1,0:T(8,128)(2,1)S(1)}, u32[]{:S(2)}) copy-start(bf16[96,2048]{1,0:T(8,128)(2,1)S(1)} %get-tuple-element.51.in_mine) | copy-start | bytes 1179652
  97.5 11.7 %copy-start = (f32[1,2048]{1,0:T(1,128)}, f32[1,2048]{1,0:T(1,128)S(1)}, u32[]{:S(2)}) copy-start(f32[1,2048]{1,0:T(1,128)S(1)} %slice_bitcast_fusion.2.gain.gain_ref) | copy-start | bytes 24580
  101.0 37.1 %collective-permute-start.2 = (bf16[3,3,64,1024]{3,2,1,0:T(8,128)(2,1)S(1)}, bf16[3,3,64,1024]{3,2,1,0:T(8,128)(2,1)S(1)}, u32[]{:S(2)}, u32[]{:S(2)}) collective-permute-start(bf16[3,3,64,1024]{3,2,1,0:T(8,128)(2,1)S(1)} %slice_bitcast_fusion.1), channel_id=1, source_target_pairs={{0,32},{16,48},{32,64},{48,80},{64,96},{80,112},{96,0},{112,16},{1... | collective-permute-start | bytes 3538952 | tf_op jit(solution)/shard_map/ppermute | solution.py:561
  101.1 37.0 %collective-permute-start.3 = (bf16[3,3,64,1024]{3,2,1,0:T(8,128)(2,1)S(1)}, bf16[3,3,64,1024]{3,2,1,0:T(8,128)(2,1)S(1)}, u32[]{:S(2)}, u32[]{:S(2)}) collective-permute-start(bf16[3,3,64,1024]{3,2,1,0:T(8,128)(2,1)S(1)} %slice_bitcast_fusion), channel_id=1, source_target_pairs={{0,96},{16,112},{32,0},{48,16},{64,32},{80,48},{96,64},{112,80},{1... | collective-permute-start | bytes 3538952 | tf_op jit(solution)/shard_map/ppermute | solution.py:561
  338.7 7.6 %copy-start.26 = (f32[256,128]{1,0:T(8,128)S(1)}, f32[256,128]{1,0:T(8,128)}, u32[]{:S(2)}) copy-start(f32[256,128]{1,0:T(8,128)} %get-tuple-element.111) | copy-start | bytes 393220
  338.7 8.3 %copy-start.25 = (f32[256,128]{1,0:T(8,128)S(1)}, f32[256,128]{1,0:T(8,128)}, u32[]{:S(2)}) copy-start(f32[256,128]{1,0:T(8,128)} %get-tuple-element.114) | copy-start | bytes 393220
  338.7 8.9 %copy-start.23 = (f32[8,16,1024]{2,1,0:T(8,128)S(1)}, f32[8,16,1024]{2,1,0:T(8,128)}, u32[]{:S(2)}) copy-start(f32[8,16,1024]{2,1,0:T(8,128)} %get-tuple-element.116) | copy-start | bytes 1572868
  338.7 9.7 %copy-start.22 = (f32[8,16,1024]{2,1,0:T(8,128)S(1)}, f32[8,16,1024]{2,1,0:T(8,128)}, u32[]{:S(2)}) copy-start(f32[8,16,1024]{2,1,0:T(8,128)} %get-tuple-element.117) | copy-start | bytes 1572868
  342.7 6.5 %copy-start.21 = (f32[8,16,1024]{2,1,0:T(8,128)S(1)}, f32[8,16,1024]{2,1,0:T(8,128)}, u32[]{:S(2)}) copy-start(f32[8,16,1024]{2,1,0:T(8,128)} %get-tuple-element.118) | copy-start | bytes 1572868
  (10 other events, 12.2 us)
